TPU v7x, 128 devices: a whole 4x4x4 slice. The times are simulated.
128 devices in a mesh: group: 8 (over y_hi, z), dp: 16 (over x, y_lo, core).
Axes of the slice: x: 4, y: 4 (y_hi: 2, y_lo: 2; y = y_hi * 2 + y_lo), z: 4, core: 2. Of those that a mesh axis runs over, the one named last changes fastest.
Arguments:
- tokens: float32 [128, 577, 384], P(('group', 'dp')), may hold values from -6 to 6
- cotangent: float32 [128, 577, 384], P(('group', 'dp')), may hold values from -6 to 6
- live: int32 [128], P(('group', 'dp')), may hold values from 0 to 1, as said below
- slot_of: int32 [8], replicated, may hold values from 0 to 7, as said below
- weights: float32 [8, 384, 1536], P('group', None, 'dp'), as said below
- momentum: float32 [8, 384, 1536], P('group', None, 'dp'), as said below
- vec: float32 [24, 384], P('group', 'dp')
- vec_first: float32 [24, 384], P('group', 'dp')
- vec_second: float32 [24, 384], P('group', 'dp'), as said below
Outputs:
- block_out: float32 [128, 577, 384], P(('group', 'dp'))
- token_grad: float32 [128, 577, 384], P(('group', 'dp'))
- weight_grad: float32 [8, 384, 1536], P('group', None, 'dp')
- new_momentum: float32 [8, 384, 1536], P('group', None, 'dp')
- new_weights: float32 [8, 384, 1536], P('group', None, 'dp')
- first_new: float32 [24, 384], P('group', 'dp')
- second_new: float32 [24, 384], P('group', 'dp')
- vec_new: float32 [24, 384], P('group', 'dp')
Inputs may be any that keep to these rules, and one draw needn't show every extreme that they name: `live`: 1 where the device's slot holds an image, 0 where it is empty; every draw has full and empty slots. A permutation: matrix m lies in slot slot_of[m]; slot q lies on group index q. `weights`: slot q holds the matrix m with slot_of[m] = q in its first n(m) columns and zeros beyond. `momentum`: laid out like weights, zeros beyond n(m) columns. `vec_second`: positive.
All inputs are finite; a program needn't handle non-finite values.
Results may differ from a plain program's by a relative error of at most 0.02.
The roundings to bfloat16 on the way count: a program that leaves them out, or rounds other values in their place, can miss the bound.
Values may be sent and summed in bfloat16 or wider, within the bound.
No kernel may reach another device: no remote copies, remote signals or barrier semaphores. Data moves between devices by JAX's collectives and lax.ppermute only.
A program may use at most 192 MiB of HBM per device.

v0:
```python
import jax
import jax.numpy as jnp
from jax import lax
from jax.experimental import pallas as pl
from jax.experimental.pallas import tpu as pltpu
from jax.sharding import PartitionSpec as P

HEADS = 6
FF = 1536
LAYERS = 2
NEWTON_STEPS = 5
STEP = 10
MATS = 8
VROWS = 24


norm_eps = 1e-06
ortho_eps = 1e-07
coef_a = 3.4445
coef_b = -4.775
coef_c = 2.0315
momentum_keep = 0.95
muon_rate = 0.25
muon_decay = 0.01
muon_shape = 0.5
adam_rate = 0.4
first_keep = 0.9
second_keep = 0.999
adam_eps = 1e-08
half_root = 0.7071067811865476
density = 0.3989422804014327


def normalize(values):
    center = values - jnp.mean(values, -1, keepdims=True)
    inv_std = lax.rsqrt(jnp.mean(center * center, -1, keepdims=True) + norm_eps)
    return (center * inv_std, inv_std)


def norm_back(upstream, normed, inv_std, gain):
    scaled = upstream * gain
    return inv_std * (
        scaled
        - jnp.mean(scaled, -1, keepdims=True)
        - normed * jnp.mean(scaled * normed, -1, keepdims=True)
    )


def gelu_slope(values):
    return (
        0.5 * (1.0 + lax.erf(values * half_root))
        + values * jnp.exp(-0.5 * values * values) * density
    )


def row_contract(left_op, right_op):
    return lax.dot_general(
        left_op, right_op, (((0,), (0,)), ((), ())), preferred_element_type=jnp.float32
    )


def col_contract(left_op, right_op):
    return lax.dot_general(
        left_op, right_op, (((1,), (1,)), ((), ())), preferred_element_type=jnp.float32
    )


BLK = 96
WIDE = 384
VPAD = 32
RINGX = 4
RINGZ = 4
STEPS = [(flip, hops) for flip in range(2) for hops in range(RINGZ)]


def half(part):
    return part.astype(jnp.bfloat16)


def full(part):
    return part.astype(jnp.float32)


def near(part, change):
    return lax.ppermute(part, "dp", [(at, change(at)) for at in range(16)])


def other_core(part):
    return near(part, lambda at: at ^ 1)


def other_row(part):
    return near(part, lambda at: at ^ 2)


def along_x(part, hops):
    return near(part, lambda at: (at + 4 * hops) % 16)


def along_group(part, flip, hops):
    pairs = [(at, (at ^ (4 * flip)) // 4 * 4 + (at + hops) % RINGZ) for at in range(8)]
    return lax.ppermute(part, "group", pairs)


def my_place():
    spot = lax.axis_index("dp")
    return spot >> 2, (spot >> 1) & 1, spot & 1


def my_group():
    group = lax.axis_index("group")
    return group >> 2, group & 3


def rows_at(start, count=BLK):
    return pl.ds(pl.multiple_of(start, 32), count)


def small_call(kernel, outs, ins, slot_first=False, scratch=(), name=None, vmem=12):
    specs = [pl.BlockSpec(memory_space=pltpu.VMEM)] * len(ins)
    if slot_first:
        specs[0] = pl.BlockSpec(memory_space=pltpu.SMEM)
    return pl.pallas_call(
        kernel,
        out_shape=[jax.ShapeDtypeStruct((rows, WIDE), kind) for rows, kind in outs],
        in_specs=specs,
        out_specs=[pl.BlockSpec(memory_space=pltpu.VMEM)] * len(outs),
        scratch_shapes=list(scratch),
        compiler_params=pltpu.CompilerParams(vmem_limit_bytes=vmem << 20),
        name=name,
    )(*ins)


def choose_kernel(slot_ref, *refs):
    pairs, (first_ref, third_ref), hold = refs[:4], refs[4:6], refs[6]
    flip, z = my_group()
    spread = None
    for turn, hops in STEPS:
        base = turn * (BLK + VPAD)
        hold[turn * RINGZ + hops] = pairs[hops][base : base + BLK]
        piece = full(pairs[hops][base + BLK : base + BLK + VPAD])
        spread = piece if spread is None else spread + piece

    def matrix(mat_index):
        slot = slot_ref[mat_index]
        return hold[((slot >> 2) ^ flip) * RINGZ + ((slot - z) & 3)]

    first_ref[4 * BLK :] = half(spread)
    for member in range(4):
        first_ref[member * BLK : (member + 1) * BLK] = matrix(member)
        third_ref[member * BLK : (member + 1) * BLK] = matrix(4 + member)


def merge_first_kernel(*refs):
    parts, head_ref, hidden_ref, hold = refs[:4], refs[4], refs[5], refs[6]
    merge_heads(parts, head_ref, hold)
    merge_hidden(parts, hidden_ref, 0)
    total = full(parts[0][4 * BLK :])
    for at in range(1, 4):
        total = total + full(parts[at][4 * BLK :])
    head_ref[4 * BLK :] = half(total)


def merge_third_kernel(*refs):
    parts, out_ref, hold = refs[:4], refs[4], refs[5]
    merge_heads(parts, out_ref, hold)
    merge_hidden(parts, out_ref, 4 * BLK)


def merge_heads(parts, out_ref, hold):
    x, _, _ = my_place()
    for at in range(4):
        hold[at] = parts[at][: 2 * BLK]
    for at in range(3):
        out_ref[at * BLK : (at + 1) * BLK] = hold[(at - x) & 3, :BLK]
    out_ref[3 * BLK : 4 * BLK] = hold[(0 - x) & 3, BLK:]


def merge_hidden(parts, out_ref, put):
    for member in (2, 3):
        for part in parts:
            out_ref[put : put + BLK] = part[member * BLK : (member + 1) * BLK]
            put += BLK


def final_kernel(heads, hidden, spread, *refs):
    parts, outs = refs[:4], list(refs[4:])
    _, row, core = my_place()
    base = 0
    if heads:
        qkv_ref, out_ref = outs[:2]
        outs = outs[2:]
        for at_part, part in enumerate(parts):
            piece = (row ^ (at_part & 1)) * 2 * BLK + (core ^ (at_part >> 1)) * BLK
            for at in range(3):
                qkv_ref[rows_at(at * WIDE + piece)] = part[at * BLK : (at + 1) * BLK]
            out_ref[rows_at(piece)] = part[3 * BLK : 4 * BLK]
        base = 4 * BLK
    if hidden:
        for member in range(2):
            for at_part, part in enumerate(parts):
                start = base + member * WIDE
                outs[member][at_part * WIDE : (at_part + 1) * WIDE] = part[start : start + WIDE]
        base += 2 * WIDE
        outs = outs[2:]
    if spread:
        total = full(parts[0][base:])
        for part in parts[1:]:
            total = total + full(part[base:])
        outs[0][...] = total


def from_x(part):
    return [part] + [along_x(part, -hops) for hops in (1, 2, 3)]


HOLD_HEADS = pltpu.VMEM((4, 2 * BLK, WIDE), jnp.bfloat16)


def all_four(own):
    beside = other_row(own)
    return [own, beside, other_core(own), other_core(beside)]


def whole(parts, heads, hidden, spread, name):
    outs = []
    if heads:
        outs += [(3 * WIDE, jnp.bfloat16), (WIDE, jnp.bfloat16)]
    if hidden:
        outs += [(FF, jnp.bfloat16)] * 2
    if spread:
        outs += [(VPAD, jnp.float32)]
    return small_call(
        lambda *refs: final_kernel(heads, hidden, spread, *refs), outs, parts, name=name + "_whole"
    )


def put_vec(ref, start, value):
    high = half(value)
    ref[start : start + VPAD] = high
    ref[start + VPAD : start + 2 * VPAD] = half(value - full(high))


def get_vec(ref, start):
    return full(ref[start : start + VPAD]) + full(ref[start + VPAD : start + 2 * VPAD])


def split_core_kernel(heads, hidden, spread, *refs):
    refs = list(refs)
    keep_ref, sent_ref = refs[-2:]
    _, _, core = my_place()
    put = 0
    if heads:
        qkv_ref, out_ref = refs[:2]
        refs = refs[2:]
        for row in range(2):
            for at in range(4):
                source = out_ref if at == 3 else qkv_ref
                start = (0 if at == 3 else at * WIDE) + row * 2 * BLK
                keep_ref[put : put + BLK] = source[rows_at(start + core * BLK)]
                sent_ref[put : put + BLK] = source[rows_at(start + (1 - core) * BLK)]
                put += BLK
    if hidden:
        for source in refs[:2]:
            keep_ref[put : put + 2 * WIDE] = source[: 2 * WIDE]
            sent_ref[put : put + 2 * WIDE] = source[2 * WIDE :]
            put += 2 * WIDE
        refs = refs[2:]
    if spread:
        *pieces, vec_ref = refs[:-2]
        vec_ref[VROWS:] = jnp.zeros((VPAD - VROWS, WIDE), jnp.float32)
        for layer_at in range(LAYERS):
            base = layer_at * (VROWS // LAYERS)
            one, two, three = pieces[3 * layer_at : 3 * layer_at + 3]
            vec_ref[base : base + 5] = one[:5]
            vec_ref[base + 5 : base + 8] = two[:3]
            vec_ref[base + 8 : base + 12] = three[...]
        put_vec(sent_ref, put, vec_ref[...])


def split_row_kernel(heads, hidden, spread, *refs):
    had_ref, came_ref = refs[:2]
    keep_ref, sent_ref = refs[2 + spread : 4 + spread]
    _, row, _ = my_place()

    def total(start):
        at = rows_at(start, WIDE)
        return full(had_ref[at]) + full(came_ref[at])

    put, base = 0, 0
    if heads:
        keep_ref[:WIDE] = total(row * WIDE)
        sent_ref[:WIDE] = half(total((1 - row) * WIDE))
        put, base = WIDE, 2 * WIDE
    if hidden:
        for _ in range(2):
            keep_ref[put : put + WIDE] = total(base)
            sent_ref[put : put + WIDE] = half(total(base + WIDE))
            put, base = put + WIDE, base + 2 * WIDE
    if spread:
        value = refs[2][...] + get_vec(came_ref, base)
        refs[-1][...] = value
        put_vec(sent_ref, put, value)


def split_x_kernel(heads, hidden, spread, *refs):
    had_ref, came_ref = refs[:2]
    keep_ref, *sent_refs = refs[2 + spread : 6 + spread]
    hold = refs[-1]
    x, _, _ = my_place()
    count = had_ref.shape[0]
    hold[...] = had_ref[...] + full(came_ref[:count])
    for hops, target in enumerate([keep_ref] + sent_refs):
        kind = target.dtype
        put, base = 0, 0
        if heads:
            at = (x + hops) & 3
            piece = hold[rows_at(at * BLK)]
            target[:BLK] = jnp.where(at == 3, 0.0, piece).astype(kind)
            target[BLK : 2 * BLK] = hold[3 * BLK : 4 * BLK].astype(kind)
            put, base = 2 * BLK, WIDE
        if hidden:
            for _ in range(2):
                start = base + hops * BLK
                target[put : put + BLK] = hold[start : start + BLK].astype(kind)
                put, base = put + BLK, base + WIDE
        if spread and hops:
            value = refs[2][...] + get_vec(came_ref, base)
            refs[-2][...] = value
            put_vec(target, put, value)


def sum_x_kernel(heads, keep_ref, *refs):
    parts, out_ref = refs[:3], refs[3]
    x, _, _ = my_place()
    total = keep_ref[...]
    for part in parts:
        total = total + full(part[...])
    out_ref[...] = total
    if heads:
        out_ref[BLK : 2 * BLK] = jnp.where(x == 0, total[BLK : 2 * BLK], 0.0)


def scatter_core(grads, heads, hidden, spread, name):
    rows = 8 * BLK * heads + 16 * BLK * hidden
    return small_call(
        lambda *refs: split_core_kernel(heads, hidden, spread, *refs),
        [(VPAD, jnp.float32)] * spread
        + [(rows, jnp.bfloat16), (rows + 2 * VPAD * spread, jnp.bfloat16)],
        grads,
        name=name + "_split_core",
    )


def scatter_row(keep, came, heads, hidden, spread, name, vec_sum=None):
    rows = 4 * BLK * heads + 8 * BLK * hidden
    return small_call(
        lambda *refs: split_row_kernel(heads, hidden, spread, *refs),
        [(rows, jnp.float32), (rows + 2 * VPAD * spread, jnp.bfloat16)]
        + [(VPAD, jnp.float32)] * spread,
        [keep, came] + [vec_sum] * spread,
        name=name + "_split_row",
    )


def scatter_x(keep, came, heads, hidden, spread, name, vec_sum=None):
    rows = 2 * BLK * heads + 2 * BLK * hidden
    return small_call(
        lambda *refs: split_x_kernel(heads, hidden, spread, *refs),
        [(rows, jnp.float32)]
        + [(rows + 2 * VPAD * spread, jnp.bfloat16)] * 3
        + [(VPAD, jnp.float32)] * spread,
        [keep, came] + [vec_sum] * spread,
        scratch=[pltpu.VMEM(keep.shape, jnp.float32)],
        name=name + "_split_x",
    )


def spread_x(sent):
    return [along_x(part, hops + 1) for hops, part in enumerate(sent)]


def split_group_kernel(slot_ref, *refs):
    second_ref, third_ref, keep_ref, *parts = refs[:6]
    vec_ref, own_ref = refs[6], refs[7]
    sent_refs, vec_out, hold = refs[8:15], refs[15], refs[16]
    flip, z = my_group()
    x, _, _ = my_place()
    total = keep_ref[...]
    value = vec_ref[...]
    for part in parts:
        total = total + full(part[: 2 * BLK])
        value = value + get_vec(part, 2 * BLK)
    vec_out[...] = value
    hold[0] = total[:BLK]
    hold[1] = jnp.where(x == 0, total[BLK:], 0.0)
    for member in range(2):
        hold[2 + member] = second_ref[member * BLK : (member + 1) * BLK]
    for member in range(4):
        hold[4 + member] = third_ref[member * BLK : (member + 1) * BLK]
    for at, (turn, hops) in enumerate(STEPS):
        slot = (flip ^ turn) * RINGZ + ((z + hops) & 3)
        mat_index = jnp.int32(0)
        for member in range(1, MATS):
            mat_index = jnp.where(slot_ref[member] == slot, member, mat_index)
        if at == 0:
            own_ref[...] = hold[mat_index]
        else:
            sent_refs[at - 1][:BLK] = half(hold[mat_index])
            put_vec(sent_refs[at - 1], BLK, value)


def renew_kernel(own_ref, *refs):
    parts, (vec_ref, moment_ref) = refs[:7], refs[7:9]
    grad_ref, new_ref, low_ref, vec_out = refs[9:]
    total, value = own_ref[...], vec_ref[...]
    for part in parts:
        total = total + full(part[:BLK])
        value = value + get_vec(part, BLK)
    grad_ref[...] = total
    vec_out[...] = value
    renewed = momentum_keep * moment_ref[...] + total
    new_ref[...] = renewed
    low_ref[...] = half(renewed)


def parts_of(value):
    high = half(value)
    return high, half(value - full(high))


def as_left(value):
    high, low = parts_of(value)
    return jnp.concatenate([high, high, low], 1)


def as_right(value):
    high, low = parts_of(value)
    return jnp.concatenate([high, low, high], 0)


def product(left, right):
    return jnp.dot(left, right, preferred_element_type=jnp.float32)


def newton_kernel(slot_ref, *refs):
    parts, own_ref, weight_ref, out_ref = refs[:4], refs[4], refs[5], refs[6]
    size = WIDE
    gram = None
    for part in parts:
        piece = row_contract(part[...], part[...])
        gram = piece if gram is None else gram + piece
    diagonal = lax.broadcasted_iota(jnp.int32, (size, size), 0) == lax.broadcasted_iota(
        jnp.int32, (size, size), 1
    )
    trace = jnp.sum(jnp.where(diagonal, gram, 0.0), keepdims=True)
    inverse = 1.0 / (jnp.sqrt(trace) + ortho_eps)
    gram = gram * inverse * inverse
    total = None
    for iteration in range(NEWTON_STEPS):
        squared = product(as_left(gram), as_right(gram))
        step = jnp.where(diagonal, coef_a, 0.0) + coef_b * gram + coef_c * squared
        left = as_left(step)
        if iteration == 0:
            total = step
            gram = product(left, as_right(product(left, as_right(gram))))
        elif iteration < NEWTON_STEPS - 1:
            both = product(left, as_right(jnp.concatenate([gram, total], 1)))
            total = both[:, size:]
            gram = product(left, as_right(both[:, :size]))
        else:
            total = product(left, as_right(total))
    high, low = parts_of(total * inverse)
    own = own_ref[...]
    ortho = product(own, high) + product(own, low)
    group = lax.axis_index("group")
    widths = [3 * WIDE, WIDE, FF, FF] * LAYERS
    scale = jnp.float32(0.0)
    for member in range(MATS):
        rate = muon_rate * muon_shape * widths[member] ** 0.5
        scale = jnp.where(slot_ref[member] == group, jnp.float32(rate), scale)
    out_ref[...] = weight_ref[...] * (1.0 - muon_rate * muon_decay) - scale * ortho


def turned(part):
    return half(full(part).T)


def column(index):
    return slice(index * 128, (index + 1) * 128)


def row_of(vec_ref, layer_at, index):
    at = layer_at * (VROWS // LAYERS) + index
    return vec_ref[at : at + 1]


def attend_kernel(layer_at, in_ref, qkv_w, out_w, vec_ref, mid_ref, qkv_ref, attn_ref, prob_ref):
    normed, _ = normalize(in_ref[...])
    normed_low = half(normed * row_of(vec_ref, layer_at, 0) + row_of(vec_ref, layer_at, 1))
    for third in range(3):
        rows = slice(third * WIDE, (third + 1) * WIDE)
        value = col_contract(normed_low, qkv_w[rows])
        if third != 1:
            value = value + row_of(vec_ref, layer_at, 2 if third == 0 else 3)
        qkv_ref[:, rows] = half(value)
    for at in range(HEADS // 2):
        attend_pair(at, qkv_ref, attn_ref, prob_ref)
    mid_ref[...] = in_ref[...] + (
        col_contract(attn_ref[...], out_w[...]) + row_of(vec_ref, layer_at, 4)
    )


def attend_pair(at, qkv_ref, attn_ref, prob_ref):
    queries = qkv_ref[:, column(at)] * jnp.bfloat16(0.125)
    keys, values = qkv_ref[:, column(3 + at)], qkv_ref[:, column(6 + at)]
    lane = lax.broadcasted_iota(jnp.int32, keys.shape, 1)
    values_t = turned(values)
    sums = []
    for head in range(2):
        mine = half(jnp.where((lane >> 6) == head, 1.0, 0.0))
        scores = col_contract(keys * mine, queries)
        exponent = jnp.exp(scores - jnp.max(scores, 0, keepdims=True))
        probs = half(exponent * (1.0 / jnp.sum(exponent, 0, keepdims=True)))
        prob_ref[2 * at + head] = probs
        sums.append(product(values_t, probs))
    row = lax.broadcasted_iota(jnp.int32, sums[0].shape, 0)
    attn_ref[:, column(at)] = half(jnp.where(row < 64, sums[0], sums[1]).T)


def attend_back_kernel(layer_at, up_ref, in_ref, qkv_ref, attn_ref, prob_ref, qkv_w, out_w, vec_ref, grad_ref, gqkv_ref, gout_ref, sum_ref, upstream_ref, back_ref):
    out_low = half(up_ref[...])
    gout_ref[...] = half(row_contract(out_low, attn_ref[...]))
    upstream_ref[...] = half(product(out_low, out_w[...]))
    sum_ref[4:5] = jnp.sum(full(out_low), 0, keepdims=True)
    for at in range(HEADS // 2):
        attend_back_pair(at, qkv_ref, upstream_ref, prob_ref, back_ref)
    normed, inv_std = normalize(in_ref[...])
    gain = row_of(vec_ref, layer_at, 0)
    normed_low = half(normed * gain + row_of(vec_ref, layer_at, 1))
    back_normed = jnp.zeros(normed.shape, jnp.float32)
    for third in range(3):
        rows = slice(third * WIDE, (third + 1) * WIDE)
        piece = back_ref[:, rows]
        gqkv_ref[rows] = half(row_contract(piece, normed_low))
        back_normed = back_normed + product(piece, qkv_w[rows])
        if third != 1:
            put = 2 if third == 0 else 3
            sum_ref[put : put + 1] = jnp.sum(full(piece), 0, keepdims=True)
    sum_ref[0:1] = jnp.sum(back_normed * normed, 0, keepdims=True)
    sum_ref[1:2] = jnp.sum(back_normed, 0, keepdims=True)
    grad_ref[...] = up_ref[...] + norm_back(back_normed, normed, inv_std, gain)


def attend_back_pair(at, qkv_ref, upstream_ref, prob_ref, back_ref):
    queries, keys, values = (qkv_ref[:, column(3 * third + at)] for third in range(3))
    upstream = upstream_ref[:, column(at)]
    lane = lax.broadcasted_iota(jnp.int32, keys.shape, 1)
    keys_t = turned(keys)
    got = []
    for head in range(2):
        mine = half(jnp.where((lane >> 6) == head, 1.0, 0.0))
        probs_low = prob_ref[2 * at + head]
        probs = full(probs_low)
        prob_grad = col_contract(values * mine, upstream)
        inner = jnp.sum(prob_grad * probs, 0, keepdims=True)
        score_low = half(probs * (prob_grad - inner))
        got.append(
            (product(keys_t, score_low), product(score_low, queries), product(probs_low, upstream))
        )
    row = lax.broadcasted_iota(jnp.int32, got[0][0].shape, 0)
    back_ref[:, column(at)] = half(jnp.where(row < 64, got[0][0], got[1][0]).T * 0.125)
    back_ref[:, column(3 + at)] = half(jnp.where(lane < 64, got[0][1], got[1][1]) * 0.125)
    back_ref[:, column(6 + at)] = half(jnp.where(lane < 64, got[0][2], got[1][2]))


def hidden_kernel(layer_at, mid_ref, up_w, down_w, vec_ref, bias_ref, out_ref, act_ref, slope_ref):
    normed, _ = normalize(mid_ref[...])
    hidden_low = half(normed * row_of(vec_ref, layer_at, 5) + row_of(vec_ref, layer_at, 6))
    total = mid_ref[...] + row_of(vec_ref, layer_at, 7)
    for chunk in range(4):
        rows = slice(chunk * WIDE, (chunk + 1) * WIDE)
        hidden = col_contract(hidden_low, up_w[rows]) + bias_ref[chunk : chunk + 1]
        share = 0.5 * (1.0 + lax.erf(hidden * half_root))
        active_low = half(hidden * share)
        act_ref[:, rows] = active_low
        slope_ref[:, rows] = share + hidden * jnp.exp(-0.5 * hidden * hidden) * density
        total = total + product(active_low, down_w[rows])
    out_ref[...] = total


def hidden_back_kernel(layer_at, up_ref, mid_ref, act_ref, slope_ref, up_w, down_w, vec_ref, grad_ref, gup_ref, gdown_ref, sum_ref, bias_ref):
    down_low = half(up_ref[...])
    normed, inv_std = normalize(mid_ref[...])
    gain = row_of(vec_ref, layer_at, 5)
    hidden_low = half(normed * gain + row_of(vec_ref, layer_at, 6))
    back_hidden = jnp.zeros(normed.shape, jnp.float32)
    for chunk in range(4):
        rows = slice(chunk * WIDE, (chunk + 1) * WIDE)
        up_low = half(col_contract(down_low, down_w[rows]) * slope_ref[:, rows])
        gdown_ref[rows] = half(row_contract(act_ref[:, rows], down_low))
        gup_ref[rows] = half(row_contract(up_low, hidden_low))
        bias_ref[chunk : chunk + 1] = jnp.sum(full(up_low), 0, keepdims=True)
        back_hidden = back_hidden + product(up_low, up_w[rows])
    sum_ref[0:1] = jnp.sum(back_hidden * normed, 0, keepdims=True)
    sum_ref[1:2] = jnp.sum(back_hidden, 0, keepdims=True)
    sum_ref[2:3] = jnp.sum(full(down_low), 0, keepdims=True)
    grad_ref[...] = up_ref[...] + norm_back(back_hidden, normed, inv_std, gain)


def layer_call(kernel, layer_at, ins, outs, scratch=(), name=None, vmem=24):
    def body(*refs):
        kernel(layer_at, *refs)

    return pl.pallas_call(
        body,
        out_shape=[jax.ShapeDtypeStruct(shape, kind) for shape, kind in outs],
        in_specs=[pl.BlockSpec(memory_space=pltpu.VMEM)] * len(ins),
        out_specs=[pl.BlockSpec(memory_space=pltpu.VMEM)] * len(outs),
        scratch_shapes=list(scratch),
        compiler_params=pltpu.CompilerParams(vmem_limit_bytes=vmem << 20),
        cost_estimate=pl.CostEstimate(flops=1 << 20, bytes_accessed=1 << 16, transcendentals=0),
        name=name,
    )(*ins)


def attention_forward(layer_at, inputs, w_qkv, w_out, vec_full):
    length = inputs.shape[0]
    return layer_call(
        attend_kernel,
        layer_at,
        [inputs, w_qkv, w_out, vec_full],
        [
            (inputs.shape, jnp.float32),
            ((length, 3 * WIDE), jnp.bfloat16),
            (inputs.shape, jnp.bfloat16),
            ((HEADS, length, length), jnp.bfloat16),
        ],
        name="attend",
    )


def attention_backward(layer_at, upstream, inputs, stored, w_qkv, w_out, vec_full):
    qkv_low, attn_low, probs = stored
    return layer_call(
        attend_back_kernel,
        layer_at,
        [upstream, inputs, qkv_low, attn_low, probs, w_qkv, w_out, vec_full],
        [
            (inputs.shape, jnp.float32),
            (w_qkv.shape, jnp.bfloat16),
            (w_out.shape, jnp.bfloat16),
            ((8, WIDE), jnp.float32),
        ],
        scratch=[
            pltpu.VMEM(attn_low.shape, jnp.bfloat16),
            pltpu.VMEM(qkv_low.shape, jnp.bfloat16),
        ],
        name="attend_back",
    )


def hidden_forward(layer_at, middle, w_up, w_down, vec_full, bias_up):
    wide = (middle.shape[0], FF)
    return layer_call(
        hidden_kernel,
        layer_at,
        [middle, w_up, w_down, vec_full, bias_up],
        [(middle.shape, jnp.float32), (wide, jnp.bfloat16), (wide, jnp.float32)],
        name="hidden",
    )


def hidden_backward(layer_at, upstream, middle, stored, w_up, w_down, vec_full):
    return layer_call(
        hidden_back_kernel,
        layer_at,
        [upstream, middle, *stored, w_up, w_down, vec_full],
        [
            (middle.shape, jnp.float32),
            (w_up.shape, jnp.bfloat16),
            (w_up.shape, jnp.bfloat16),
            ((8, WIDE), jnp.float32),
            ((4, WIDE), jnp.float32),
        ],
        name="hidden_back",
    )


def turn(parts, count):
    turned_parts = [jnp.roll(parts, -by, 0) for by in range(RINGX)]
    low = jnp.where((count & 1) == 0, turned_parts[0], turned_parts[1])
    high = jnp.where((count & 1) == 0, turned_parts[2], turned_parts[3])
    return jnp.where((count & 2) == 0, low, high)


def swap(parts, flag, axis):
    return jnp.where(flag == 0, parts, jnp.flip(parts, axis))


def to_own_order(row, place):
    cube = row.reshape(RINGX, 2, 2, BLK)
    cube = turn(swap(swap(cube, place[2], 2), place[1], 1), place[0])
    return cube.transpose(2, 1, 0, 3).reshape(4, WIDE)


def from_own_order(row, place):
    cube = row.reshape(2, 2, RINGX, BLK).transpose(2, 1, 0, 3)
    cube = swap(swap(turn(cube, (4 - place[0]) & 3), place[2], 2), place[1], 1)
    return cube.reshape(4, WIDE)


def on_device(tokens, cotangent, live, slot_of, weights, momentum, vec, vec_first, vec_second):
    place = my_place()
    group_at = lax.axis_index("group")
    data_at = lax.axis_index("dp")
    vec_here, vec_cols = vec.shape
    per_layer = VROWS // LAYERS
    tie = lax.optimization_barrier
    spread = lax.dynamic_update_slice(
        jnp.zeros((VPAD, WIDE), jnp.bfloat16),
        half(vec),
        (group_at * vec_here, data_at * vec_cols),
    )
    own_block = jnp.concatenate([half(weights[0].T), spread], 0)
    pair = jnp.concatenate([own_block, along_group(own_block, 1, 0)], 0)
    slots = [pair] + [along_group(pair, 0, -hops) for hops in (1, 2, 3)]
    first, third = small_call(
        choose_kernel,
        [(4 * BLK + VPAD, jnp.bfloat16), (4 * BLK, jnp.bfloat16)],
        [slot_of] + slots,
        slot_first=True,
        scratch=[pltpu.VMEM((MATS, BLK, WIDE), jnp.bfloat16)],
        name="choose",
    )
    first_x, second_x = small_call(
        merge_first_kernel,
        [(4 * BLK + VPAD, jnp.bfloat16), (8 * BLK, jnp.bfloat16)],
        from_x(first),
        scratch=[HOLD_HEADS],
        name="first_merge_x",
    )
    second_x, third, first_x = tie((second_x, third, first_x))
    first_parts = all_four(first_x)
    beside_second, core_second = other_row(second_x), other_core(second_x)
    third_parts = from_x(third)
    first_parts, third_parts = tie((first_parts, third_parts))
    w_qkv0, w_out0, vec_full = whole(first_parts, True, False, True, "first")
    (third_x,) = small_call(
        merge_third_kernel,
        [(12 * BLK, jnp.bfloat16)],
        third_parts,
        scratch=[HOLD_HEADS],
        name="third_merge_x",
    )
    bias0 = to_own_order(vec_full[8:12].reshape(-1), place)
    bias1 = to_own_order(vec_full[20:24].reshape(-1), place)

    inputs0 = tokens[0]
    middle0, *attn0 = attention_forward(0, inputs0, w_qkv0, w_out0, vec_full)
    third_x, beside_second, middle0 = tie((third_x, beside_second, middle0))
    beside = other_row(third_x)
    core_third = other_core(third_x)
    second_parts = [second_x, beside_second, core_second, other_core(beside_second)]
    w_up0, w_down0 = whole(second_parts, False, True, False, "second")
    inputs1, *mlp0 = hidden_forward(0, middle0, w_up0, w_down0, vec_full, bias0)
    beside, inputs1 = tie((beside, inputs1))
    third_parts = [third_x, beside, core_third, other_core(beside)]
    w_qkv1, w_out1, w_up1, w_down1 = whole(third_parts, True, True, False, "third")
    middle1, *attn1 = attention_forward(1, inputs1, w_qkv1, w_out1, vec_full)
    stream, *mlp1 = hidden_forward(1, middle1, w_up1, w_down1, vec_full, bias1)

    upstream = cotangent[0] * full(live)[0]
    mid_grad, grad_up, grad_down, sums_two1, sums_up1 = hidden_backward(
        1, upstream, middle1, mlp1, w_up1, w_down1, vec_full
    )
    upstream, grad_qkv, grad_out, sums_one1 = attention_backward(
        1, mid_grad, inputs1, attn1, w_qkv1, w_out1, vec_full
    )
    keep, sent = scatter_core([grad_qkv, grad_out, grad_up, grad_down], True, True, False, "third")
    upstream, sent = tie((upstream, sent))
    came = other_core(sent)
    mid_grad, grad_up, grad_down, sums_two0, sums_up0 = hidden_backward(
        0, upstream, middle0, mlp0, w_up0, w_down0, vec_full
    )
    keep_f, sent_f = scatter_core([grad_up, grad_down], False, True, False, "second")
    mid_grad, sent_f, came = tie((mid_grad, sent_f, came))
    came_f = other_core(sent_f)
    keep, sent = scatter_row(keep, came, True, True, False, "third")
    mid_grad, sent = tie((mid_grad, sent))
    came = other_row(sent)
    token_grad, grad_qkv, grad_out, sums_one0 = attention_backward(
        0, mid_grad, inputs0, attn0, w_qkv0, w_out0, vec_full
    )
    grad_qkv, came_f = tie((grad_qkv, came_f))
    keep_f, sent_f = scatter_row(keep_f, came_f, False, True, False, "second")
    grad_qkv, sent_f, came = tie((grad_qkv, sent_f, came))
    came_f = other_row(sent_f)
    bias_sum0, bias_sum1 = (from_own_order(part, place) for part in (sums_up0, sums_up1))
    vec_sum, keep_h, sent_h = scatter_core(
        [grad_qkv, grad_out, sums_one0, sums_two0, bias_sum0, sums_one1, sums_two1, bias_sum1],
        True,
        False,
        True,
        "first",
    )
    came_h = other_core(sent_h)
    came_h, came = tie((came_h, came))
    keep, *sent_x = scatter_x(keep, came, True, True, False, "third")
    came_x = spread_x(sent_x)
    came_f, came_x = tie((came_f, came_x))
    keep_h, sent_h, vec_sum = scatter_row(keep_h, came_h, True, False, True, "first", vec_sum)
    came_h = other_row(sent_h)
    keep_f, *sent_f = scatter_x(keep_f, came_f, False, True, False, "second")
    (third_sum,) = small_call(
        lambda *refs: sum_x_kernel(True, *refs),
        [(4 * BLK, jnp.float32)],
        [keep] + came_x,
        name="third_sum_x",
    )
    came_f = spread_x(sent_f)
    (second_sum,) = small_call(
        lambda *refs: sum_x_kernel(False, *refs),
        [(2 * BLK, jnp.float32)],
        [keep_f] + came_f,
        name="second_sum_x",
    )
    keep_h, *sent_h, vec_sum = scatter_x(keep_h, came_h, True, False, True, "first", vec_sum)
    came_h = spread_x(sent_h)
    own, *sent_g, vec_sum = small_call(
        split_group_kernel,
        [(BLK, jnp.float32)]
        + [(BLK + 2 * VPAD, jnp.bfloat16)] * 7
        + [(VPAD, jnp.float32)],
        [slot_of, second_sum, third_sum, keep_h] + came_h + [vec_sum],
        slot_first=True,
        scratch=[pltpu.VMEM((MATS, BLK, WIDE), jnp.float32)],
        name="split_group",
    )
    came_g = [along_group(part, flip, hops) for part, (flip, hops) in zip(sent_g, STEPS[1:])]
    grad_rows, moment_rows, moment_low, vec_sum = small_call(
        renew_kernel,
        [(BLK, jnp.float32), (BLK, jnp.float32), (BLK, jnp.bfloat16), (VPAD, jnp.float32)],
        [own] + came_g + [vec_sum, momentum[0].T],
        name="renew",
    )
    ring = jnp.concatenate([moment_low] + [along_x(moment_low, -hops) for hops in (1, 2, 3)], 0)
    beside = other_row(ring)
    (weight_rows,) = small_call(
        newton_kernel,
        [(BLK, jnp.float32)],
        [slot_of, ring, beside, other_core(ring), other_core(beside), moment_low, weights[0].T],
        slot_first=True,
        name="newton",
    )
    shard_vec = lax.dynamic_slice(
        vec_sum, (group_at * vec_here, data_at * vec_cols), (vec_here, vec_cols)
    )
    first_new = first_keep * vec_first + (1.0 - first_keep) * shard_vec
    second_new = second_keep * vec_second + (1.0 - second_keep) * shard_vec * shard_vec
    vec_new = vec - adam_rate * (
        first_new
        / (1.0 - first_keep**STEP)
        / (jnp.sqrt(second_new / (1.0 - second_keep**STEP)) + adam_eps)
    )
    return (
        stream[None],
        token_grad[None],
        grad_rows.T[None],
        moment_rows.T[None],
        weight_rows.T[None],
        first_new,
        second_new,
        vec_new,
    )


def solution(mesh):
    placed = (
        P(("group", "dp"), None, None),
        P(("group", "dp"), None, None),
        P(("group", "dp")),
        P(),
        P("group", None, "dp"),
        P("group", None, "dp"),
        P("group", "dp"),
        P("group", "dp"),
        P("group", "dp"),
    )
    return jax.shard_map(
        on_device,
        mesh=mesh,
        in_specs=placed,
        out_specs=(
            P(("group", "dp"), None, None),
            P(("group", "dp"), None, None),
            P("group", None, "dp"),
            P("group", None, "dp"),
            P("group", None, "dp"),
            P("group", "dp"),
            P("group", "dp"),
            P("group", "dp"),
        ),
        check_vma=False,
    )
```

profile of v0, /device:TPU:1, one launch (start us, length us, event | category | flops | bytes accessed | tf_op | source)
XLA Modules:
  0.0 291.9 jit_solution(13275877112215998926)
XLA Ops:
  2.8 3.8 %collective-permute-start = (bf16[128,384]{1,0:T(8,128)(2,1)S(1)}, bf16[128,384]{1,0:T(8,128)(2,1)S(1)}, u32[]{:S(2)}, u32[]{:S(2)}) collective-permute-start(bf16[128,384]{1,0:T(8,128)(2,1)S(1)} %pad_maximum_fusion.1), channel_id=1, source_target_pairs={{0,64},{16,80},{32,96},{48,112},{64,0},{80,16},{96,32},{112,48},{1... | collective-permute-start | bytes 294920 | tf_op jit(solution)/shard_map/ppermute | solution.py:102
  9.1 3.8 %collective-permute-start.1 = (bf16[256,384]{1,0:T(8,128)(2,1)S(1)}, bf16[256,384]{1,0:T(8,128)(2,1)S(1)}, u32[]{:S(2)}, u32[]{:S(2)}) collective-permute-start(bf16[256,384]{1,0:T(8,128)(2,1)S(1)} %pad_maximum_fusion.refs_0_), channel_id=1, source_target_pairs={{0,48},{16,0},{32,16},{48,32},{64,112},{80,64},{96,80},{112,96},{1... | collective-permute-start | bytes 589832 | tf_op jit(solution)/shard_map/ppermute | solution.py:102
  13.7 6.9 %collective-permute-done.1.refs_1_ = bf16[256,384]{1,0:T(8,128)(2,1)S(1)} collective-permute-done((bf16[256,384]{1,0:T(8,128)(2,1)S(1)}, bf16[256,384]{1,0:T(8,128)(2,1)S(1)}, u32[]{:S(2)}, u32[]{:S(2)}) %collective-permute-start.1) | collective-permute-done | bytes 196640 | tf_op jit(solution)/shard_map/ppermute | solution.py:102
  20.6 4.3 %collective-permute-done.3.refs_3_ = bf16[256,384]{1,0:T(8,128)(2,1)S(1)} collective-permute-done((bf16[256,384]{1,0:T(8,128)(2,1)S(1)}, bf16[256,384]{1,0:T(8,128)(2,1)S(1)}, u32[]{:S(2)}, u32[]{:S(2)}) %collective-permute-start.3) | collective-permute-done | bytes 196640 | tf_op jit(solution)/shard_map/ppermute | solution.py:102
  29.4 5.1 %collective-permute-done.4.refs_1_ = bf16[416,384]{1,0:T(8,128)(2,1)S(1)} collective-permute-done((bf16[416,384]{1,0:T(8,128)(2,1)S(1)}, bf16[416,384]{1,0:T(8,128)(2,1)S(1)}, u32[]{:S(2)}, u32[]{:S(2)}) %collective-permute-start.4) | collective-permute-done | bytes 319520 | tf_op jit(solution)/shard_map/ppermute | solution.py:85
  34.4 3.1 %collective-permute-done.5.refs_2_ = bf16[416,384]{1,0:T(8,128)(2,1)S(1)} collective-permute-done((bf16[416,384]{1,0:T(8,128)(2,1)S(1)}, bf16[416,384]{1,0:T(8,128)(2,1)S(1)}, u32[]{:S(2)}, u32[]{:S(2)}) %collective-permute-start.5) | collective-permute-done | bytes 319520 | tf_op jit(solution)/shard_map/ppermute | solution.py:85
  37.6 8.4 %collective-permute-done.6.refs_3_ = bf16[416,384]{1,0:T(8,128)(2,1)S(1)} collective-permute-done((bf16[416,384]{1,0:T(8,128)(2,1)S(1)}, bf16[416,384]{1,0:T(8,128)(2,1)S(1)}, u32[]{:S(2)}, u32[]{:S(2)}) %collective-permute-start.6) | collective-permute-done | bytes 319520 | tf_op jit(solution)/shard_map/ppermute | solution.py:85
  49.0 6.5 %collective-permute-done.7.refs_1_ = bf16[416,384]{1,0:T(8,128)(2,1)S(1)} collective-permute-done((bf16[416,384]{1,0:T(8,128)(2,1)S(1)}, bf16[416,384]{1,0:T(8,128)(2,1)S(1)}, u32[]{:S(2)}, u32[]{:S(2)}) %collective-permute-start.7) | collective-permute-done | bytes 319520 | tf_op jit(solution)/shard_map/ppermute | solution.py:85
  62.4 3.2 %collective-permute-done.10.refs_1_ = bf16[384,384]{1,0:T(8,128)(2,1)S(1)} collective-permute-done((bf16[384,384]{1,0:T(8,128)(2,1)S(1)}, bf16[384,384]{1,0:T(8,128)(2,1)S(1)}, u32[]{:S(2)}, u32[]{:S(2)}) %collective-permute-start.10) | collective-permute-done | bytes 294944 | tf_op jit(solution)/shard_map/ppermute | solution.py:85
  69.8 3.9 %collective-permute-done.12.refs_3_ = bf16[384,384]{1,0:T(8,128)(2,1)} collective-permute-done((bf16[384,384]{1,0:T(8,128)(2,1)S(1)}, bf16[384,384]{1,0:T(8,128)(2,1)}, u32[]{:S(2)}, u32[]{:S(2)}) %collective-permute-start.12) | collective-permute-done | bytes 294944 | tf_op jit(solution)/shard_map/ppermute | solution.py:85
  77.6 6.5 %attend.2 = (f32[577,384]{1,0:T(8,128)S(1)}, bf16[577,1152]{1,0:T(8,128)(2,1)S(1)}, bf16[577,384]{1,0:T(8,128)(2,1)S(1)}, bf16[6,577,577]{2,1,0:T(8,128)(2,1)S(1)}) custom-call(f32[577,384]{1,0:T(8,128)S(1)} %bitcast.38, bf16[1152,384]{1,0:T(8,128)(2,1)S(1)} %get-tuple-element.142.refs_1_.refs_5_, bf16[384,384]{1,0:T(8,128)(2,1)S(1)} %copy-done.21, ...), custom_call_target="tpu_custom_call" | custom-call | flops 1048576 | bytes 65536 | tf_op jit(solution)/shard_map/attend/pallas_call | solution.py:615
  94.8 2.7 collective-permute-done.16.refs_3_
  101.0 3.7 %hidden.2 = (f32[577,384]{1,0:T(8,128)S(1)}, bf16[577,1536]{1,0:T(8,128)(2,1)S(1)}, f32[577,1536]{1,0:T(8,128)S(1)}) custom-call(f32[577,384]{1,0:T(8,128)S(1)} %copy-done.3, bf16[1536,384]{1,0:T(8,128)(2,1)S(1)} %get-tuple-element.149.refs_1_.refs_4_, bf16[1536,384]{1,0:T(8,128)(2,1)S(1)} %get-tuple-element.150.refs_2_.refs_5_, ...), custom_call_target="tpu_custom_call" | custom-call | flops 1048576 | bytes 65536 | tf_op jit(solution)/shard_map/hidden/pallas_call | solution.py:615
  108.7 4.8 %collective-permute-done.14.refs_1_ = bf16[1152,384]{1,0:T(8,128)(2,1)} collective-permute-done((bf16[1152,384]{1,0:T(8,128)(2,1)}, bf16[1152,384]{1,0:T(8,128)(2,1)}, u32[]{:S(2)}, u32[]{:S(2)}) %collective-permute-start.14) | collective-permute-done | bytes 884768 | tf_op jit(solution)/shard_map/ppermute | solution.py:85
  119.9 6.5 %attend.3 = (f32[577,384]{1,0:T(8,128)S(1)}, bf16[577,1152]{1,0:T(8,128)(2,1)S(1)}, bf16[577,384]{1,0:T(8,128)(2,1)S(1)}, bf16[6,577,577]{2,1,0:T(8,128)(2,1)S(1)}) custom-call(f32[577,384]{1,0:T(8,128)S(1)} %copy-done.7, bf16[1152,384]{1,0:T(8,128)(2,1)S(1)} %get-tuple-element.154.refs_1_.refs_5_, bf16[384,384]{1,0:T(8,128)(2,1)S(1)} %get-tuple-element.155.refs_2_.refs_6_, ...), custom_call_target="tpu_custom_call" | custom-call | flops 1048576 | bytes 65536 | tf_op jit(solution)/shard_map/attend/pallas_call | solution.py:615
  126.5 3.8 %hidden.3 = (f32[577,384]{1,0:T(8,128)S(1)}, bf16[577,1536]{1,0:T(8,128)(2,1)S(1)}, f32[577,1536]{1,0:T(8,128)S(1)}) custom-call(f32[577,384]{1,0:T(8,128)S(1)} %get-tuple-element.156.refs_0_.refs_1_, bf16[1536,384]{1,0:T(8,128)(2,1)S(1)} %get-tuple-element.157.refs_1_.refs_4_, bf16[1536,384]{1,0:T(8,128)(2,1)S(1)} %get-tuple-element.158.refs_2_.refs_5_, ...), custom_call_target="tpu_custom_call" | custom-call | flops 1048576 | bytes 65536 | tf_op jit(solution)/shard_map/hidden/pallas_call | solution.py:615
  130.3 5.5 %hidden_back.2 = (f32[577,384]{1,0:T(8,128)S(1)}, bf16[1536,384]{1,0:T(8,128)(2,1)S(1)}, bf16[1536,384]{1,0:T(8,128)(2,1)S(1)}, f32[8,384]{1,0:T(8,128)S(1)}, f32[4,384]{1,0:T(4,128)S(1)}) custom-call(f32[577,384]{1,0:T(8,128)S(1)} %copy-done.5, f32[577,384]{1,0:T(8,128)S(1)} %get-tuple-element.156.refs_0_.refs_1_, ...), custom_call_target="tpu_custom_call" | custom-call | flops 1048576 | bytes 65536 | tf_op jit(solution)/shard_map/hidden_back/pallas_call | solution.py:615
  135.8 9.8 %attend_back.2 = (f32[577,384]{1,0:T(8,128)S(1)}, bf16[1152,384]{1,0:T(8,128)(2,1)S(1)}, bf16[384,384]{1,0:T(8,128)(2,1)S(1)}, f32[8,384]{1,0:T(8,128)S(1)}) custom-call(f32[577,384]{1,0:T(8,128)S(1)} %get-tuple-element.162.refs_0_, f32[577,384]{1,0:T(8,128)S(1)} %copy-done.7, bf16[577,1152]{1,0:T(8,128)(2,1)S(1)} %get-tuple-element.163.refs_2_, ...), custom_call_target="tpu_custom_call" | custom-call | flops 1048576 | bytes 65536 | tf_op jit(solution)/shard_map/attend_back/pallas_call | solution.py:615
  154.8 5.3 %hidden_back.3 = (f32[577,384]{1,0:T(8,128)S(1)}, bf16[1536,384]{1,0:T(8,128)(2,1)S(1)}, bf16[1536,384]{1,0:T(8,128)(2,1)S(1)}, f32[8,384]{1,0:T(8,128)S(1)}, f32[4,384]{1,0:T(4,128)S(1)}) custom-call(f32[577,384]{1,0:T(8,128)S(1)} %copy-done.32, f32[577,384]{1,0:T(8,128)S(1)} %copy-done.4, bf16[577,1536]{1,0:T(8,128)(2,1)S(1)} %copy-done.13, ...), custom_call_target="tpu_custom_call" | custom-call | flops 1048576 | bytes 65536 | tf_op jit(solution)/shard_map/hidden_back/pallas_call | solution.py:615
  169.9 2.9 third_split_row.1
  181.2 9.9 %attend_back.3 = (f32[577,384]{1,0:T(8,128)S(1)}, bf16[1152,384]{1,0:T(8,128)(2,1)S(1)}, bf16[384,384]{1,0:T(8,128)(2,1)S(1)}, f32[8,384]{1,0:T(8,128)S(1)}) custom-call(f32[577,384]{1,0:T(8,128)S(1)} %copy-done.30, f32[577,384]{1,0:T(8,128)S(1)} %bitcast.39, bf16[577,1152]{1,0:T(8,128)(2,1)S(1)} %copy-done.19, bf16[577,384]{1,0:T(8,128)(2,1)S(1)} %copy-done.39, ...), custom_call_target="tpu_custom_call" | custom-call | flops 1048576 | bytes 65536 | tf_op jit(solution)/shard_map/attend_back/pallas_call | solution.py:615
  200.1 3.3 %collective-permute-start.25 = (bf16[384,384]{1,0:T(8,128)(2,1)S(1)}, bf16[384,384]{1,0:T(8,128)(2,1)S(1)}, u32[]{:S(2)}, u32[]{:S(2)}) collective-permute-start(bf16[384,384]{1,0:T(8,128)(2,1)S(1)} %get-tuple-element.211), channel_id=1, source_target_pairs={{0,8},{1,9},{2,10},{3,11},{4,12},{5,13},{6,14},{7,15},{8,0},{9,1},... | collective-permute-start | bytes 884744 | tf_op jit(solution)/shard_map/ppermute | solution.py:85
  204.9 6.7 %collective-permute-done.22.refs_1_ = bf16[768,384]{1,0:T(8,128)(2,1)S(1)} collective-permute-done((bf16[768,384]{1,0:T(8,128)(2,1)S(1)}, bf16[768,384]{1,0:T(8,128)(2,1)S(1)}, u32[]{:S(2)}, u32[]{:S(2)}) %collective-permute-start.22) | collective-permute-done | bytes 589856 | tf_op jit(solution)/shard_map/ppermute | solution.py:85
  211.7 4.8 %collective-permute-done.25.refs_2_ = bf16[384,384]{1,0:T(8,128)(2,1)S(1)} collective-permute-done((bf16[384,384]{1,0:T(8,128)(2,1)S(1)}, bf16[384,384]{1,0:T(8,128)(2,1)S(1)}, u32[]{:S(2)}, u32[]{:S(2)}) %collective-permute-start.25) | collective-permute-done | bytes 294944 | tf_op jit(solution)/shard_map/ppermute | solution.py:85
  219.3 3.3 %collective-permute-start.32 = (bf16[256,384]{1,0:T(8,128)(2,1)S(1)}, bf16[256,384]{1,0:T(8,128)(2,1)S(1)}, u32[]{:S(2)}, u32[]{:S(2)}) collective-permute-start(bf16[256,384]{1,0:T(8,128)(2,1)S(1)} %get-tuple-element.230), channel_id=1, source_target_pairs={{0,8},{1,9},{2,10},{3,11},{4,12},{5,13},{6,14},{7,15},{8,0},{9,1},... | collective-permute-start | bytes 589832 | tf_op jit(solution)/shard_map/ppermute | solution.py:85
  226.6 9.8 %collective-permute-done.28.refs_2_ = bf16[192,384]{1,0:T(8,128)(2,1)S(1)} collective-permute-done((bf16[192,384]{1,0:T(8,128)(2,1)S(1)}, bf16[192,384]{1,0:T(8,128)(2,1)S(1)}, u32[]{:S(2)}, u32[]{:S(2)}) %collective-permute-start.28) | collective-permute-done | bytes 147488 | tf_op jit(solution)/shard_map/ppermute | solution.py:85
  240.8 2.9 %collective-permute-start.37 = (bf16[160,384]{1,0:T(8,128)(2,1)S(1)}, bf16[160,384]{1,0:T(8,128)(2,1)S(1)}, u32[]{:S(2)}, u32[]{:S(2)}) collective-permute-start(bf16[160,384]{1,0:T(8,128)(2,1)S(1)} %get-tuple-element.237), channel_id=1, source_target_pairs={{0,64},{16,80},{32,96},{48,112},{64,0},{80,16},{96,32},{112,48},{1... | collective-permute-start | bytes 368648 | tf_op jit(solution)/shard_map/ppermute | solution.py:102
  244.3 3.6 %collective-permute-start.39 = (bf16[160,384]{1,0:T(8,128)(2,1)S(1)}, bf16[160,384]{1,0:T(8,128)(2,1)S(1)}, u32[]{:S(2)}, u32[]{:S(2)}) collective-permute-start(bf16[160,384]{1,0:T(8,128)(2,1)S(1)} %get-tuple-element.239), channel_id=1, source_target_pairs={{0,96},{16,112},{32,64},{48,80},{64,32},{80,48},{96,0},{112,16},{1... | collective-permute-start | bytes 368648 | tf_op jit(solution)/shard_map/ppermute | solution.py:102
  256.5 3.6 %collective-permute-start.41 = (bf16[96,384]{1,0:T(8,128)(2,1)S(1)}, bf16[96,384]{1,0:T(8,128)(2,1)S(1)}, u32[]{:S(2)}, u32[]{:S(2)}) collective-permute-start(bf16[96,384]{1,0:T(8,128)(2,1)S(1)} %get-tuple-element.244.refs_4_), channel_id=1, source_target_pairs={{0,12},{1,13},{2,14},{3,15},{4,0},{5,1},{6,2},{7,3},{8,4},{9,5},{1... | collective-permute-start | bytes 221192 | tf_op jit(solution)/shard_map/ppermute | solution.py:85
  266.6 4.2 %collective-permute-start.45 = (bf16[384,384]{1,0:T(8,128)(2,1)S(1)}, bf16[384,384]{1,0:T(8,128)(2,1)S(1)}, u32[]{:S(2)}, u32[]{:S(2)}) collective-permute-start(bf16[384,384]{1,0:T(8,128)(2,1)S(1)} %constant_dynamic-update-slice_fusion.refs_0_), channel_id=1, source_target_pairs={{0,1},{1,0},{2,3},{3,2},{4,5},{5,4},{6,7},{7,6},{8,9},{9,8},{10,11... | collective-permute-start | bytes 884744 | tf_op jit(solution)/shard_map/ppermute | solution.py:85
  271.3 4.8 %collective-permute-start.46 = (bf16[384,384]{1,0:T(8,128)(2,1)S(1)}, bf16[384,384]{1,0:T(8,128)(2,1)S(1)}, u32[]{:S(2)}, u32[]{:S(2)}) collective-permute-start(bf16[384,384]{1,0:T(8,128)(2,1)S(1)} %collective-permute-done.44.refs_1_), channel_id=1, source_target_pairs={{0,1},{1,0},{2,3},{3,2},{4,5},{5,4},{6,7},{7,6},{8,9},{9,8},{10,11... | collective-permute-start | bytes 884744 | tf_op jit(solution)/shard_map/ppermute | solution.py:85
  280.4 11.3 %newton.1 = f32[96,384]{1,0:T(8,128)} custom-call(s32[8]{0:T(128)S(1)} %copy-done.50, bf16[384,384]{1,0:T(8,128)(2,1)S(1)} %constant_dynamic-update-slice_fusion.refs_0_, bf16[384,384]{1,0:T(8,128)(2,1)S(1)} %collective-permute-done.44.refs_1_, bf16[384,384]{1,0:T(8,128)(2,1)S(1)} %collective-permute-done.45.refs_2_, ...), custom_call_target="tpu_custom_call" | custom-call | tf_op jit(solution)/shard_map/newton/pallas_call | solution.py:123
  (253 shorter events, 120.9 us)
Async XLA Ops:
  9.1 11.4 %collective-permute-start.1 = (bf16[256,384]{1,0:T(8,128)(2,1)S(1)}, bf16[256,384]{1,0:T(8,128)(2,1)S(1)}, u32[]{:S(2)}, u32[]{:S(2)}) collective-permute-start(bf16[256,384]{1,0:T(8,128)(2,1)S(1)} %pad_maximum_fusion.refs_0_), channel_id=1, source_target_pairs={{0,48},{16,0},{32,16},{48,32},{64,112},{80,64},{96,80},{112,96},{1... | collective-permute-start | bytes 589832 | tf_op jit(solution)/shard_map/ppermute | solution.py:102
  13.0 11.9 %collective-permute-start.3 = (bf16[256,384]{1,0:T(8,128)(2,1)S(1)}, bf16[256,384]{1,0:T(8,128)(2,1)S(1)}, u32[]{:S(2)}, u32[]{:S(2)}) collective-permute-start(bf16[256,384]{1,0:T(8,128)(2,1)S(1)} %pad_maximum_fusion.refs_0_), channel_id=1, source_target_pairs={{0,16},{16,32},{32,48},{48,0},{64,80},{80,96},{96,112},{112,64},{1... | collective-permute-start | bytes 589832 | tf_op jit(solution)/shard_map/ppermute | solution.py:102
  28.2 9.4 %collective-permute-start.5 = (bf16[416,384]{1,0:T(8,128)(2,1)S(1)}, bf16[416,384]{1,0:T(8,128)(2,1)S(1)}, u32[]{:S(2)}, u32[]{:S(2)}) collective-permute-start(bf16[416,384]{1,0:T(8,128)(2,1)S(1)} %get-tuple-element.127.refs_0_), channel_id=1, source_target_pairs={{0,8},{1,9},{2,10},{3,11},{4,12},{5,13},{6,14},{7,15},{8,0},{9,1},... | collective-permute-start | bytes 958472 | tf_op jit(solution)/shard_map/ppermute | solution.py:85
  28.8 17.2 %collective-permute-start.6 = (bf16[416,384]{1,0:T(8,128)(2,1)S(1)}, bf16[416,384]{1,0:T(8,128)(2,1)S(1)}, u32[]{:S(2)}, u32[]{:S(2)}) collective-permute-start(bf16[416,384]{1,0:T(8,128)(2,1)S(1)} %get-tuple-element.127.refs_0_), channel_id=1, source_target_pairs={{0,4},{1,5},{2,6},{3,7},{4,8},{5,9},{6,10},{7,11},{8,12},{9,13},{1... | collective-permute-start | bytes 958472 | tf_op jit(solution)/shard_map/ppermute | solution.py:85
  48.2 25.5 %collective-permute-start.8 = (bf16[416,384]{1,0:T(8,128)(2,1)S(1)}, bf16[416,384]{1,0:T(8,128)(2,1)S(1)}, u32[]{:S(2)}, u32[]{:S(2)}) collective-permute-start(bf16[416,384]{1,0:T(8,128)(2,1)S(1)} %get-tuple-element.138.refs_0_), channel_id=1, source_target_pairs={{0,1},{1,0},{2,3},{3,2},{4,5},{5,4},{6,7},{7,6},{8,9},{9,8},{10,11... | collective-permute-start | bytes 958472 | tf_op jit(solution)/shard_map/ppermute | solution.py:85
  55.6 18.2 %collective-permute-start.9 = (bf16[416,384]{1,0:T(8,128)(2,1)S(1)}, bf16[416,384]{1,0:T(8,128)(2,1)S(1)}, u32[]{:S(2)}, u32[]{:S(2)}) collective-permute-start(bf16[416,384]{1,0:T(8,128)(2,1)S(1)} %collective-permute-done.7.refs_1_), channel_id=1, source_target_pairs={{0,1},{1,0},{2,3},{3,2},{4,5},{5,4},{6,7},{7,6},{8,9},{9,8},{10,11... | collective-permute-start | bytes 958472 | tf_op jit(solution)/shard_map/ppermute | solution.py:85
  56.9 8.7 %collective-permute-start.10 = (bf16[384,384]{1,0:T(8,128)(2,1)S(1)}, bf16[384,384]{1,0:T(8,128)(2,1)S(1)}, u32[]{:S(2)}, u32[]{:S(2)}) collective-permute-start(bf16[384,384]{1,0:T(8,128)(2,1)S(1)} %get-tuple-element.133.refs_0_), channel_id=1, source_target_pairs={{0,12},{1,13},{2,14},{3,15},{4,0},{5,1},{6,2},{7,3},{8,4},{9,5},{1... | collective-permute-start | bytes 884744 | tf_op jit(solution)/shard_map/ppermute | solution.py:85
  56.9 10.7 %collective-permute-start.11 = (bf16[384,384]{1,0:T(8,128)(2,1)S(1)}, bf16[384,384]{1,0:T(8,128)(2,1)S(1)}, u32[]{:S(2)}, u32[]{:S(2)}) collective-permute-start(bf16[384,384]{1,0:T(8,128)(2,1)S(1)} %get-tuple-element.133.refs_0_), channel_id=1, source_target_pairs={{0,8},{1,9},{2,10},{3,11},{4,12},{5,13},{6,14},{7,15},{8,0},{9,1},... | collective-permute-start | bytes 884744 | tf_op jit(solution)/shard_map/ppermute | solution.py:85
  57.5 16.3 %collective-permute-start.12 = (bf16[384,384]{1,0:T(8,128)(2,1)S(1)}, bf16[384,384]{1,0:T(8,128)(2,1)}, u32[]{:S(2)}, u32[]{:S(2)}) collective-permute-start(bf16[384,384]{1,0:T(8,128)(2,1)S(1)} %get-tuple-element.133.refs_0_), channel_id=1, source_target_pairs={{0,4},{1,5},{2,6},{3,7},{4,8},{5,9},{6,10},{7,11},{8,12},{9,13},{1... | collective-permute-start | bytes 884744 | tf_op jit(solution)/shard_map/ppermute | solution.py:85
  66.3 26.0 %collective-permute-start.13 = (bf16[768,384]{1,0:T(8,128)(2,1)}, bf16[768,384]{1,0:T(8,128)(2,1)}, u32[]{:S(2)}, u32[]{:S(2)}) collective-permute-start(bf16[768,384]{1,0:T(8,128)(2,1)} %get-tuple-element.137.refs_0_), channel_id=1, source_target_pairs={{0,2},{1,3},{2,0},{3,1},{4,6},{5,7},{6,4},{7,5},{8,10},{9,11},{10,... | collective-permute-start | bytes 1769480 | tf_op jit(solution)/shard_map/ppermute | solution.py:85
  68.3 26.4 %collective-permute-start.15 = (bf16[768,384]{1,0:T(8,128)(2,1)}, bf16[768,384]{1,0:T(8,128)(2,1)}, u32[]{:S(2)}, u32[]{:S(2)}) collective-permute-start(bf16[768,384]{1,0:T(8,128)(2,1)} %get-tuple-element.137.refs_0_), channel_id=1, source_target_pairs={{0,1},{1,0},{2,3},{3,2},{4,5},{5,4},{6,7},{7,6},{8,9},{9,8},{10,11... | collective-permute-start | bytes 1769480 | tf_op jit(solution)/shard_map/ppermute | solution.py:85
  92.4 21.1 %collective-permute-start.14 = (bf16[1152,384]{1,0:T(8,128)(2,1)}, bf16[1152,384]{1,0:T(8,128)(2,1)}, u32[]{:S(2)}, u32[]{:S(2)}) collective-permute-start(bf16[1152,384]{1,0:T(8,128)(2,1)} %third_merge_x.1.refs_0_), channel_id=1, source_target_pairs={{0,2},{1,3},{2,0},{3,1},{4,6},{5,7},{6,4},{7,5},{8,10},{9,11},{10,... | collective-permute-start | bytes 2654216 | tf_op jit(solution)/shard_map/ppermute | solution.py:85
  93.7 21.6 %collective-permute-start.17 = (bf16[1152,384]{1,0:T(8,128)(2,1)}, bf16[1152,384]{1,0:T(8,128)(2,1)}, u32[]{:S(2)}, u32[]{:S(2)}) collective-permute-start(bf16[1152,384]{1,0:T(8,128)(2,1)} %third_merge_x.1.refs_0_), channel_id=1, source_target_pairs={{0,1},{1,0},{2,3},{3,2},{4,5},{5,4},{6,7},{7,6},{8,9},{9,8},{10,11... | collective-permute-start | bytes 2654216 | tf_op jit(solution)/shard_map/ppermute | solution.py:85
  148.5 19.7 %collective-permute-start.19 = (bf16[2304,384]{1,0:T(8,128)(2,1)}, bf16[2304,384]{1,0:T(8,128)(2,1)}, u32[]{:S(2)}, u32[]{:S(2)}) collective-permute-start(bf16[2304,384]{1,0:T(8,128)(2,1)} %get-tuple-element.179), channel_id=1, source_target_pairs={{0,1},{1,0},{2,3},{3,2},{4,5},{5,4},{6,7},{7,6},{8,9},{9,8},{10,11... | collective-permute-start | bytes 5308424 | tf_op jit(solution)/shard_map/ppermute | solution.py:85
  168.2 22.9 %collective-permute-start.20 = (bf16[1536,384]{1,0:T(8,128)(2,1)}, bf16[1536,384]{1,0:T(8,128)(2,1)}, u32[]{:S(2)}, u32[]{:S(2)}) collective-permute-start(bf16[1536,384]{1,0:T(8,128)(2,1)} %get-tuple-element.191), channel_id=1, source_target_pairs={{0,1},{1,0},{2,3},{3,2},{4,5},{5,4},{6,7},{7,6},{8,9},{9,8},{10,11... | collective-permute-start | bytes 3538952 | tf_op jit(solution)/shard_map/ppermute | solution.py:85
  174.0 21.4 %collective-permute-start.21 = (bf16[1152,384]{1,0:T(8,128)(2,1)}, bf16[1152,384]{1,0:T(8,128)(2,1)}, u32[]{:S(2)}, u32[]{:S(2)}) collective-permute-start(bf16[1152,384]{1,0:T(8,128)(2,1)} %get-tuple-element.196), channel_id=1, source_target_pairs={{0,2},{1,3},{2,0},{3,1},{4,6},{5,7},{6,4},{7,5},{8,10},{9,11},{10,... | collective-permute-start | bytes 2654216 | tf_op jit(solution)/shard_map/ppermute | solution.py:85
  196.8 14.9 %collective-permute-start.22 = (bf16[768,384]{1,0:T(8,128)(2,1)S(1)}, bf16[768,384]{1,0:T(8,128)(2,1)S(1)}, u32[]{:S(2)}, u32[]{:S(2)}) collective-permute-start(bf16[768,384]{1,0:T(8,128)(2,1)S(1)} %get-tuple-element.197), channel_id=1, source_target_pairs={{0,2},{1,3},{2,0},{3,1},{4,6},{5,7},{6,4},{7,5},{8,10},{9,11},{10,... | collective-permute-start | bytes 1769480 | tf_op jit(solution)/shard_map/ppermute | solution.py:85
  200.0 11.7 %collective-permute-start.24 = (bf16[384,384]{1,0:T(8,128)(2,1)S(1)}, bf16[384,384]{1,0:T(8,128)(2,1)S(1)}, u32[]{:S(2)}, u32[]{:S(2)}) collective-permute-start(bf16[384,384]{1,0:T(8,128)(2,1)S(1)} %get-tuple-element.210), channel_id=1, source_target_pairs={{0,4},{1,5},{2,6},{3,7},{4,8},{5,9},{6,10},{7,11},{8,12},{9,13},{1... | collective-permute-start | bytes 884744 | tf_op jit(solution)/shard_map/ppermute | solution.py:85
  200.1 16.4 %collective-permute-start.25 = (bf16[384,384]{1,0:T(8,128)(2,1)S(1)}, bf16[384,384]{1,0:T(8,128)(2,1)S(1)}, u32[]{:S(2)}, u32[]{:S(2)}) collective-permute-start(bf16[384,384]{1,0:T(8,128)(2,1)S(1)} %get-tuple-element.211), channel_id=1, source_target_pairs={{0,8},{1,9},{2,10},{3,11},{4,12},{5,13},{6,14},{7,15},{8,0},{9,1},... | collective-permute-start | bytes 884744 | tf_op jit(solution)/shard_map/ppermute | solution.py:85
  203.4 13.1 %collective-permute-start.26 = (bf16[384,384]{1,0:T(8,128)(2,1)S(1)}, bf16[384,384]{1,0:T(8,128)(2,1)S(1)}, u32[]{:S(2)}, u32[]{:S(2)}) collective-permute-start(bf16[384,384]{1,0:T(8,128)(2,1)S(1)} %get-tuple-element.212), channel_id=1, source_target_pairs={{0,12},{1,13},{2,14},{3,15},{4,0},{5,1},{6,2},{7,3},{8,4},{9,5},{1... | collective-permute-start | bytes 884744 | tf_op jit(solution)/shard_map/ppermute | solution.py:85
  203.6 15.5 %collective-permute-start.30 = (bf16[448,384]{1,0:T(8,128)(2,1)S(1)}, bf16[448,384]{1,0:T(8,128)(2,1)S(1)}, u32[]{:S(2)}, u32[]{:S(2)}) collective-permute-start(bf16[448,384]{1,0:T(8,128)(2,1)S(1)} %get-tuple-element.226), channel_id=1, source_target_pairs={{0,2},{1,3},{2,0},{3,1},{4,6},{5,7},{6,4},{7,5},{8,10},{9,11},{10,... | collective-permute-start | bytes 1032200 | tf_op jit(solution)/shard_map/ppermute | solution.py:85
  219.2 17.9 %collective-permute-start.31 = (bf16[256,384]{1,0:T(8,128)(2,1)S(1)}, bf16[256,384]{1,0:T(8,128)(2,1)S(1)}, u32[]{:S(2)}, u32[]{:S(2)}) collective-permute-start(bf16[256,384]{1,0:T(8,128)(2,1)S(1)} %get-tuple-element.229), channel_id=1, source_target_pairs={{0,4},{1,5},{2,6},{3,7},{4,8},{5,9},{6,10},{7,11},{8,12},{9,13},{1... | collective-permute-start | bytes 589832 | tf_op jit(solution)/shard_map/ppermute | solution.py:85
  219.3 17.9 %collective-permute-start.32 = (bf16[256,384]{1,0:T(8,128)(2,1)S(1)}, bf16[256,384]{1,0:T(8,128)(2,1)S(1)}, u32[]{:S(2)}, u32[]{:S(2)}) collective-permute-start(bf16[256,384]{1,0:T(8,128)(2,1)S(1)} %get-tuple-element.230), channel_id=1, source_target_pairs={{0,8},{1,9},{2,10},{3,11},{4,12},{5,13},{6,14},{7,15},{8,0},{9,1},... | collective-permute-start | bytes 589832 | tf_op jit(solution)/shard_map/ppermute | solution.py:85
  222.6 14.6 %collective-permute-start.33 = (bf16[256,384]{1,0:T(8,128)(2,1)S(1)}, bf16[256,384]{1,0:T(8,128)(2,1)S(1)}, u32[]{:S(2)}, u32[]{:S(2)}) collective-permute-start(bf16[256,384]{1,0:T(8,128)(2,1)S(1)} %get-tuple-element.231), channel_id=1, source_target_pairs={{0,12},{1,13},{2,14},{3,15},{4,0},{5,1},{6,2},{7,3},{8,4},{9,5},{1... | collective-permute-start | bytes 589832 | tf_op jit(solution)/shard_map/ppermute | solution.py:85
  223.6 12.7 %collective-permute-start.28 = (bf16[192,384]{1,0:T(8,128)(2,1)S(1)}, bf16[192,384]{1,0:T(8,128)(2,1)S(1)}, u32[]{:S(2)}, u32[]{:S(2)}) collective-permute-start(bf16[192,384]{1,0:T(8,128)(2,1)S(1)} %get-tuple-element.216), channel_id=1, source_target_pairs={{0,8},{1,9},{2,10},{3,11},{4,12},{5,13},{6,14},{7,15},{8,0},{9,1},... | collective-permute-start | bytes 442376 | tf_op jit(solution)/shard_map/ppermute | solution.py:85
  224.3 12.7 %collective-permute-start.29 = (bf16[192,384]{1,0:T(8,128)(2,1)S(1)}, bf16[192,384]{1,0:T(8,128)(2,1)S(1)}, u32[]{:S(2)}, u32[]{:S(2)}) collective-permute-start(bf16[192,384]{1,0:T(8,128)(2,1)S(1)} %get-tuple-element.217), channel_id=1, source_target_pairs={{0,12},{1,13},{2,14},{3,15},{4,0},{5,1},{6,2},{7,3},{8,4},{9,5},{1... | collective-permute-start | bytes 442376 | tf_op jit(solution)/shard_map/ppermute | solution.py:85
  238.1 9.9 %collective-permute-start.35 = (bf16[160,384]{1,0:T(8,128)(2,1)S(1)}, bf16[160,384]{1,0:T(8,128)(2,1)S(1)}, u32[]{:S(2)}, u32[]{:S(2)}) collective-permute-start(bf16[160,384]{1,0:T(8,128)(2,1)S(1)} %get-tuple-element.235), channel_id=1, source_target_pairs={{0,32},{16,48},{32,0},{48,16},{64,96},{80,112},{96,64},{112,80},{1... | collective-permute-start | bytes 368648 | tf_op jit(solution)/shard_map/ppermute | solution.py:102
  238.4 11.9 %collective-permute-start.36 = (bf16[160,384]{1,0:T(8,128)(2,1)S(1)}, bf16[160,384]{1,0:T(8,128)(2,1)S(1)}, u32[]{:S(2)}, u32[]{:S(2)}) collective-permute-start(bf16[160,384]{1,0:T(8,128)(2,1)S(1)} %get-tuple-element.236), channel_id=1, source_target_pairs={{0,48},{16,0},{32,16},{48,32},{64,112},{80,64},{96,80},{112,96},{1... | collective-permute-start | bytes 368648 | tf_op jit(solution)/shard_map/ppermute | solution.py:102
  240.8 9.5 %collective-permute-start.37 = (bf16[160,384]{1,0:T(8,128)(2,1)S(1)}, bf16[160,384]{1,0:T(8,128)(2,1)S(1)}, u32[]{:S(2)}, u32[]{:S(2)}) collective-permute-start(bf16[160,384]{1,0:T(8,128)(2,1)S(1)} %get-tuple-element.237), channel_id=1, source_target_pairs={{0,64},{16,80},{32,96},{48,112},{64,0},{80,16},{96,32},{112,48},{1... | collective-permute-start | bytes 368648 | tf_op jit(solution)/shard_map/ppermute | solution.py:102
  244.3 9.1 %collective-permute-start.39 = (bf16[160,384]{1,0:T(8,128)(2,1)S(1)}, bf16[160,384]{1,0:T(8,128)(2,1)S(1)}, u32[]{:S(2)}, u32[]{:S(2)}) collective-permute-start(bf16[160,384]{1,0:T(8,128)(2,1)S(1)} %get-tuple-element.239), channel_id=1, source_target_pairs={{0,96},{16,112},{32,64},{48,80},{64,32},{80,48},{96,0},{112,16},{1... | collective-permute-start | bytes 368648 | tf_op jit(solution)/shard_map/ppermute | solution.py:102
  266.6 13.9 %collective-permute-start.45 = (bf16[384,384]{1,0:T(8,128)(2,1)S(1)}, bf16[384,384]{1,0:T(8,128)(2,1)S(1)}, u32[]{:S(2)}, u32[]{:S(2)}) collective-permute-start(bf16[384,384]{1,0:T(8,128)(2,1)S(1)} %constant_dynamic-update-slice_fusion.refs_0_), channel_id=1, source_target_pairs={{0,1},{1,0},{2,3},{3,2},{4,5},{5,4},{6,7},{7,6},{8,9},{9,8},{10,11... | collective-permute-start | bytes 884744 | tf_op jit(solution)/shard_map/ppermute | solution.py:85
  271.3 9.1 %collective-permute-start.46 = (bf16[384,384]{1,0:T(8,128)(2,1)S(1)}, bf16[384,384]{1,0:T(8,128)(2,1)S(1)}, u32[]{:S(2)}, u32[]{:S(2)}) collective-permute-start(bf16[384,384]{1,0:T(8,128)(2,1)S(1)} %collective-permute-done.44.refs_1_), channel_id=1, source_target_pairs={{0,1},{1,0},{2,3},{3,2},{4,5},{5,4},{6,7},{7,6},{8,9},{9,8},{10,11... | collective-permute-start | bytes 884744 | tf_op jit(solution)/shard_map/ppermute | solution.py:85
  (69 other events, 319.5 us)
where the time goes:
time: 297 us; the launch traced here: 292 us
  waiting for transfers between devices  90.8 us (31%)
  Pallas kernels  81.5 us (27%)
  starting transfers between devices  67.2 us (23%)
  local copies, waits for them, and re-layouts  45.7 us (15%)
  other arithmetic  4.62 us (2%)
    ppermute x36, waiting for transfers between devices, near(): return lax.ppermute(part, 'dp', [(at, change(at)) for at in range(16)])  71.4 us
    pallas_call x8, Pallas kernels, layer_call(): pl.pallas_call(body, out_shape=[jax.ShapeDtypeStruct(shape, kind) for sha...  51.1 us
    ppermute x36, starting transfers between devices, near(): return lax.ppermute(part, 'dp', [(at, change(at)) for at in range(16)])  46.9 us
    unnamed x114, local copies, waits for them, and re-layouts  44.3 us
    pallas_call x20, Pallas kernels, small_call(): pl.pallas_call(kernel, out_shape=[jax.ShapeDtypeStruct((rows, WIDE), kind...  30.4 us
    ppermute x11, starting transfers between devices, along_group(): return lax.ppermute(part, 'group', pairs)  20.3 us
    ppermute x11, waiting for transfers between devices, along_group(): return lax.ppermute(part, 'group', pairs)  19.3 us
  transfers between devices with their start and end apart: 47, of which 27 were waited for; matrix products, arithmetic and copies ran while one was open for 3% of the time, Pallas kernels for 13%

commit v1 on v0

--- a/solution.py
+++ b/solution.py
@@ -116,17 +116,44 @@
     return pl.ds(pl.multiple_of(start, 32), count)
 
 
-def small_call(kernel, outs, ins, slot_first=False, scratch=(), name=None, vmem=12):
-    specs = [pl.BlockSpec(memory_space=pltpu.VMEM)] * len(ins)
-    if slot_first:
-        specs[0] = pl.BlockSpec(memory_space=pltpu.SMEM)
+def far_spec():
+    return pl.BlockSpec(memory_space=pltpu.HBM)
+
+
+def small_call(kernel, outs, ins, slot_first=False, scratch=(), name=None, vmem=64):
+    lead, count, total = int(slot_first), len(ins) - int(slot_first), len(outs)
+
+    def body(*refs):
+        far, near = refs[lead : lead + count + total], refs[lead + count + total :]
+        sems, rest = near[count + total], near[count + total + 1 :]
+        come = [
+            pltpu.make_async_copy(far[at], near[at], sems.at[at]) for at in range(count)
+        ]
+        for copy in come:
+            copy.start()
+        for copy in come:
+            copy.wait()
+        kernel(*refs[:lead], *near[: count + total], *rest)
+        leave = [
+            pltpu.make_async_copy(near[at], far[at], sems.at[at])
+            for at in range(count, count + total)
+        ]
+        for copy in leave:
+            copy.start()
+        for copy in leave:
+            copy.wait()
+
     return pl.pallas_call(
-        kernel,
+        body,
         out_shape=[jax.ShapeDtypeStruct((rows, WIDE), kind) for rows, kind in outs],
-        in_specs=specs,
-        out_specs=[pl.BlockSpec(memory_space=pltpu.VMEM)] * len(outs),
-        scratch_shapes=list(scratch),
+        in_specs=[pl.BlockSpec(memory_space=pltpu.SMEM)] * lead + [far_spec()] * count,
+        out_specs=[far_spec()] * total,
+        scratch_shapes=[pltpu.VMEM(part.shape, part.dtype) for part in ins[lead:]]
+        + [pltpu.VMEM((rows, WIDE), kind) for rows, kind in outs]
+        + [pltpu.SemaphoreType.DMA((count + total,))]
+        + list(scratch),
         compiler_params=pltpu.CompilerParams(vmem_limit_bytes=vmem << 20),
+        cost_estimate=pl.CostEstimate(flops=1 << 20, bytes_accessed=1 << 16, transcendentals=0),
         name=name,
     )(*ins)
 
@@ -245,40 +272,18 @@
     return full(ref[start : start + VPAD]) + full(ref[start + VPAD : start + 2 * VPAD])
 
 
-def split_core_kernel(heads, hidden, spread, *refs):
-    refs = list(refs)
-    keep_ref, sent_ref = refs[-2:]
+def split_heads(grads, keep_ref, sent_ref):
     _, _, core = my_place()
     put = 0
-    if heads:
-        qkv_ref, out_ref = refs[:2]
-        refs = refs[2:]
-        for row in range(2):
-            for at in range(4):
-                source = out_ref if at == 3 else qkv_ref
-                start = (0 if at == 3 else at * WIDE) + row * 2 * BLK
-                keep_ref[put : put + BLK] = source[rows_at(start + core * BLK)]
-                sent_ref[put : put + BLK] = source[rows_at(start + (1 - core) * BLK)]
-                put += BLK
-    if hidden:
-        for source in refs[:2]:
-            keep_ref[put : put + 2 * WIDE] = source[: 2 * WIDE]
-            sent_ref[put : put + 2 * WIDE] = source[2 * WIDE :]
-            put += 2 * WIDE
-        refs = refs[2:]
-    if spread:
-        *pieces, vec_ref = refs[:-2]
-        vec_ref[VROWS:] = jnp.zeros((VPAD - VROWS, WIDE), jnp.float32)
-        for layer_at in range(LAYERS):
-            base = layer_at * (VROWS // LAYERS)
-            one, two, three = pieces[3 * layer_at : 3 * layer_at + 3]
-            vec_ref[base : base + 5] = one[:5]
-            vec_ref[base + 5 : base + 8] = two[:3]
-            vec_ref[base + 8 : base + 12] = three[...]
-        put_vec(sent_ref, put, vec_ref[...])
-
-
-def split_row_kernel(heads, hidden, spread, *refs):
+    for row in range(2):
+        for at in range(4):
+            start = at * WIDE + row * 2 * BLK
+            keep_ref[put : put + BLK] = grads[rows_at(start + core * BLK)]
+            sent_ref[put : put + BLK] = grads[rows_at(start + (1 - core) * BLK)]
+            put += BLK
+
+
+def split_row_kernel(heads, spread, *refs):
     had_ref, came_ref = refs[:2]
     keep_ref, sent_ref = refs[2 + spread : 4 + spread]
     _, row, _ = my_place()
@@ -287,46 +292,48 @@
         at = rows_at(start, WIDE)
         return full(had_ref[at]) + full(came_ref[at])
 
-    put, base = 0, 0
     if heads:
-        keep_ref[:WIDE] = total(row * WIDE)
+        keep_ref[...] = total(row * WIDE)
         sent_ref[:WIDE] = half(total((1 - row) * WIDE))
-        put, base = WIDE, 2 * WIDE
-    if hidden:
-        for _ in range(2):
-            keep_ref[put : put + WIDE] = total(base)
-            sent_ref[put : put + WIDE] = half(total(base + WIDE))
-            put, base = put + WIDE, base + 2 * WIDE
+    else:
+        for member in range(2):
+            rows = slice(member * WIDE, (member + 1) * WIDE)
+            keep_ref[rows] = total(2 * member * WIDE)
+            sent_ref[rows] = half(total((2 * member + 1) * WIDE))
     if spread:
-        value = refs[2][...] + get_vec(came_ref, base)
+        value = refs[2][...] + get_vec(came_ref, 2 * WIDE)
         refs[-1][...] = value
-        put_vec(sent_ref, put, value)
+        put_vec(sent_ref, WIDE, value)
 
 
 def split_x_kernel(heads, hidden, spread, *refs):
-    had_ref, came_ref = refs[:2]
-    keep_ref, *sent_refs = refs[2 + spread : 6 + spread]
-    hold = refs[-1]
+    pairs = 2 * (heads + hidden)
+    sources = refs[:pairs]
+    keep_ref, *sent_refs = refs[pairs + spread : pairs + spread + 4]
     x, _, _ = my_place()
-    count = had_ref.shape[0]
-    hold[...] = had_ref[...] + full(came_ref[:count])
-    for hops, target in enumerate([keep_ref] + sent_refs):
-        kind = target.dtype
-        put, base = 0, 0
-        if heads:
+    put = 0
+    if heads:
+        hold = refs[-1]
+        hold[...] = sources[0][...] + full(sources[1][:WIDE])
+        for hops, target in enumerate([keep_ref] + sent_refs):
+            kind = target.dtype
             at = (x + hops) & 3
             piece = hold[rows_at(at * BLK)]
             target[:BLK] = jnp.where(at == 3, 0.0, piece).astype(kind)
             target[BLK : 2 * BLK] = hold[3 * BLK : 4 * BLK].astype(kind)
-            put, base = 2 * BLK, WIDE
-        if hidden:
-            for _ in range(2):
-                start = base + hops * BLK
-                target[put : put + BLK] = hold[start : start + BLK].astype(kind)
-                put, base = put + BLK, base + WIDE
-        if spread and hops:
-            value = refs[2][...] + get_vec(came_ref, base)
-            refs[-2][...] = value
+        put = 2 * BLK
+    if hidden:
+        had_ref, came_ref = sources[-2:]
+        for member in range(2):
+            for hops, target in enumerate([keep_ref] + sent_refs):
+                rows = slice(member * WIDE + hops * BLK, member * WIDE + (hops + 1) * BLK)
+                value = had_ref[rows] + full(came_ref[rows])
+                target[put : put + BLK] = value.astype(target.dtype)
+            put += BLK
+    if spread:
+        value = refs[pairs][...] + get_vec(sources[1], WIDE)
+        refs[-2][...] = value
+        for target in sent_refs:
             put_vec(target, put, value)
 
 
@@ -341,21 +348,10 @@
         out_ref[BLK : 2 * BLK] = jnp.where(x == 0, total[BLK : 2 * BLK], 0.0)
 
 
-def scatter_core(grads, heads, hidden, spread, name):
-    rows = 8 * BLK * heads + 16 * BLK * hidden
+def scatter_row(keep, came, heads, spread, name, vec_sum=None):
+    rows = 4 * BLK if heads else 8 * BLK
     return small_call(
-        lambda *refs: split_core_kernel(heads, hidden, spread, *refs),
-        [(VPAD, jnp.float32)] * spread
-        + [(rows, jnp.bfloat16), (rows + 2 * VPAD * spread, jnp.bfloat16)],
-        grads,
-        name=name + "_split_core",
-    )
-
-
-def scatter_row(keep, came, heads, hidden, spread, name, vec_sum=None):
-    rows = 4 * BLK * heads + 8 * BLK * hidden
-    return small_call(
-        lambda *refs: split_row_kernel(heads, hidden, spread, *refs),
+        lambda *refs: split_row_kernel(heads, spread, *refs),
         [(rows, jnp.float32), (rows + 2 * VPAD * spread, jnp.bfloat16)]
         + [(VPAD, jnp.float32)] * spread,
         [keep, came] + [vec_sum] * spread,
@@ -363,15 +359,15 @@
     )
 
 
-def scatter_x(keep, came, heads, hidden, spread, name, vec_sum=None):
+def scatter_x(sources, heads, hidden, spread, name, vec_sum=None):
     rows = 2 * BLK * heads + 2 * BLK * hidden
     return small_call(
         lambda *refs: split_x_kernel(heads, hidden, spread, *refs),
         [(rows, jnp.float32)]
         + [(rows + 2 * VPAD * spread, jnp.bfloat16)] * 3
         + [(VPAD, jnp.float32)] * spread,
-        [keep, came] + [vec_sum] * spread,
-        scratch=[pltpu.VMEM(keep.shape, jnp.float32)],
+        list(sources) + [vec_sum] * spread,
+        scratch=[pltpu.VMEM((WIDE, WIDE), jnp.float32)],
         name=name + "_split_x",
     )
 
@@ -495,7 +491,7 @@
     return vec_ref[at : at + 1]
 
 
-def attend_kernel(layer_at, in_ref, qkv_w, out_w, vec_ref, mid_ref, qkv_ref, attn_ref, prob_ref):
+def attend_kernel(layer_at, need, flush, in_ref, qkv_w, out_w, vec_ref, mid_ref, qkv_ref, attn_ref, prob_ref):
     normed, _ = normalize(in_ref[...])
     normed_low = half(normed * row_of(vec_ref, layer_at, 0) + row_of(vec_ref, layer_at, 1))
     for third in range(3):
@@ -504,8 +500,11 @@
         if third != 1:
             value = value + row_of(vec_ref, layer_at, 2 if third == 0 else 3)
         qkv_ref[:, rows] = half(value)
+    flush(1)
     for at in range(HEADS // 2):
         attend_pair(at, qkv_ref, attn_ref, prob_ref)
+        flush(3, at)
+    flush(2)
     mid_ref[...] = in_ref[...] + (
         col_contract(attn_ref[...], out_w[...]) + row_of(vec_ref, layer_at, 4)
     )
@@ -528,12 +527,17 @@
     attn_ref[:, column(at)] = half(jnp.where(row < 64, sums[0], sums[1]).T)
 
 
-def attend_back_kernel(layer_at, up_ref, in_ref, qkv_ref, attn_ref, prob_ref, qkv_w, out_w, vec_ref, grad_ref, gqkv_ref, gout_ref, sum_ref, upstream_ref, back_ref):
+def attend_back_kernel(layer_at, need, flush, up_ref, in_ref, qkv_ref, attn_ref, prob_ref, qkv_w, out_w, vec_ref, *refs):
+    spread = len(refs) > 8
+    others = refs[:5] if spread else ()
+    grad_ref, keep_ref, sent_ref, total_ref, upstream_ref, back_ref, grads_ref, sum_ref = refs[-8:]
+    sum_ref[...] = jnp.zeros_like(sum_ref)
     out_low = half(up_ref[...])
-    gout_ref[...] = half(row_contract(out_low, attn_ref[...]))
+    grads_ref[3 * WIDE :] = half(row_contract(out_low, attn_ref[...]))
     upstream_ref[...] = half(product(out_low, out_w[...]))
     sum_ref[4:5] = jnp.sum(full(out_low), 0, keepdims=True)
     for at in range(HEADS // 2):
+        need(at)
         attend_back_pair(at, qkv_ref, upstream_ref, prob_ref, back_ref)
     normed, inv_std = normalize(in_ref[...])
     gain = row_of(vec_ref, layer_at, 0)
@@ -542,7 +546,7 @@
     for third in range(3):
         rows = slice(third * WIDE, (third + 1) * WIDE)
         piece = back_ref[:, rows]
-        gqkv_ref[rows] = half(row_contract(piece, normed_low))
+        grads_ref[rows] = half(row_contract(piece, normed_low))
         back_normed = back_normed + product(piece, qkv_w[rows])
         if third != 1:
             put = 2 if third == 0 else 3
@@ -550,6 +554,20 @@
     sum_ref[0:1] = jnp.sum(back_normed * normed, 0, keepdims=True)
     sum_ref[1:2] = jnp.sum(back_normed, 0, keepdims=True)
     grad_ref[...] = up_ref[...] + norm_back(back_normed, normed, inv_std, gain)
+    flush(0)
+    split_heads(grads_ref, keep_ref, sent_ref)
+    if not spread:
+        total_ref[...] = sum_ref[...]
+        return
+    total_ref[VROWS:] = jnp.zeros((VPAD - VROWS, WIDE), jnp.float32)
+    pieces = (sum_ref, *others)
+    for layer in range(LAYERS):
+        base = layer * (VROWS // LAYERS)
+        one, two, three = pieces[3 * layer : 3 * layer + 3]
+        total_ref[base : base + 5] = one[:5]
+        total_ref[base + 5 : base + 8] = two[:3]
+        total_ref[base + 8 : base + 12] = three[:4]
+    put_vec(sent_ref, 2 * WIDE, total_ref[...])
 
 
 def attend_back_pair(at, qkv_ref, upstream_ref, prob_ref, back_ref):
@@ -574,11 +592,12 @@
     back_ref[:, column(6 + at)] = half(jnp.where(lane < 64, got[0][2], got[1][2]))
 
 
-def hidden_kernel(layer_at, mid_ref, up_w, down_w, vec_ref, bias_ref, out_ref, act_ref, slope_ref):
+def hidden_kernel(layer_at, need, flush, mid_ref, up_w, down_w, vec_ref, bias_ref, out_ref, act_ref, slope_ref):
     normed, _ = normalize(mid_ref[...])
     hidden_low = half(normed * row_of(vec_ref, layer_at, 5) + row_of(vec_ref, layer_at, 6))
     total = mid_ref[...] + row_of(vec_ref, layer_at, 7)
     for chunk in range(4):
+        need(chunk)
         rows = slice(chunk * WIDE, (chunk + 1) * WIDE)
         hidden = col_contract(hidden_low, up_w[rows]) + bias_ref[chunk : chunk + 1]
         share = 0.5 * (1.0 + lax.erf(hidden * half_root))
@@ -586,20 +605,30 @@
         act_ref[:, rows] = active_low
         slope_ref[:, rows] = share + hidden * jnp.exp(-0.5 * hidden * hidden) * density
         total = total + product(active_low, down_w[rows])
+        flush(1, chunk)
+        flush(2, chunk)
     out_ref[...] = total
 
 
-def hidden_back_kernel(layer_at, up_ref, mid_ref, act_ref, slope_ref, up_w, down_w, vec_ref, grad_ref, gup_ref, gdown_ref, sum_ref, bias_ref):
+def hidden_back_kernel(layer_at, need, flush, up_ref, mid_ref, act_ref, slope_ref, up_w, down_w, vec_ref, grad_ref, keep_ref, sent_ref, sum_ref, bias_ref):
     down_low = half(up_ref[...])
     normed, inv_std = normalize(mid_ref[...])
     gain = row_of(vec_ref, layer_at, 5)
     hidden_low = half(normed * gain + row_of(vec_ref, layer_at, 6))
     back_hidden = jnp.zeros(normed.shape, jnp.float32)
+    sum_ref[...] = jnp.zeros_like(sum_ref)
+    bias_ref[...] = jnp.zeros_like(bias_ref)
     for chunk in range(4):
+        need(chunk)
         rows = slice(chunk * WIDE, (chunk + 1) * WIDE)
         up_low = half(col_contract(down_low, down_w[rows]) * slope_ref[:, rows])
-        gdown_ref[rows] = half(row_contract(act_ref[:, rows], down_low))
-        gup_ref[rows] = half(row_contract(up_low, hidden_low))
+        target, turn_at = (keep_ref, sent_ref)[chunk // 2], chunk % 2
+        for member, value in enumerate(
+            (row_contract(up_low, hidden_low), row_contract(act_ref[:, rows], down_low))
+        ):
+            put = (2 * member + turn_at) * WIDE
+            target[put : put + WIDE] = half(value)
+            flush(1 + chunk // 2, 2 * member + turn_at)
         bias_ref[chunk : chunk + 1] = jnp.sum(full(up_low), 0, keepdims=True)
         back_hidden = back_hidden + product(up_low, up_w[rows])
     sum_ref[0:1] = jnp.sum(back_hidden * normed, 0, keepdims=True)
@@ -608,17 +637,74 @@
     grad_ref[...] = up_ref[...] + norm_back(back_hidden, normed, inv_std, gain)
 
 
-def layer_call(kernel, layer_at, ins, outs, scratch=(), name=None, vmem=24):
+def cut_piece(ref, how, at):
+    if how is None:
+        return ref
+    dimension, pieces = how
+    size = ref.shape[dimension] // pieces
+    return ref.at[(slice(None),) * dimension + (pl.ds(at * size, size),)]
+
+
+def layer_call(kernel, layer_at, ins, outs, in_cut, out_cut, scratch=(), name=None):
+    count, total = len(ins), len(outs)
+    pieces = max([how[1] for how in in_cut.values()] + [1])
+    in_plan = [(at, None, 0) for at in range(count) if at not in in_cut]
+    in_plan += [(at, in_cut[at], piece) for piece in range(pieces) for at in sorted(in_cut)]
+    out_plan = []
+    for at in range(total):
+        how = out_cut.get(at)
+        out_plan += [(at, how, piece) for piece in range(how[1] if how else 1)]
+
     def body(*refs):
-        kernel(layer_at, *refs)
+        far, near = refs[: count + total], refs[count + total : 2 * (count + total)]
+        come_sems, leave_sems = refs[2 * (count + total) : 2 * (count + total) + 2]
+        rest = refs[2 * (count + total) + 2 :]
+        come = [
+            pltpu.make_async_copy(
+                cut_piece(far[at], how, piece), cut_piece(near[at], how, piece), come_sems.at[index]
+            )
+            for index, (at, how, piece) in enumerate(in_plan)
+        ]
+        leave = [
+            pltpu.make_async_copy(
+                cut_piece(near[count + at], how, piece),
+                cut_piece(far[count + at], how, piece),
+                leave_sems.at[index],
+            )
+            for index, (at, how, piece) in enumerate(out_plan)
+        ]
+        started = []
+
+        def need(wanted):
+            for (_, how, piece), copy in zip(in_plan, come):
+                if (how is None and wanted is None) or (how is not None and piece == wanted):
+                    copy.wait()
+
+        def flush(out_at, wanted=0):
+            index = [(at, piece) for at, _, piece in out_plan].index((out_at, wanted))
+            leave[index].start()
+            started.append(index)
+
+        for copy in come:
+            copy.start()
+        need(None)
+        kernel(layer_at, need, flush, *near, *rest)
+        for index, copy in enumerate(leave):
+            if index not in started:
+                copy.start()
+        for copy in leave:
+            copy.wait()
 
     return pl.pallas_call(
         body,
         out_shape=[jax.ShapeDtypeStruct(shape, kind) for shape, kind in outs],
-        in_specs=[pl.BlockSpec(memory_space=pltpu.VMEM)] * len(ins),
-        out_specs=[pl.BlockSpec(memory_space=pltpu.VMEM)] * len(outs),
-        scratch_shapes=list(scratch),
-        compiler_params=pltpu.CompilerParams(vmem_limit_bytes=vmem << 20),
+        in_specs=[far_spec()] * count,
+        out_specs=[far_spec()] * total,
+        scratch_shapes=[pltpu.VMEM(part.shape, part.dtype) for part in ins]
+        + [pltpu.VMEM(shape, kind) for shape, kind in outs]
+        + [pltpu.SemaphoreType.DMA((len(in_plan),)), pltpu.SemaphoreType.DMA((len(out_plan),))]
+        + list(scratch),
+        compiler_params=pltpu.CompilerParams(vmem_limit_bytes=64 << 20),
         cost_estimate=pl.CostEstimate(flops=1 << 20, bytes_accessed=1 << 16, transcendentals=0),
         name=name,
     )(*ins)
@@ -636,25 +722,32 @@
             (inputs.shape, jnp.bfloat16),
             ((HEADS, length, length), jnp.bfloat16),
         ],
+        {},
+        {3: (0, HEADS // 2)},
         name="attend",
     )
 
 
-def attention_backward(layer_at, upstream, inputs, stored, w_qkv, w_out, vec_full):
+def attention_backward(layer_at, upstream, inputs, stored, w_qkv, w_out, vec_full, others=()):
     qkv_low, attn_low, probs = stored
+    spread = len(others) > 0
     return layer_call(
         attend_back_kernel,
         layer_at,
-        [upstream, inputs, qkv_low, attn_low, probs, w_qkv, w_out, vec_full],
+        [upstream, inputs, qkv_low, attn_low, probs, w_qkv, w_out, vec_full, *others],
         [
             (inputs.shape, jnp.float32),
-            (w_qkv.shape, jnp.bfloat16),
-            (w_out.shape, jnp.bfloat16),
-            ((8, WIDE), jnp.float32),
+            ((2 * WIDE, WIDE), jnp.bfloat16),
+            ((2 * WIDE + 2 * VPAD * spread, WIDE), jnp.bfloat16),
+            ((VPAD if spread else 8, WIDE), jnp.float32),
         ],
+        {4: (0, HEADS // 2)},
+        {},
         scratch=[
             pltpu.VMEM(attn_low.shape, jnp.bfloat16),
             pltpu.VMEM(qkv_low.shape, jnp.bfloat16),
+            pltpu.VMEM((4 * WIDE, WIDE), jnp.bfloat16),
+            pltpu.VMEM((8, WIDE), jnp.float32),
         ],
         name="attend_back",
     )
@@ -667,6 +760,8 @@
         layer_at,
         [middle, w_up, w_down, vec_full, bias_up],
         [(middle.shape, jnp.float32), (wide, jnp.bfloat16), (wide, jnp.float32)],
+        {1: (0, 4), 2: (0, 4)},
+        {1: (1, 4), 2: (1, 4)},
         name="hidden",
     )
 
@@ -681,8 +776,10 @@
             (w_up.shape, jnp.bfloat16),
             (w_up.shape, jnp.bfloat16),
             ((8, WIDE), jnp.float32),
-            ((4, WIDE), jnp.float32),
+            ((8, WIDE), jnp.float32),
         ],
+        {2: (1, 4), 3: (1, 4), 4: (0, 4), 5: (0, 4)},
+        {1: (0, 4), 2: (0, 4)},
         name="hidden_back",
     )
 
@@ -701,13 +798,13 @@
 def to_own_order(row, place):
     cube = row.reshape(RINGX, 2, 2, BLK)
     cube = turn(swap(swap(cube, place[2], 2), place[1], 1), place[0])
-    return cube.transpose(2, 1, 0, 3).reshape(4, WIDE)
+    return jnp.pad(cube.transpose(2, 1, 0, 3).reshape(4, WIDE), ((0, 4), (0, 0)))
 
 
 def from_own_order(row, place):
-    cube = row.reshape(2, 2, RINGX, BLK).transpose(2, 1, 0, 3)
+    cube = row[:4].reshape(2, 2, RINGX, BLK).transpose(2, 1, 0, 3)
     cube = swap(swap(turn(cube, (4 - place[0]) & 3), place[2], 2), place[1], 1)
-    return cube.reshape(4, WIDE)
+    return jnp.pad(cube.reshape(4, WIDE), ((0, 4), (0, 0)))
 
 
 def on_device(tokens, cotangent, live, slot_of, weights, momentum, vec, vec_first, vec_second):
@@ -741,10 +838,11 @@
         name="first_merge_x",
     )
     second_x, third, first_x = tie((second_x, third, first_x))
-    first_parts = all_four(first_x)
+    beside_first, core_first = other_row(first_x), other_core(first_x)
     beside_second, core_second = other_row(second_x), other_core(second_x)
     third_parts = from_x(third)
-    first_parts, third_parts = tie((first_parts, third_parts))
+    beside_first, third_parts = tie((beside_first, third_parts))
+    first_parts = [first_x, beside_first, core_first, other_core(beside_first)]
     w_qkv0, w_out0, vec_full = whole(first_parts, True, False, True, "first")
     (third_x,) = small_call(
         merge_third_kernel,
@@ -771,47 +869,48 @@
     stream, *mlp1 = hidden_forward(1, middle1, w_up1, w_down1, vec_full, bias1)
 
     upstream = cotangent[0] * full(live)[0]
-    mid_grad, grad_up, grad_down, sums_two1, sums_up1 = hidden_backward(
+    mid_grad, keep_f1, sent, sums_two1, sums_up1 = hidden_backward(
         1, upstream, middle1, mlp1, w_up1, w_down1, vec_full
     )
-    upstream, grad_qkv, grad_out, sums_one1 = attention_backward(
+    came_f1 = other_core(sent)
+    upstream, keep_h1, sent, sums_one1 = attention_backward(
         1, mid_grad, inputs1, attn1, w_qkv1, w_out1, vec_full
     )
-    keep, sent = scatter_core([grad_qkv, grad_out, grad_up, grad_down], True, True, False, "third")
+    came_h1 = other_core(sent)
+    upstream, came_f1 = tie((upstream, came_f1))
+    keep_f1, sent = scatter_row(keep_f1, came_f1, False, False, "third")
     upstream, sent = tie((upstream, sent))
-    came = other_core(sent)
-    mid_grad, grad_up, grad_down, sums_two0, sums_up0 = hidden_backward(
+    came_f1 = other_row(sent)
+    mid_grad, keep_f, sent, sums_two0, sums_up0 = hidden_backward(
         0, upstream, middle0, mlp0, w_up0, w_down0, vec_full
     )
-    keep_f, sent_f = scatter_core([grad_up, grad_down], False, True, False, "second")
-    mid_grad, sent_f, came = tie((mid_grad, sent_f, came))
-    came_f = other_core(sent_f)
-    keep, sent = scatter_row(keep, came, True, True, False, "third")
+    came_f = other_core(sent)
+    mid_grad, came_h1 = tie((mid_grad, came_h1))
+    keep_h1, sent = scatter_row(keep_h1, came_h1, True, False, "fourth")
     mid_grad, sent = tie((mid_grad, sent))
-    came = other_row(sent)
-    token_grad, grad_qkv, grad_out, sums_one0 = attention_backward(
-        0, mid_grad, inputs0, attn0, w_qkv0, w_out0, vec_full
-    )
-    grad_qkv, came_f = tie((grad_qkv, came_f))
-    keep_f, sent_f = scatter_row(keep_f, came_f, False, True, False, "second")
-    grad_qkv, sent_f, came = tie((grad_qkv, sent_f, came))
+    came_h1 = other_row(sent)
+    bias_sum0, bias_sum1 = (from_own_order(part, place) for part in (sums_up0, sums_up1))
+    token_grad, keep_h, sent_h, vec_sum = attention_backward(
+        0,
+        mid_grad,
+        inputs0,
+        attn0,
+        w_qkv0,
+        w_out0,
+        vec_full,
+        (sums_two0, bias_sum0, sums_one1, sums_two1, bias_sum1),
+    )
+    sent_h, came_f = tie((sent_h, came_f))
+    keep_f, sent_f = scatter_row(keep_f, came_f, False, False, "second")
+    sent_h, sent_f, came_f1, came_h1 = tie((sent_h, sent_f, came_f1, came_h1))
     came_f = other_row(sent_f)
-    bias_sum0, bias_sum1 = (from_own_order(part, place) for part in (sums_up0, sums_up1))
-    vec_sum, keep_h, sent_h = scatter_core(
-        [grad_qkv, grad_out, sums_one0, sums_two0, bias_sum0, sums_one1, sums_two1, bias_sum1],
-        True,
-        False,
-        True,
-        "first",
-    )
     came_h = other_core(sent_h)
-    came_h, came = tie((came_h, came))
-    keep, *sent_x = scatter_x(keep, came, True, True, False, "third")
+    keep, *sent_x = scatter_x([keep_h1, came_h1, keep_f1, came_f1], True, True, False, "third")
     came_x = spread_x(sent_x)
     came_f, came_x = tie((came_f, came_x))
-    keep_h, sent_h, vec_sum = scatter_row(keep_h, came_h, True, False, True, "first", vec_sum)
+    keep_h, sent_h, vec_sum = scatter_row(keep_h, came_h, True, True, "first", vec_sum)
     came_h = other_row(sent_h)
-    keep_f, *sent_f = scatter_x(keep_f, came_f, False, True, False, "second")
+    keep_f, *sent_f = scatter_x([keep_f, came_f], False, True, False, "second")
     (third_sum,) = small_call(
         lambda *refs: sum_x_kernel(True, *refs),
         [(4 * BLK, jnp.float32)],
@@ -825,7 +924,7 @@
         [keep_f] + came_f,
         name="second_sum_x",
     )
-    keep_h, *sent_h, vec_sum = scatter_x(keep_h, came_h, True, False, True, "first", vec_sum)
+    keep_h, *sent_h, vec_sum = scatter_x([keep_h, came_h], True, False, True, "first", vec_sum)
     came_h = spread_x(sent_h)
     own, *sent_g, vec_sum = small_call(
         split_group_kernel,

time: 297 us -> 321 us (1.081)
  Pallas kernels: 81.5 us -> 137 us
  local copies, waits for them, and re-layouts: 45.7 us -> 23.9 us
  waiting for transfers between devices: 90.8 us -> 80 us
  other arithmetic: 4.62 us -> 9.13 us
  starting transfers between devices: 67.2 us -> 62.7 us
    unnamed x114 -> x38, local copies, waits for them, and re-layouts: 44.3 us -> 11.9 us
    pallas_call x8, Pallas kernels: 51.1 us -> 79.2 us  [layer_call(): pl.pallas_call(body, out_shape=[jax.ShapeDtypeStruct(shape, kind) for sha...]
    pallas_call x20 -> x18, Pallas kernels: 30.4 us -> 58.1 us  [small_call(): pl.pallas_call(body, out_shape=[jax.ShapeDtypeStruct((rows, WIDE), kind)...]
    ppermute x36 -> x38, waiting for transfers between devices: 71.4 us -> 61.7 us  [near(): return lax.ppermute(part, 'dp', [(at, change(at)) for at in range(16)])]
    ppermute x36 -> x38, starting transfers between devices: 46.9 us -> 42.7 us  [near(): return lax.ppermute(part, 'dp', [(at, change(at)) for at in range(16)])]
    slice x12, local copies, waits for them, and re-layouts: 0.03 us -> 4.15 us  [turn(): turned_parts = [jnp.roll(parts, -by, 0) for by in range(RINGX)]]
  transfers between devices with their start and end apart: 47 -> 49, of which waited for: 27 -> 23; matrix products, arithmetic and copies ran while one was open for 3% -> 9% of each run, Pallas kernels for 13% -> 27%
where the time goes in v1:
time: 321 us; the launch traced here: 315 us
  Pallas kernels  137 us (43%)
  waiting for transfers between devices  80 us (25%)
  starting transfers between devices  62.7 us (20%)
  local copies, waits for them, and re-layouts  23.9 us (7%)
  other arithmetic  9.13 us (3%)
    pallas_call x8, Pallas kernels, layer_call(): pl.pallas_call(body, out_shape=[jax.ShapeDtypeStruct(shape, kind) for sha...  79.2 us
    ppermute x38, waiting for transfers between devices, near(): return lax.ppermute(part, 'dp', [(at, change(at)) for at in range(16)])  61.7 us
    pallas_call x18, Pallas kernels, small_call(): pl.pallas_call(body, out_shape=[jax.ShapeDtypeStruct((rows, WIDE), kind)...  58.1 us
    ppermute x38, starting transfers between devices, near(): return lax.ppermute(part, 'dp', [(at, change(at)) for at in range(16)])  42.7 us
    ppermute x11, starting transfers between devices, along_group(): return lax.ppermute(part, 'group', pairs)  20 us
    ppermute x11, waiting for transfers between devices, along_group(): return lax.ppermute(part, 'group', pairs)  18.3 us
    unnamed x38, local copies, waits for them, and re-layouts  11.9 us
  transfers between devices with their start and end apart: 49, of which 23 were waited for; matrix products, arithmetic and copies ran while one was open for 9% of the time, Pallas kernels for 27%

profile of v1, /device:TPU:1, one launch (start us, length us, event | category | flops | bytes accessed | tf_op | source)
XLA Modules:
  0.0 315.0 jit_solution(13546758471861044766)
XLA Ops:
  2.8 3.8 %collective-permute-start = (bf16[128,384]{1,0:T(8,128)(2,1)S(1)}, bf16[128,384]{1,0:T(8,128)(2,1)S(1)}, u32[]{:S(2)}, u32[]{:S(2)}) collective-permute-start(bf16[128,384]{1,0:T(8,128)(2,1)S(1)} %pad_maximum_fusion.1), channel_id=1, source_target_pairs={{0,64},{16,80},{32,96},{48,112},{64,0},{80,16},{96,32},{112,48},{1... | collective-permute-start | bytes 294920 | tf_op jit(solution)/shard_map/ppermute | solution.py:102
  9.1 3.8 %collective-permute-start.1 = (bf16[256,384]{1,0:T(8,128)(2,1)S(1)}, bf16[256,384]{1,0:T(8,128)(2,1)S(1)}, u32[]{:S(2)}, u32[]{:S(2)}) collective-permute-start(bf16[256,384]{1,0:T(8,128)(2,1)S(1)} %pad_maximum_fusion.refs_1_), channel_id=1, source_target_pairs={{0,48},{16,0},{32,16},{48,32},{64,112},{80,64},{96,80},{112,96},{1... | collective-permute-start | bytes 589832 | tf_op jit(solution)/shard_map/ppermute | solution.py:102
  13.7 6.9 %collective-permute-done.1.refs_2_ = bf16[256,384]{1,0:T(8,128)(2,1)S(1)} collective-permute-done((bf16[256,384]{1,0:T(8,128)(2,1)S(1)}, bf16[256,384]{1,0:T(8,128)(2,1)S(1)}, u32[]{:S(2)}, u32[]{:S(2)}) %collective-permute-start.1) | collective-permute-done | bytes 196640 | tf_op jit(solution)/shard_map/ppermute | solution.py:102
  21.9 3.0 collective-permute-done.3.refs_4_
  31.0 5.4 %collective-permute-done.4.refs_1_ = bf16[416,384]{1,0:T(8,128)(2,1)} collective-permute-done((bf16[416,384]{1,0:T(8,128)(2,1)}, bf16[416,384]{1,0:T(8,128)(2,1)}, u32[]{:S(2)}, u32[]{:S(2)}) %collective-permute-start.4) | collective-permute-done | bytes 319520 | tf_op jit(solution)/shard_map/ppermute | solution.py:85
  36.4 3.1 collective-permute-done.5.refs_2_
  39.5 8.4 %collective-permute-done.6.refs_3_ = bf16[416,384]{1,0:T(8,128)(2,1)} collective-permute-done((bf16[416,384]{1,0:T(8,128)(2,1)}, bf16[416,384]{1,0:T(8,128)(2,1)}, u32[]{:S(2)}, u32[]{:S(2)}) %collective-permute-start.6) | collective-permute-done | bytes 319520 | tf_op jit(solution)/shard_map/ppermute | solution.py:85
  54.8 5.0 %collective-permute-done.8.refs_1_ = bf16[384,384]{1,0:T(8,128)(2,1)} collective-permute-done((bf16[384,384]{1,0:T(8,128)(2,1)}, bf16[384,384]{1,0:T(8,128)(2,1)}, u32[]{:S(2)}, u32[]{:S(2)}) %collective-permute-start.8) | collective-permute-done | bytes 294944 | tf_op jit(solution)/shard_map/ppermute | solution.py:85
  60.7 8.1 %collective-permute-done.10.refs_3_ = bf16[384,384]{1,0:T(8,128)(2,1)} collective-permute-done((bf16[384,384]{1,0:T(8,128)(2,1)}, bf16[384,384]{1,0:T(8,128)(2,1)}, u32[]{:S(2)}, u32[]{:S(2)}) %collective-permute-start.10) | collective-permute-done | bytes 294944 | tf_op jit(solution)/shard_map/ppermute | solution.py:85
  80.6 9.2 %attend.2 = (f32[577,384]{1,0:T(8,128)}, bf16[577,1152]{1,0:T(8,128)(2,1)}, bf16[577,384]{1,0:T(8,128)(2,1)}, bf16[6,577,577]{2,1,0:T(8,128)(2,1)}) custom-call(f32[577,384]{1,0:T(8,128)} %bitcast.38, bf16[1152,384]{1,0:T(8,128)(2,1)} %get-tuple-element.131.refs_1_.refs_5_, bf16[384,384]{1,0:T(8,128)(2,1)} %get-tuple-element.132.refs_2_.refs_6_, ...), custom_call_target="tpu_custom_call" | custom-call | flops 1048576 | bytes 65536 | tf_op jit(solution)/shard_map/attend/pallas_call | solution.py:698
  96.0 3.2 %second_whole.1 = (bf16[1536,384]{1,0:T(8,128)(2,1)}, bf16[1536,384]{1,0:T(8,128)(2,1)}) custom-call(bf16[768,384]{1,0:T(8,128)(2,1)} %get-tuple-element.129.refs_0_, bf16[768,384]{1,0:T(8,128)(2,1)} %collective-permute-done.11.refs_1_, bf16[768,384]{1,0:T(8,128)(2,1)} %collective-permute-done.15.refs_2_, bf16[768,384]{1,0:T(8,128)(2,1)} %collective-permute-done.16.refs_3_), custom_call_target="tpu_custom_call" | custom-call | flops 1048576 | bytes 65536 | tf_op jit(solution)/shard_map/second_whole/pallas_call | solution.py:146
  99.2 6.9 %hidden.2 = (f32[577,384]{1,0:T(8,128)}, bf16[577,1536]{1,0:T(8,128)(2,1)}, f32[577,1536]{1,0:T(8,128)}) custom-call(f32[577,384]{1,0:T(8,128)} %get-tuple-element.136.refs_0_.refs_1_, bf16[1536,384]{1,0:T(8,128)(2,1)} %get-tuple-element.138.refs_1_.refs_4_, bf16[1536,384]{1,0:T(8,128)(2,1)} %get-tuple-element.139.refs_2_.refs_5_, ...), custom_call_target="tpu_custom_call" | custom-call | flops 1048576 | bytes 65536 | tf_op jit(solution)/shard_map/hidden/pallas_call | solution.py:698
  106.1 5.9 %collective-permute-done.14.refs_1_ = bf16[1152,384]{1,0:T(8,128)(2,1)} collective-permute-done((bf16[1152,384]{1,0:T(8,128)(2,1)}, bf16[1152,384]{1,0:T(8,128)(2,1)}, u32[]{:S(2)}, u32[]{:S(2)}) %collective-permute-start.14) | collective-permute-done | bytes 884768 | tf_op jit(solution)/shard_map/ppermute | solution.py:85
  117.1 4.0 %third_whole.1 = (bf16[1152,384]{1,0:T(8,128)(2,1)}, bf16[384,384]{1,0:T(8,128)(2,1)}, bf16[1536,384]{1,0:T(8,128)(2,1)}, bf16[1536,384]{1,0:T(8,128)(2,1)}) custom-call(bf16[1152,384]{1,0:T(8,128)(2,1)} %third_merge_x.1.refs_0_, bf16[1152,384]{1,0:T(8,128)(2,1)} %collective-permute-done.14.refs_1_, bf16[1152,384]{1,0:T(8,128)(2,1)} %collective-permute-done.17.refs_2_, ...), custom_call_target="tpu_custom_call" | custom-call | flops 1048576 | bytes 65536 | tf_op jit(solution)/shard_map/third_whole/pallas_call | solution.py:146
  121.1 9.1 %attend.3 = (f32[577,384]{1,0:T(8,128)}, bf16[577,1152]{1,0:T(8,128)(2,1)}, bf16[577,384]{1,0:T(8,128)(2,1)}, bf16[6,577,577]{2,1,0:T(8,128)(2,1)}) custom-call(f32[577,384]{1,0:T(8,128)} %get-tuple-element.141.refs_0_.refs_1_, bf16[1152,384]{1,0:T(8,128)(2,1)} %get-tuple-element.143.refs_1_.refs_5_, bf16[384,384]{1,0:T(8,128)(2,1)} %get-tuple-element.144.refs_2_.refs_6_, ...), custom_call_target="tpu_custom_call" | custom-call | flops 1048576 | bytes 65536 | tf_op jit(solution)/shard_map/attend/pallas_call | solution.py:698
  130.2 7.0 %hidden.3 = (f32[577,384]{1,0:T(8,128)}, bf16[577,1536]{1,0:T(8,128)(2,1)}, f32[577,1536]{1,0:T(8,128)}) custom-call(f32[577,384]{1,0:T(8,128)} %get-tuple-element.145.refs_0_.refs_1_, bf16[1536,384]{1,0:T(8,128)(2,1)} %get-tuple-element.146.refs_1_.refs_4_, bf16[1536,384]{1,0:T(8,128)(2,1)} %get-tuple-element.147.refs_2_.refs_5_, ...), custom_call_target="tpu_custom_call" | custom-call | flops 1048576 | bytes 65536 | tf_op jit(solution)/shard_map/hidden/pallas_call | solution.py:698
  137.1 9.6 %hidden_back.2 = (f32[577,384]{1,0:T(8,128)}, bf16[1536,384]{1,0:T(8,128)(2,1)}, bf16[1536,384]{1,0:T(8,128)(2,1)}, f32[8,384]{1,0:T(8,128)}, f32[8,384]{1,0:T(8,128)}) custom-call(f32[577,384]{1,0:T(8,128)} %fusion.refs_0_, f32[577,384]{1,0:T(8,128)} %get-tuple-element.145.refs_0_.refs_1_, bf16[577,1536]{1,0:T(8,128)(2,1)} %get-tuple-element.149.refs_2_, ...), custom_call_target="tpu_custom_call" | custom-call | flops 1048576 | bytes 65536 | tf_op jit(solution)/shard_map/hidden_back/pallas_call | solution.py:698
  146.8 14.0 %attend_back.2 = (f32[577,384]{1,0:T(8,128)}, bf16[768,384]{1,0:T(8,128)(2,1)}, bf16[768,384]{1,0:T(8,128)(2,1)}, f32[8,384]{1,0:T(8,128)}) custom-call(f32[577,384]{1,0:T(8,128)} %get-tuple-element.151.refs_0_, f32[577,384]{1,0:T(8,128)} %get-tuple-element.141.refs_0_.refs_1_, bf16[577,1152]{1,0:T(8,128)(2,1)} %get-tuple-element.152.refs_2_, ...), custom_call_target="tpu_custom_call" | custom-call | flops 1048576 | bytes 65536 | tf_op jit(solution)/shard_map/attend_back/pallas_call | solution.py:698
  163.5 3.0 third_split_row.1
  166.5 9.4 %hidden_back.3 = (f32[577,384]{1,0:T(8,128)}, bf16[1536,384]{1,0:T(8,128)(2,1)}, bf16[1536,384]{1,0:T(8,128)(2,1)}, f32[8,384]{1,0:T(8,128)}, f32[8,384]{1,0:T(8,128)}) custom-call(f32[577,384]{1,0:T(8,128)} %get-tuple-element.161.refs_0_, f32[577,384]{1,0:T(8,128)} %get-tuple-element.136.refs_0_.refs_1_, bf16[577,1536]{1,0:T(8,128)(2,1)} %get-tuple-element.162.refs_2_, ...), custom_call_target="tpu_custom_call" | custom-call | flops 1048576 | bytes 65536 | tf_op jit(solution)/shard_map/hidden_back/pallas_call | solution.py:698
  185.9 14.1 %attend_back.3 = (f32[577,384]{1,0:T(8,128)}, bf16[768,384]{1,0:T(8,128)(2,1)}, bf16[832,384]{1,0:T(8,128)(2,1)}, f32[32,384]{1,0:T(8,128)}) custom-call(f32[577,384]{1,0:T(8,128)} %get-tuple-element.170.refs_0_, f32[577,384]{1,0:T(8,128)} %bitcast.39, bf16[577,1152]{1,0:T(8,128)(2,1)} %get-tuple-element.171.refs_2_, ...), custom_call_target="tpu_custom_call" | custom-call | flops 1048576 | bytes 65536 | tf_op jit(solution)/shard_map/attend_back/pallas_call | solution.py:698
  205.6 3.1 third_split_x.1
  214.0 5.2 %collective-permute-done.25.refs_1_ = bf16[384,384]{1,0:T(8,128)(2,1)} collective-permute-done((bf16[384,384]{1,0:T(8,128)(2,1)}, bf16[384,384]{1,0:T(8,128)(2,1)}, u32[]{:S(2)}, u32[]{:S(2)}) %collective-permute-start.25) | collective-permute-done | bytes 294944 | tf_op jit(solution)/shard_map/ppermute | solution.py:85
  219.2 5.2 %collective-permute-done.26.refs_2_ = bf16[384,384]{1,0:T(8,128)(2,1)} collective-permute-done((bf16[384,384]{1,0:T(8,128)(2,1)}, bf16[384,384]{1,0:T(8,128)(2,1)}, u32[]{:S(2)}, u32[]{:S(2)}) %collective-permute-start.26) | collective-permute-done | bytes 294944 | tf_op jit(solution)/shard_map/ppermute | solution.py:85
  231.1 3.0 collective-permute-start.34
  240.3 6.2 %collective-permute-done.29.refs_2_ = bf16[192,384]{1,0:T(8,128)(2,1)} collective-permute-done((bf16[192,384]{1,0:T(8,128)(2,1)}, bf16[192,384]{1,0:T(8,128)(2,1)}, u32[]{:S(2)}, u32[]{:S(2)}) %collective-permute-start.29) | collective-permute-done | bytes 147488 | tf_op jit(solution)/shard_map/ppermute | solution.py:85
  250.8 3.4 %split_group.1 = (f32[96,384]{1,0:T(8,128)}, bf16[160,384]{1,0:T(8,128)(2,1)}, bf16[160,384]{1,0:T(8,128)(2,1)}, bf16[160,384]{1,0:T(8,128)(2,1)}, bf16[160,384]...) custom-call(s32[8]{0:T(128)} %refs_0_.5, ...), custom_call_target="tpu_custom_call" | custom-call | flops 1048576 | bytes 65536 | tf_op jit(solution)/shard_map/split_group/pallas_call | solution.py:146
  274.0 3.6 %collective-permute-start.43 = (bf16[96,384]{1,0:T(8,128)(2,1)}, bf16[96,384]{1,0:T(8,128)(2,1)S(1)}, u32[]{:S(2)}, u32[]{:S(2)}) collective-permute-start(bf16[96,384]{1,0:T(8,128)(2,1)} %get-tuple-element.228.refs_5_), channel_id=1, source_target_pairs={{0,12},{1,13},{2,14},{3,15},{4,0},{5,1},{6,2},{7,3},{8,4},{9,5},{1... | collective-permute-start | bytes 221192 | tf_op jit(solution)/shard_map/ppermute | solution.py:85
  283.1 4.4 %collective-permute-start.47 = (bf16[384,384]{1,0:T(8,128)(2,1)S(1)}, bf16[384,384]{1,0:T(8,128)(2,1)S(1)}, u32[]{:S(2)}, u32[]{:S(2)}) collective-permute-start(bf16[384,384]{1,0:T(8,128)(2,1)S(1)} %constant_dynamic-update-slice_fusion.refs_1_), channel_id=1, source_target_pairs={{0,1},{1,0},{2,3},{3,2},{4,5},{5,4},{6,7},{7,6},{8,9},{9,8},{10,11... | collective-permute-start | bytes 884744 | tf_op jit(solution)/shard_map/ppermute | solution.py:85
  288.7 5.6 %collective-permute-start.48 = (bf16[384,384]{1,0:T(8,128)(2,1)S(1)}, bf16[384,384]{1,0:T(8,128)(2,1)S(1)}, u32[]{:S(2)}, u32[]{:S(2)}) collective-permute-start(bf16[384,384]{1,0:T(8,128)(2,1)S(1)} %collective-permute-done.46.refs_2_), channel_id=1, source_target_pairs={{0,1},{1,0},{2,3},{3,2},{4,5},{5,4},{6,7},{7,6},{8,9},{9,8},{10,11... | collective-permute-start | bytes 884744 | tf_op jit(solution)/shard_map/ppermute | solution.py:85
  294.3 3.0 copy.22
  302.0 12.8 %newton.1 = f32[96,384]{1,0:T(8,128)} custom-call(s32[8]{0:T(128)} %refs_0_.5, bf16[384,384]{1,0:T(8,128)(2,1)} %copy-done.3, bf16[384,384]{1,0:T(8,128)(2,1)} %copy-done.4, bf16[384,384]{1,0:T(8,128)(2,1)} %copy-done.5, bf16[384,384]{1,0:T(8,128)(2,1)} %copy-done.6, bf16[96,384]{1,0:T(8,128)(2,1)} %get-tuple-element.228.refs_5_, f32[96,384]{1,0:T(8,128)} %bitcast.42), custom_call_target="tpu_custom_call" | custom-call | flops 1048576 | bytes 65536 | tf_op jit(solution)/shard_map/newton/pallas_call | solution.py:146
  (185 shorter events, 114.6 us)
Async XLA Ops:
  9.1 11.4 %collective-permute-start.1 = (bf16[256,384]{1,0:T(8,128)(2,1)S(1)}, bf16[256,384]{1,0:T(8,128)(2,1)S(1)}, u32[]{:S(2)}, u32[]{:S(2)}) collective-permute-start(bf16[256,384]{1,0:T(8,128)(2,1)S(1)} %pad_maximum_fusion.refs_1_), channel_id=1, source_target_pairs={{0,48},{16,0},{32,16},{48,32},{64,112},{80,64},{96,80},{112,96},{1... | collective-permute-start | bytes 589832 | tf_op jit(solution)/shard_map/ppermute | solution.py:102
  13.0 12.0 %collective-permute-start.3 = (bf16[256,384]{1,0:T(8,128)(2,1)S(1)}, bf16[256,384]{1,0:T(8,128)(2,1)}, u32[]{:S(2)}, u32[]{:S(2)}) collective-permute-start(bf16[256,384]{1,0:T(8,128)(2,1)S(1)} %pad_maximum_fusion.refs_1_), channel_id=1, source_target_pairs={{0,16},{16,32},{32,48},{48,0},{64,80},{80,96},{96,112},{112,64},{1... | collective-permute-start | bytes 589832 | tf_op jit(solution)/shard_map/ppermute | solution.py:102
  29.8 9.7 %collective-permute-start.5 = (bf16[416,384]{1,0:T(8,128)(2,1)}, bf16[416,384]{1,0:T(8,128)(2,1)}, u32[]{:S(2)}, u32[]{:S(2)}) collective-permute-start(bf16[416,384]{1,0:T(8,128)(2,1)} %get-tuple-element.119.refs_0_), channel_id=1, source_target_pairs={{0,8},{1,9},{2,10},{3,11},{4,12},{5,13},{6,14},{7,15},{8,0},{9,1},... | collective-permute-start | bytes 958472 | tf_op jit(solution)/shard_map/ppermute | solution.py:85
  30.4 17.6 %collective-permute-start.6 = (bf16[416,384]{1,0:T(8,128)(2,1)}, bf16[416,384]{1,0:T(8,128)(2,1)}, u32[]{:S(2)}, u32[]{:S(2)}) collective-permute-start(bf16[416,384]{1,0:T(8,128)(2,1)} %get-tuple-element.119.refs_0_), channel_id=1, source_target_pairs={{0,4},{1,5},{2,6},{3,7},{4,8},{5,9},{6,10},{7,11},{8,12},{9,13},{1... | collective-permute-start | bytes 958472 | tf_op jit(solution)/shard_map/ppermute | solution.py:85
  50.3 18.5 %collective-permute-start.7 = (bf16[416,384]{1,0:T(8,128)(2,1)}, bf16[416,384]{1,0:T(8,128)(2,1)}, u32[]{:S(2)}, u32[]{:S(2)}) collective-permute-start(bf16[416,384]{1,0:T(8,128)(2,1)} %get-tuple-element.123.refs_0_), channel_id=1, source_target_pairs={{0,2},{1,3},{2,0},{3,1},{4,6},{5,7},{6,4},{7,5},{8,10},{9,11},{10,... | collective-permute-start | bytes 958472 | tf_op jit(solution)/shard_map/ppermute | solution.py:85
  52.3 16.5 %collective-permute-start.10 = (bf16[384,384]{1,0:T(8,128)(2,1)}, bf16[384,384]{1,0:T(8,128)(2,1)}, u32[]{:S(2)}, u32[]{:S(2)}) collective-permute-start(bf16[384,384]{1,0:T(8,128)(2,1)} %get-tuple-element.125.refs_0_), channel_id=1, source_target_pairs={{0,4},{1,5},{2,6},{3,7},{4,8},{5,9},{6,10},{7,11},{8,12},{9,13},{1... | collective-permute-start | bytes 884744 | tf_op jit(solution)/shard_map/ppermute | solution.py:85
  53.2 22.9 %collective-permute-start.12 = (bf16[416,384]{1,0:T(8,128)(2,1)}, bf16[416,384]{1,0:T(8,128)(2,1)}, u32[]{:S(2)}, u32[]{:S(2)}) collective-permute-start(bf16[416,384]{1,0:T(8,128)(2,1)} %get-tuple-element.123.refs_0_), channel_id=1, source_target_pairs={{0,1},{1,0},{2,3},{3,2},{4,5},{5,4},{6,7},{7,6},{8,9},{9,8},{10,11... | collective-permute-start | bytes 958472 | tf_op jit(solution)/shard_map/ppermute | solution.py:85
  73.1 17.4 %collective-permute-start.11 = (bf16[768,384]{1,0:T(8,128)(2,1)}, bf16[768,384]{1,0:T(8,128)(2,1)}, u32[]{:S(2)}, u32[]{:S(2)}) collective-permute-start(bf16[768,384]{1,0:T(8,128)(2,1)} %get-tuple-element.129.refs_0_), channel_id=1, source_target_pairs={{0,2},{1,3},{2,0},{3,1},{4,6},{5,7},{6,4},{7,5},{8,10},{9,11},{10,... | collective-permute-start | bytes 1769480 | tf_op jit(solution)/shard_map/ppermute | solution.py:85
  73.3 22.7 %collective-permute-start.15 = (bf16[768,384]{1,0:T(8,128)(2,1)}, bf16[768,384]{1,0:T(8,128)(2,1)}, u32[]{:S(2)}, u32[]{:S(2)}) collective-permute-start(bf16[768,384]{1,0:T(8,128)(2,1)} %get-tuple-element.129.refs_0_), channel_id=1, source_target_pairs={{0,1},{1,0},{2,3},{3,2},{4,5},{5,4},{6,7},{7,6},{8,9},{9,8},{10,11... | collective-permute-start | bytes 1769480 | tf_op jit(solution)/shard_map/ppermute | solution.py:85
  90.6 21.4 %collective-permute-start.14 = (bf16[1152,384]{1,0:T(8,128)(2,1)}, bf16[1152,384]{1,0:T(8,128)(2,1)}, u32[]{:S(2)}, u32[]{:S(2)}) collective-permute-start(bf16[1152,384]{1,0:T(8,128)(2,1)} %third_merge_x.1.refs_0_), channel_id=1, source_target_pairs={{0,2},{1,3},{2,0},{3,1},{4,6},{5,7},{6,4},{7,5},{8,10},{9,11},{10,... | collective-permute-start | bytes 2654216 | tf_op jit(solution)/shard_map/ppermute | solution.py:85
  91.9 25.1 %collective-permute-start.17 = (bf16[1152,384]{1,0:T(8,128)(2,1)}, bf16[1152,384]{1,0:T(8,128)(2,1)}, u32[]{:S(2)}, u32[]{:S(2)}) collective-permute-start(bf16[1152,384]{1,0:T(8,128)(2,1)} %third_merge_x.1.refs_0_), channel_id=1, source_target_pairs={{0,1},{1,0},{2,3},{3,2},{4,5},{5,4},{6,7},{7,6},{8,9},{9,8},{10,11... | collective-permute-start | bytes 2654216 | tf_op jit(solution)/shard_map/ppermute | solution.py:85
  146.7 16.8 %collective-permute-start.19 = (bf16[1536,384]{1,0:T(8,128)(2,1)}, bf16[1536,384]{1,0:T(8,128)(2,1)}, u32[]{:S(2)}, u32[]{:S(2)}) collective-permute-start(bf16[1536,384]{1,0:T(8,128)(2,1)} %get-tuple-element.156), channel_id=1, source_target_pairs={{0,1},{1,0},{2,3},{3,2},{4,5},{5,4},{6,7},{7,6},{8,9},{9,8},{10,11... | collective-permute-start | bytes 3538952 | tf_op jit(solution)/shard_map/ppermute | solution.py:85
  160.8 17.2 %collective-permute-start.20 = (bf16[768,384]{1,0:T(8,128)(2,1)}, bf16[768,384]{1,0:T(8,128)(2,1)}, u32[]{:S(2)}, u32[]{:S(2)}) collective-permute-start(bf16[768,384]{1,0:T(8,128)(2,1)} %get-tuple-element.165), channel_id=1, source_target_pairs={{0,1},{1,0},{2,3},{3,2},{4,5},{5,4},{6,7},{7,6},{8,9},{9,8},{10,11... | collective-permute-start | bytes 1769480 | tf_op jit(solution)/shard_map/ppermute | solution.py:85
  176.7 23.3 %collective-permute-start.21 = (bf16[1536,384]{1,0:T(8,128)(2,1)}, bf16[1536,384]{1,0:T(8,128)(2,1)}, u32[]{:S(2)}, u32[]{:S(2)}) collective-permute-start(bf16[1536,384]{1,0:T(8,128)(2,1)} %get-tuple-element.182), channel_id=1, source_target_pairs={{0,1},{1,0},{2,3},{3,2},{4,5},{5,4},{6,7},{7,6},{8,9},{9,8},{10,11... | collective-permute-start | bytes 3538952 | tf_op jit(solution)/shard_map/ppermute | solution.py:85
  181.8 21.2 %collective-permute-start.22 = (bf16[768,384]{1,0:T(8,128)(2,1)}, bf16[768,384]{1,0:T(8,128)(2,1)}, u32[]{:S(2)}, u32[]{:S(2)}) collective-permute-start(bf16[768,384]{1,0:T(8,128)(2,1)} %get-tuple-element.187), channel_id=1, source_target_pairs={{0,2},{1,3},{2,0},{3,1},{4,6},{5,7},{6,4},{7,5},{8,10},{9,11},{10,... | collective-permute-start | bytes 1769480 | tf_op jit(solution)/shard_map/ppermute | solution.py:85
  183.2 19.8 %collective-permute-start.23 = (bf16[384,384]{1,0:T(8,128)(2,1)}, bf16[384,384]{1,0:T(8,128)(2,1)}, u32[]{:S(2)}, u32[]{:S(2)}) collective-permute-start(bf16[384,384]{1,0:T(8,128)(2,1)} %get-tuple-element.188), channel_id=1, source_target_pairs={{0,2},{1,3},{2,0},{3,1},{4,6},{5,7},{6,4},{7,5},{8,10},{9,11},{10,... | collective-permute-start | bytes 884744 | tf_op jit(solution)/shard_map/ppermute | solution.py:85
  204.3 20.9 %collective-permute-start.24 = (bf16[768,384]{1,0:T(8,128)(2,1)}, bf16[768,384]{1,0:T(8,128)(2,1)}, u32[]{:S(2)}, u32[]{:S(2)}) collective-permute-start(bf16[768,384]{1,0:T(8,128)(2,1)} %get-tuple-element.189), channel_id=1, source_target_pairs={{0,2},{1,3},{2,0},{3,1},{4,6},{5,7},{6,4},{7,5},{8,10},{9,11},{10,... | collective-permute-start | bytes 1769480 | tf_op jit(solution)/shard_map/ppermute | solution.py:85
  208.7 10.5 %collective-permute-start.25 = (bf16[384,384]{1,0:T(8,128)(2,1)}, bf16[384,384]{1,0:T(8,128)(2,1)}, u32[]{:S(2)}, u32[]{:S(2)}) collective-permute-start(bf16[384,384]{1,0:T(8,128)(2,1)} %get-tuple-element.194), channel_id=1, source_target_pairs={{0,4},{1,5},{2,6},{3,7},{4,8},{5,9},{6,10},{7,11},{8,12},{9,13},{1... | collective-permute-start | bytes 884744 | tf_op jit(solution)/shard_map/ppermute | solution.py:85
  208.8 15.6 %collective-permute-start.26 = (bf16[384,384]{1,0:T(8,128)(2,1)}, bf16[384,384]{1,0:T(8,128)(2,1)}, u32[]{:S(2)}, u32[]{:S(2)}) collective-permute-start(bf16[384,384]{1,0:T(8,128)(2,1)} %get-tuple-element.195), channel_id=1, source_target_pairs={{0,8},{1,9},{2,10},{3,11},{4,12},{5,13},{6,14},{7,15},{8,0},{9,1},... | collective-permute-start | bytes 884744 | tf_op jit(solution)/shard_map/ppermute | solution.py:85
  210.8 14.4 %collective-permute-start.27 = (bf16[384,384]{1,0:T(8,128)(2,1)}, bf16[384,384]{1,0:T(8,128)(2,1)}, u32[]{:S(2)}, u32[]{:S(2)}) collective-permute-start(bf16[384,384]{1,0:T(8,128)(2,1)} %get-tuple-element.196), channel_id=1, source_target_pairs={{0,12},{1,13},{2,14},{3,15},{4,0},{5,1},{6,2},{7,3},{8,4},{9,5},{1... | collective-permute-start | bytes 884744 | tf_op jit(solution)/shard_map/ppermute | solution.py:85
  213.7 15.0 %collective-permute-start.32 = (bf16[448,384]{1,0:T(8,128)(2,1)}, bf16[448,384]{1,0:T(8,128)(2,1)}, u32[]{:S(2)}, u32[]{:S(2)}) collective-permute-start(bf16[448,384]{1,0:T(8,128)(2,1)} %get-tuple-element.210), channel_id=1, source_target_pairs={{0,2},{1,3},{2,0},{3,1},{4,6},{5,7},{6,4},{7,5},{8,10},{9,11},{10,... | collective-permute-start | bytes 1032200 | tf_op jit(solution)/shard_map/ppermute | solution.py:85
  231.0 19.7 %collective-permute-start.33 = (bf16[256,384]{1,0:T(8,128)(2,1)}, bf16[256,384]{1,0:T(8,128)(2,1)}, u32[]{:S(2)}, u32[]{:S(2)}) collective-permute-start(bf16[256,384]{1,0:T(8,128)(2,1)} %get-tuple-element.213), channel_id=1, source_target_pairs={{0,4},{1,5},{2,6},{3,7},{4,8},{5,9},{6,10},{7,11},{8,12},{9,13},{1... | collective-permute-start | bytes 589832 | tf_op jit(solution)/shard_map/ppermute | solution.py:85
  231.1 19.6 %collective-permute-start.34 = (bf16[256,384]{1,0:T(8,128)(2,1)}, bf16[256,384]{1,0:T(8,128)(2,1)}, u32[]{:S(2)}, u32[]{:S(2)}) collective-permute-start(bf16[256,384]{1,0:T(8,128)(2,1)} %get-tuple-element.214), channel_id=1, source_target_pairs={{0,8},{1,9},{2,10},{3,11},{4,12},{5,13},{6,14},{7,15},{8,0},{9,1},... | collective-permute-start | bytes 589832 | tf_op jit(solution)/shard_map/ppermute | solution.py:85
  234.1 16.6 %collective-permute-start.35 = (bf16[256,384]{1,0:T(8,128)(2,1)}, bf16[256,384]{1,0:T(8,128)(2,1)}, u32[]{:S(2)}, u32[]{:S(2)}) collective-permute-start(bf16[256,384]{1,0:T(8,128)(2,1)} %get-tuple-element.215), channel_id=1, source_target_pairs={{0,12},{1,13},{2,14},{3,15},{4,0},{5,1},{6,2},{7,3},{8,4},{9,5},{1... | collective-permute-start | bytes 589832 | tf_op jit(solution)/shard_map/ppermute | solution.py:85
  236.1 10.4 %collective-permute-start.29 = (bf16[192,384]{1,0:T(8,128)(2,1)}, bf16[192,384]{1,0:T(8,128)(2,1)}, u32[]{:S(2)}, u32[]{:S(2)}) collective-permute-start(bf16[192,384]{1,0:T(8,128)(2,1)} %get-tuple-element.200), channel_id=1, source_target_pairs={{0,8},{1,9},{2,10},{3,11},{4,12},{5,13},{6,14},{7,15},{8,0},{9,1},... | collective-permute-start | bytes 442376 | tf_op jit(solution)/shard_map/ppermute | solution.py:85
  236.1 12.6 %collective-permute-start.30 = (bf16[192,384]{1,0:T(8,128)(2,1)}, bf16[192,384]{1,0:T(8,128)(2,1)}, u32[]{:S(2)}, u32[]{:S(2)}) collective-permute-start(bf16[192,384]{1,0:T(8,128)(2,1)} %get-tuple-element.201), channel_id=1, source_target_pairs={{0,12},{1,13},{2,14},{3,15},{4,0},{5,1},{6,2},{7,3},{8,4},{9,5},{1... | collective-permute-start | bytes 442376 | tf_op jit(solution)/shard_map/ppermute | solution.py:85
  254.2 9.5 %collective-permute-start.37 = (bf16[160,384]{1,0:T(8,128)(2,1)}, bf16[160,384]{1,0:T(8,128)(2,1)}, u32[]{:S(2)}, u32[]{:S(2)}) collective-permute-start(bf16[160,384]{1,0:T(8,128)(2,1)} %get-tuple-element.219), channel_id=1, source_target_pairs={{0,32},{16,48},{32,0},{48,16},{64,96},{80,112},{96,64},{112,80},{1... | collective-permute-start | bytes 368648 | tf_op jit(solution)/shard_map/ppermute | solution.py:102
  255.8 10.6 %collective-permute-start.38 = (bf16[160,384]{1,0:T(8,128)(2,1)}, bf16[160,384]{1,0:T(8,128)(2,1)}, u32[]{:S(2)}, u32[]{:S(2)}) collective-permute-start(bf16[160,384]{1,0:T(8,128)(2,1)} %get-tuple-element.220), channel_id=1, source_target_pairs={{0,48},{16,0},{32,16},{48,32},{64,112},{80,64},{96,80},{112,96},{1... | collective-permute-start | bytes 368648 | tf_op jit(solution)/shard_map/ppermute | solution.py:102
  256.9 9.5 %collective-permute-start.39 = (bf16[160,384]{1,0:T(8,128)(2,1)}, bf16[160,384]{1,0:T(8,128)(2,1)}, u32[]{:S(2)}, u32[]{:S(2)}) collective-permute-start(bf16[160,384]{1,0:T(8,128)(2,1)} %get-tuple-element.221), channel_id=1, source_target_pairs={{0,64},{16,80},{32,96},{48,112},{64,0},{80,16},{96,32},{112,48},{1... | collective-permute-start | bytes 368648 | tf_op jit(solution)/shard_map/ppermute | solution.py:102
  260.8 9.5 %collective-permute-start.41 = (bf16[160,384]{1,0:T(8,128)(2,1)}, bf16[160,384]{1,0:T(8,128)(2,1)}, u32[]{:S(2)}, u32[]{:S(2)}) collective-permute-start(bf16[160,384]{1,0:T(8,128)(2,1)} %get-tuple-element.223), channel_id=1, source_target_pairs={{0,96},{16,112},{32,64},{48,80},{64,32},{80,48},{96,0},{112,16},{1... | collective-permute-start | bytes 368648 | tf_op jit(solution)/shard_map/ppermute | solution.py:102
  283.1 17.4 %collective-permute-start.47 = (bf16[384,384]{1,0:T(8,128)(2,1)S(1)}, bf16[384,384]{1,0:T(8,128)(2,1)S(1)}, u32[]{:S(2)}, u32[]{:S(2)}) collective-permute-start(bf16[384,384]{1,0:T(8,128)(2,1)S(1)} %constant_dynamic-update-slice_fusion.refs_1_), channel_id=1, source_target_pairs={{0,1},{1,0},{2,3},{3,2},{4,5},{5,4},{6,7},{7,6},{8,9},{9,8},{10,11... | collective-permute-start | bytes 884744 | tf_op jit(solution)/shard_map/ppermute | solution.py:85
  288.7 11.8 %collective-permute-start.48 = (bf16[384,384]{1,0:T(8,128)(2,1)S(1)}, bf16[384,384]{1,0:T(8,128)(2,1)S(1)}, u32[]{:S(2)}, u32[]{:S(2)}) collective-permute-start(bf16[384,384]{1,0:T(8,128)(2,1)S(1)} %collective-permute-done.46.refs_2_), channel_id=1, source_target_pairs={{0,1},{1,0},{2,3},{3,2},{4,5},{5,4},{6,7},{7,6},{8,9},{9,8},{10,11... | collective-permute-start | bytes 884744 | tf_op jit(solution)/shard_map/ppermute | solution.py:85
  (33 other events, 204.0 us)

commit v2 on v0

--- a/solution.py
+++ b/solution.py
@@ -184,7 +184,12 @@
 
 
 def final_kernel(heads, hidden, spread, *refs):
-    parts, outs = refs[:4], list(refs[4:])
+    if spread:
+        rows = refs[0].shape[0] // 2
+        parts = [ref.at[pl.ds(at * rows, rows)] for ref in refs[:2] for at in range(2)]
+        outs = list(refs[2:])
+    else:
+        parts, outs = refs[:4], list(refs[4:])
     _, row, core = my_place()
     base = 0
     if heads:
@@ -204,9 +209,9 @@
         base += 2 * WIDE
         outs = outs[2:]
     if spread:
-        total = full(parts[0][base:])
+        total = full(parts[0][base : base + VPAD])
         for part in parts[1:]:
-            total = total + full(part[base:])
+            total = total + full(part[base : base + VPAD])
         outs[0][...] = total
 
 
@@ -245,37 +250,15 @@
     return full(ref[start : start + VPAD]) + full(ref[start + VPAD : start + 2 * VPAD])
 
 
-def split_core_kernel(heads, hidden, spread, *refs):
-    refs = list(refs)
-    keep_ref, sent_ref = refs[-2:]
+def split_heads(grads, keep_ref, sent_ref):
     _, _, core = my_place()
     put = 0
-    if heads:
-        qkv_ref, out_ref = refs[:2]
-        refs = refs[2:]
-        for row in range(2):
-            for at in range(4):
-                source = out_ref if at == 3 else qkv_ref
-                start = (0 if at == 3 else at * WIDE) + row * 2 * BLK
-                keep_ref[put : put + BLK] = source[rows_at(start + core * BLK)]
-                sent_ref[put : put + BLK] = source[rows_at(start + (1 - core) * BLK)]
-                put += BLK
-    if hidden:
-        for source in refs[:2]:
-            keep_ref[put : put + 2 * WIDE] = source[: 2 * WIDE]
-            sent_ref[put : put + 2 * WIDE] = source[2 * WIDE :]
-            put += 2 * WIDE
-        refs = refs[2:]
-    if spread:
-        *pieces, vec_ref = refs[:-2]
-        vec_ref[VROWS:] = jnp.zeros((VPAD - VROWS, WIDE), jnp.float32)
-        for layer_at in range(LAYERS):
-            base = layer_at * (VROWS // LAYERS)
-            one, two, three = pieces[3 * layer_at : 3 * layer_at + 3]
-            vec_ref[base : base + 5] = one[:5]
-            vec_ref[base + 5 : base + 8] = two[:3]
-            vec_ref[base + 8 : base + 12] = three[...]
-        put_vec(sent_ref, put, vec_ref[...])
+    for row in range(2):
+        for at in range(4):
+            start = at * WIDE + row * 2 * BLK
+            keep_ref[put : put + BLK] = grads[rows_at(start + core * BLK)]
+            sent_ref[put : put + BLK] = grads[rows_at(start + (1 - core) * BLK)]
+            put += BLK
 
 
 def split_row_kernel(heads, hidden, spread, *refs):
@@ -339,17 +322,6 @@
     out_ref[...] = total
     if heads:
         out_ref[BLK : 2 * BLK] = jnp.where(x == 0, total[BLK : 2 * BLK], 0.0)
-
-
-def scatter_core(grads, heads, hidden, spread, name):
-    rows = 8 * BLK * heads + 16 * BLK * hidden
-    return small_call(
-        lambda *refs: split_core_kernel(heads, hidden, spread, *refs),
-        [(VPAD, jnp.float32)] * spread
-        + [(rows, jnp.bfloat16), (rows + 2 * VPAD * spread, jnp.bfloat16)],
-        grads,
-        name=name + "_split_core",
-    )
 
 
 def scatter_row(keep, came, heads, hidden, spread, name, vec_sum=None):
@@ -528,9 +500,13 @@
     attn_ref[:, column(at)] = half(jnp.where(row < 64, sums[0], sums[1]).T)
 
 
-def attend_back_kernel(layer_at, up_ref, in_ref, qkv_ref, attn_ref, prob_ref, qkv_w, out_w, vec_ref, grad_ref, gqkv_ref, gout_ref, sum_ref, upstream_ref, back_ref):
+def attend_back_kernel(layer_at, up_ref, in_ref, qkv_ref, attn_ref, prob_ref, qkv_w, out_w, vec_ref, *refs):
+    spread = len(refs) > 8
+    others = refs[:5] if spread else ()
+    grad_ref, keep_ref, sent_ref, total_ref, upstream_ref, back_ref, grads_ref, sum_ref = refs[-8:]
+    sum_ref[...] = jnp.zeros_like(sum_ref)
     out_low = half(up_ref[...])
-    gout_ref[...] = half(row_contract(out_low, attn_ref[...]))
+    grads_ref[3 * WIDE :] = half(row_contract(out_low, attn_ref[...]))
     upstream_ref[...] = half(product(out_low, out_w[...]))
     sum_ref[4:5] = jnp.sum(full(out_low), 0, keepdims=True)
     for at in range(HEADS // 2):
@@ -542,7 +518,7 @@
     for third in range(3):
         rows = slice(third * WIDE, (third + 1) * WIDE)
         piece = back_ref[:, rows]
-        gqkv_ref[rows] = half(row_contract(piece, normed_low))
+        grads_ref[rows] = half(row_contract(piece, normed_low))
         back_normed = back_normed + product(piece, qkv_w[rows])
         if third != 1:
             put = 2 if third == 0 else 3
@@ -550,6 +526,19 @@
     sum_ref[0:1] = jnp.sum(back_normed * normed, 0, keepdims=True)
     sum_ref[1:2] = jnp.sum(back_normed, 0, keepdims=True)
     grad_ref[...] = up_ref[...] + norm_back(back_normed, normed, inv_std, gain)
+    split_heads(grads_ref, keep_ref, sent_ref)
+    if not spread:
+        total_ref[...] = sum_ref[...]
+        return
+    total_ref[VROWS:] = jnp.zeros((VPAD - VROWS, WIDE), jnp.float32)
+    pieces = (sum_ref, *others)
+    for layer in range(LAYERS):
+        base = layer * (VROWS // LAYERS)
+        one, two, three = pieces[3 * layer : 3 * layer + 3]
+        total_ref[base : base + 5] = one[:5]
+        total_ref[base + 5 : base + 8] = two[:3]
+        total_ref[base + 8 : base + 12] = three[...]
+    put_vec(sent_ref, 2 * WIDE, total_ref[...])
 
 
 def attend_back_pair(at, qkv_ref, upstream_ref, prob_ref, back_ref):
@@ -589,23 +578,69 @@
     out_ref[...] = total
 
 
-def hidden_back_kernel(layer_at, up_ref, mid_ref, act_ref, slope_ref, up_w, down_w, vec_ref, grad_ref, gup_ref, gdown_ref, sum_ref, bias_ref):
+def hidden_back_kernel(layer_at, up_ref, mid_ref, act_ref, slope_ref, up_w, down_w, vec_ref, grad_ref, keep_ref, sent_ref, sum_ref, bias_ref):
     down_low = half(up_ref[...])
     normed, inv_std = normalize(mid_ref[...])
     gain = row_of(vec_ref, layer_at, 5)
     hidden_low = half(normed * gain + row_of(vec_ref, layer_at, 6))
     back_hidden = jnp.zeros(normed.shape, jnp.float32)
+    sum_ref[...] = jnp.zeros_like(sum_ref)
     for chunk in range(4):
         rows = slice(chunk * WIDE, (chunk + 1) * WIDE)
         up_low = half(col_contract(down_low, down_w[rows]) * slope_ref[:, rows])
-        gdown_ref[rows] = half(row_contract(act_ref[:, rows], down_low))
-        gup_ref[rows] = half(row_contract(up_low, hidden_low))
+        target, turn_at = (keep_ref, sent_ref)[chunk // 2], chunk % 2
+        for member, value in enumerate(
+            (row_contract(up_low, hidden_low), row_contract(act_ref[:, rows], down_low))
+        ):
+            put = (2 * member + turn_at) * WIDE
+            target[put : put + WIDE] = half(value)
         bias_ref[chunk : chunk + 1] = jnp.sum(full(up_low), 0, keepdims=True)
         back_hidden = back_hidden + product(up_low, up_w[rows])
     sum_ref[0:1] = jnp.sum(back_hidden * normed, 0, keepdims=True)
     sum_ref[1:2] = jnp.sum(back_hidden, 0, keepdims=True)
     sum_ref[2:3] = jnp.sum(full(down_low), 0, keepdims=True)
     grad_ref[...] = up_ref[...] + norm_back(back_hidden, normed, inv_std, gain)
+
+
+def layer_one_kernel(layer_at, in_ref, cot_ref, qkv_w, out_w, up_w, down_w, vec_ref, bias_ref, *refs):
+    stream_ref, grad_ref, keep_ref, sent_ref, one_ref, two_ref, bias_sum_ref = refs[:7]
+    mid_ref, qkv_ref, attn_ref, prob_ref, act_ref, slope_ref, mid_grad_ref, *rest = refs[7:]
+    heads, hidden = pl.ds(0, 2 * WIDE), pl.ds(2 * WIDE, 4 * WIDE)
+    attend_kernel(layer_at, in_ref, qkv_w, out_w, vec_ref, mid_ref, qkv_ref, attn_ref, prob_ref)
+    hidden_kernel(
+        layer_at, mid_ref, up_w, down_w, vec_ref, bias_ref, stream_ref, act_ref, slope_ref
+    )
+    hidden_back_kernel(
+        layer_at,
+        cot_ref,
+        mid_ref,
+        act_ref,
+        slope_ref,
+        up_w,
+        down_w,
+        vec_ref,
+        mid_grad_ref,
+        keep_ref.at[hidden],
+        sent_ref.at[hidden],
+        two_ref,
+        bias_sum_ref,
+    )
+    attend_back_kernel(
+        layer_at,
+        mid_grad_ref,
+        in_ref,
+        qkv_ref,
+        attn_ref,
+        prob_ref,
+        qkv_w,
+        out_w,
+        vec_ref,
+        grad_ref,
+        keep_ref.at[heads],
+        sent_ref.at[heads],
+        one_ref,
+        *rest,
+    )
 
 
 def layer_call(kernel, layer_at, ins, outs, scratch=(), name=None, vmem=24):
@@ -640,23 +675,59 @@
     )
 
 
-def attention_backward(layer_at, upstream, inputs, stored, w_qkv, w_out, vec_full):
+def back_scratch(length):
+    return [
+        pltpu.VMEM((length, WIDE), jnp.bfloat16),
+        pltpu.VMEM((length, 3 * WIDE), jnp.bfloat16),
+        pltpu.VMEM((4 * WIDE, WIDE), jnp.bfloat16),
+        pltpu.VMEM((8, WIDE), jnp.float32),
+    ]
+
+
+def attention_backward(layer_at, upstream, inputs, stored, w_qkv, w_out, vec_full, others):
     qkv_low, attn_low, probs = stored
     return layer_call(
         attend_back_kernel,
         layer_at,
-        [upstream, inputs, qkv_low, attn_low, probs, w_qkv, w_out, vec_full],
+        [upstream, inputs, qkv_low, attn_low, probs, w_qkv, w_out, vec_full, *others],
         [
             (inputs.shape, jnp.float32),
-            (w_qkv.shape, jnp.bfloat16),
-            (w_out.shape, jnp.bfloat16),
+            ((2 * WIDE, WIDE), jnp.bfloat16),
+            ((2 * WIDE + 2 * VPAD, WIDE), jnp.bfloat16),
+            ((VPAD, WIDE), jnp.float32),
+        ],
+        scratch=back_scratch(inputs.shape[0]),
+        name="attend_back",
+    )
+
+
+def layer_one(inputs, cotangent, w_qkv, w_out, w_up, w_down, vec_full, bias_up):
+    length = inputs.shape[0]
+    return layer_call(
+        layer_one_kernel,
+        1,
+        [inputs, cotangent, w_qkv, w_out, w_up, w_down, vec_full, bias_up],
+        [
+            (inputs.shape, jnp.float32),
+            (inputs.shape, jnp.float32),
+            ((6 * WIDE, WIDE), jnp.bfloat16),
+            ((6 * WIDE, WIDE), jnp.bfloat16),
             ((8, WIDE), jnp.float32),
+            ((8, WIDE), jnp.float32),
+            ((4, WIDE), jnp.float32),
         ],
         scratch=[
-            pltpu.VMEM(attn_low.shape, jnp.bfloat16),
-            pltpu.VMEM(qkv_low.shape, jnp.bfloat16),
+            pltpu.VMEM(inputs.shape, jnp.float32),
+            pltpu.VMEM((length, 3 * WIDE), jnp.bfloat16),
+            pltpu.VMEM(inputs.shape, jnp.bfloat16),
+            pltpu.VMEM((HEADS, length, length), jnp.bfloat16),
+            pltpu.VMEM((length, FF), jnp.bfloat16),
+            pltpu.VMEM((length, FF), jnp.float32),
+            pltpu.VMEM(inputs.shape, jnp.float32),
+            *back_scratch(length),
         ],
-        name="attend_back",
+        name="layer_one",
+        vmem=36,
     )
 
 
@@ -741,11 +812,18 @@
         name="first_merge_x",
     )
     second_x, third, first_x = tie((second_x, third, first_x))
-    first_parts = all_four(first_x)
+    beside_first = other_row(first_x)
+    pair_first = jnp.concatenate([first_x, beside_first], 0)
+    first_parts = [pair_first, other_core(pair_first)]
     beside_second, core_second = other_row(second_x), other_core(second_x)
     third_parts = from_x(third)
-    first_parts, third_parts = tie((first_parts, third_parts))
     w_qkv0, w_out0, vec_full = whole(first_parts, True, False, True, "first")
+    bias0 = to_own_order(vec_full[8:12].reshape(-1), place)
+    bias1 = to_own_order(vec_full[20:24].reshape(-1), place)
+
+    inputs0 = tokens[0]
+    middle0, *attn0 = attention_forward(0, inputs0, w_qkv0, w_out0, vec_full)
+    third_parts, beside_second, middle0 = tie((third_parts, beside_second, middle0))
     (third_x,) = small_call(
         merge_third_kernel,
         [(12 * BLK, jnp.bfloat16)],
@@ -753,12 +831,6 @@
         scratch=[HOLD_HEADS],
         name="third_merge_x",
     )
-    bias0 = to_own_order(vec_full[8:12].reshape(-1), place)
-    bias1 = to_own_order(vec_full[20:24].reshape(-1), place)
-
-    inputs0 = tokens[0]
-    middle0, *attn0 = attention_forward(0, inputs0, w_qkv0, w_out0, vec_full)
-    third_x, beside_second, middle0 = tie((third_x, beside_second, middle0))
     beside = other_row(third_x)
     core_third = other_core(third_x)
     second_parts = [second_x, beside_second, core_second, other_core(beside_second)]
@@ -767,45 +839,35 @@
     beside, inputs1 = tie((beside, inputs1))
     third_parts = [third_x, beside, core_third, other_core(beside)]
     w_qkv1, w_out1, w_up1, w_down1 = whole(third_parts, True, True, False, "third")
-    middle1, *attn1 = attention_forward(1, inputs1, w_qkv1, w_out1, vec_full)
-    stream, *mlp1 = hidden_forward(1, middle1, w_up1, w_down1, vec_full, bias1)
-
     upstream = cotangent[0] * full(live)[0]
-    mid_grad, grad_up, grad_down, sums_two1, sums_up1 = hidden_backward(
-        1, upstream, middle1, mlp1, w_up1, w_down1, vec_full
-    )
-    upstream, grad_qkv, grad_out, sums_one1 = attention_backward(
-        1, mid_grad, inputs1, attn1, w_qkv1, w_out1, vec_full
-    )
-    keep, sent = scatter_core([grad_qkv, grad_out, grad_up, grad_down], True, True, False, "third")
-    upstream, sent = tie((upstream, sent))
+    stream, upstream, keep, sent, sums_one1, sums_two1, sums_up1 = layer_one(
+        inputs1, upstream, w_qkv1, w_out1, w_up1, w_down1, vec_full, bias1
+    )
     came = other_core(sent)
-    mid_grad, grad_up, grad_down, sums_two0, sums_up0 = hidden_backward(
+    mid_grad, keep_f, sent_f, sums_two0, sums_up0 = hidden_backward(
         0, upstream, middle0, mlp0, w_up0, w_down0, vec_full
     )
-    keep_f, sent_f = scatter_core([grad_up, grad_down], False, True, False, "second")
-    mid_grad, sent_f, came = tie((mid_grad, sent_f, came))
     came_f = other_core(sent_f)
+    vec_full, came = tie((vec_full, came))
     keep, sent = scatter_row(keep, came, True, True, False, "third")
-    mid_grad, sent = tie((mid_grad, sent))
+    vec_full, sent = tie((vec_full, sent))
     came = other_row(sent)
-    token_grad, grad_qkv, grad_out, sums_one0 = attention_backward(
-        0, mid_grad, inputs0, attn0, w_qkv0, w_out0, vec_full
-    )
-    grad_qkv, came_f = tie((grad_qkv, came_f))
+    bias_sum0, bias_sum1 = (from_own_order(part, place) for part in (sums_up0, sums_up1))
+    token_grad, keep_h, sent_h, vec_sum = attention_backward(
+        0,
+        mid_grad,
+        inputs0,
+        attn0,
+        w_qkv0,
+        w_out0,
+        vec_full,
+        (sums_two0, bias_sum0, sums_one1, sums_two1, bias_sum1),
+    )
+    vec_sum, came_f = tie((vec_sum, came_f))
     keep_f, sent_f = scatter_row(keep_f, came_f, False, True, False, "second")
-    grad_qkv, sent_f, came = tie((grad_qkv, sent_f, came))
+    sent_h, sent_f, came = tie((sent_h, sent_f, came))
     came_f = other_row(sent_f)
-    bias_sum0, bias_sum1 = (from_own_order(part, place) for part in (sums_up0, sums_up1))
-    vec_sum, keep_h, sent_h = scatter_core(
-        [grad_qkv, grad_out, sums_one0, sums_two0, bias_sum0, sums_one1, sums_two1, bias_sum1],
-        True,
-        False,
-        True,
-        "first",
-    )
     came_h = other_core(sent_h)
-    came_h, came = tie((came_h, came))
     keep, *sent_x = scatter_x(keep, came, True, True, False, "third")
     came_x = spread_x(sent_x)
     came_f, came_x = tie((came_f, came_x))

time: 297 us -> 295 us (level)
  waiting for transfers between devices: 90.8 us -> 82.6 us
  local copies, waits for them, and re-layouts: 45.7 us -> 49.8 us
  other arithmetic: 4.62 us -> 8.51 us
    ppermute x36 -> x35, waiting for transfers between devices: 71.4 us -> 63.8 us  [near(): return lax.ppermute(part, 'dp', [(at, change(at)) for at in range(16)])]
    select_n x7, other arithmetic: 0.05 us -> 3.33 us  [swap(): return jnp.where(flag == 0, parts, jnp.flip(parts, axis))]
    ppermute x36 -> x35, starting transfers between devices: 46.9 us -> 44.3 us  [near(): return lax.ppermute(part, 'dp', [(at, change(at)) for at in range(16)])]
    pallas_call x20 -> x17, Pallas kernels: 30.4 us -> 28.1 us  [small_call(): pl.pallas_call(kernel, out_shape=[jax.ShapeDtypeStruct((rows, WIDE), kind...]
    pallas_call x8 -> x5, Pallas kernels: 51.1 us -> 53.3 us  [layer_call(): pl.pallas_call(body, out_shape=[jax.ShapeDtypeStruct(shape, kind) for sha...]
    unnamed x114 -> x123, local copies, waits for them, and re-layouts: 44.3 us -> 42.7 us
  transfers between devices with their start and end apart: 47 -> 46, of which waited for: 27 -> 23; matrix products, arithmetic and copies ran while one was open for 3% -> 6% of each run, Pallas kernels for 13% -> 13%
where the time goes in v2:
time: 295 us; the launch traced here: 289 us
  waiting for transfers between devices  82.6 us (28%)
  Pallas kernels  81.4 us (28%)
  starting transfers between devices  64.9 us (22%)
  local copies, waits for them, and re-layouts  49.8 us (17%)
  other arithmetic  8.51 us (3%)
    ppermute x35, waiting for transfers between devices, near(): return lax.ppermute(part, 'dp', [(at, change(at)) for at in range(16)])  63.8 us
    pallas_call x5, Pallas kernels, layer_call(): pl.pallas_call(body, out_shape=[jax.ShapeDtypeStruct(shape, kind) for sha...  53.3 us
    ppermute x35, starting transfers between devices, near(): return lax.ppermute(part, 'dp', [(at, change(at)) for at in range(16)])  44.3 us
    unnamed x123, local copies, waits for them, and re-layouts  42.7 us
    pallas_call x17, Pallas kernels, small_call(): pl.pallas_call(kernel, out_shape=[jax.ShapeDtypeStruct((rows, WIDE), kind...  28.1 us
    ppermute x11, starting transfers between devices, along_group(): return lax.ppermute(part, 'group', pairs)  20.6 us
    ppermute x11, waiting for transfers between devices, along_group(): return lax.ppermute(part, 'group', pairs)  18.8 us
  transfers between devices with their start and end apart: 46, of which 23 were waited for; matrix products, arithmetic and copies ran while one was open for 6% of the time, Pallas kernels for 13%

profile of v2, /device:TPU:1, one launch (start us, length us, event | category | flops | bytes accessed | tf_op | source)
XLA Modules:
  0.0 289.2 jit_solution(7508139110689572050)
XLA Ops:
  2.8 3.8 %collective-permute-start = (bf16[128,384]{1,0:T(8,128)(2,1)S(1)}, bf16[128,384]{1,0:T(8,128)(2,1)S(1)}, u32[]{:S(2)}, u32[]{:S(2)}) collective-permute-start(bf16[128,384]{1,0:T(8,128)(2,1)S(1)} %pad_maximum_fusion.1), channel_id=1, source_target_pairs={{0,64},{16,80},{32,96},{48,112},{64,0},{80,16},{96,32},{112,48},{1... | collective-permute-start | bytes 294920 | tf_op jit(solution)/shard_map/ppermute | solution.py:102
  6.6 2.5 collective-permute-done
  9.1 3.8 %collective-permute-start.1 = (bf16[256,384]{1,0:T(8,128)(2,1)S(1)}, bf16[256,384]{1,0:T(8,128)(2,1)S(1)}, u32[]{:S(2)}, u32[]{:S(2)}) collective-permute-start(bf16[256,384]{1,0:T(8,128)(2,1)S(1)} %pad_maximum_fusion.refs_0_), channel_id=1, source_target_pairs={{0,48},{16,0},{32,16},{48,32},{64,112},{80,64},{96,80},{112,96},{1... | collective-permute-start | bytes 589832 | tf_op jit(solution)/shard_map/ppermute | solution.py:102
  13.7 6.9 %collective-permute-done.1.refs_1_ = bf16[256,384]{1,0:T(8,128)(2,1)S(1)} collective-permute-done((bf16[256,384]{1,0:T(8,128)(2,1)S(1)}, bf16[256,384]{1,0:T(8,128)(2,1)S(1)}, u32[]{:S(2)}, u32[]{:S(2)}) %collective-permute-start.1) | collective-permute-done | bytes 196640 | tf_op jit(solution)/shard_map/ppermute | solution.py:102
  20.6 4.3 %collective-permute-done.3.refs_3_ = bf16[256,384]{1,0:T(8,128)(2,1)S(1)} collective-permute-done((bf16[256,384]{1,0:T(8,128)(2,1)S(1)}, bf16[256,384]{1,0:T(8,128)(2,1)S(1)}, u32[]{:S(2)}, u32[]{:S(2)}) %collective-permute-start.3) | collective-permute-done | bytes 196640 | tf_op jit(solution)/shard_map/ppermute | solution.py:102
  30.0 5.1 %collective-permute-done.4.refs_1_ = bf16[416,384]{1,0:T(8,128)(2,1)S(1)} collective-permute-done((bf16[416,384]{1,0:T(8,128)(2,1)S(1)}, bf16[416,384]{1,0:T(8,128)(2,1)S(1)}, u32[]{:S(2)}, u32[]{:S(2)}) %collective-permute-start.4) | collective-permute-done | bytes 319520 | tf_op jit(solution)/shard_map/ppermute | solution.py:85
  35.1 3.1 %collective-permute-done.5.refs_2_ = bf16[416,384]{1,0:T(8,128)(2,1)S(1)} collective-permute-done((bf16[416,384]{1,0:T(8,128)(2,1)S(1)}, bf16[416,384]{1,0:T(8,128)(2,1)S(1)}, u32[]{:S(2)}, u32[]{:S(2)}) %collective-permute-start.5) | collective-permute-done | bytes 319520 | tf_op jit(solution)/shard_map/ppermute | solution.py:85
  38.2 8.4 %collective-permute-done.6.refs_3_ = bf16[416,384]{1,0:T(8,128)(2,1)S(1)} collective-permute-done((bf16[416,384]{1,0:T(8,128)(2,1)S(1)}, bf16[416,384]{1,0:T(8,128)(2,1)S(1)}, u32[]{:S(2)}, u32[]{:S(2)}) %collective-permute-start.6) | collective-permute-done | bytes 319520 | tf_op jit(solution)/shard_map/ppermute | solution.py:85
  48.9 7.3 %collective-permute-done.11 = bf16[416,384]{1,0:T(8,128)(2,1)S(1)} collective-permute-done((bf16[416,384]{1,0:T(8,128)(2,1)S(1)}, bf16[416,384]{1,0:T(8,128)(2,1)S(1)}, u32[]{:S(2)}, u32[]{:S(2)}) %collective-permute-start.11) | collective-permute-done | bytes 319520 | tf_op jit(solution)/shard_map/ppermute | solution.py:85
  66.8 6.5 %attend.1 = (f32[577,384]{1,0:T(8,128)S(1)}, bf16[577,1152]{1,0:T(8,128)(2,1)S(1)}, bf16[577,384]{1,0:T(8,128)(2,1)S(1)}, bf16[6,577,577]{2,1,0:T(8,128)(2,1)S(1)}) custom-call(f32[577,384]{1,0:T(8,128)S(1)} %bitcast.38, bf16[1152,384]{1,0:T(8,128)(2,1)S(1)} %get-tuple-element.108.refs_1_.refs_5_, bf16[384,384]{1,0:T(8,128)(2,1)S(1)} %copy-done.19, ...), custom_call_target="tpu_custom_call" | custom-call | flops 1048576 | bytes 65536 | tf_op jit(solution)/shard_map/attend/pallas_call | solution.py:650
  82.4 2.7 collective-permute-done.15.refs_3_
  89.8 3.8 %hidden.1 = (f32[577,384]{1,0:T(8,128)S(1)}, bf16[577,1536]{1,0:T(8,128)(2,1)S(1)}, f32[577,1536]{1,0:T(8,128)S(1)}) custom-call(f32[577,384]{1,0:T(8,128)S(1)} %copy-done.3, bf16[1536,384]{1,0:T(8,128)(2,1)S(1)} %get-tuple-element.118.refs_1_.refs_4_, bf16[1536,384]{1,0:T(8,128)(2,1)S(1)} %get-tuple-element.119.refs_2_.refs_5_, ...), custom_call_target="tpu_custom_call" | custom-call | flops 1048576 | bytes 65536 | tf_op jit(solution)/shard_map/hidden/pallas_call | solution.py:650
  97.6 3.5 %collective-permute-done.13.refs_1_ = bf16[1152,384]{1,0:T(8,128)(2,1)} collective-permute-done((bf16[1152,384]{1,0:T(8,128)(2,1)}, bf16[1152,384]{1,0:T(8,128)(2,1)}, u32[]{:S(2)}, u32[]{:S(2)}) %collective-permute-start.13) | collective-permute-done | bytes 884768 | tf_op jit(solution)/shard_map/ppermute | solution.py:85
  107.4 26.9 %layer_one.1 = (f32[577,384]{1,0:T(8,128)S(1)}, f32[577,384]{1,0:T(8,128)S(1)}, bf16[2304,384]{1,0:T(8,128)(2,1)S(1)}, bf16[2304,384]{1,0:T(8,128)(2,1)}, f32[8,...) custom-call(f32[577,384]{1,0:T(8,128)S(1)} %copy-done.30, f32[577,384]{1,0:T(8,128)S(1)} %copy-done.7, ...), custom_call_target="tpu_custom_call" | custom-call | flops 1048576 | bytes 65536 | tf_op jit(solution)/shard_map/layer_one/pallas_call | solution.py:650
  144.8 5.8 %hidden_back.1 = (f32[577,384]{1,0:T(8,128)S(1)}, bf16[1536,384]{1,0:T(8,128)(2,1)S(1)}, bf16[1536,384]{1,0:T(8,128)(2,1)S(1)}, f32[8,384]{1,0:T(8,128)S(1)}, f32[4,384]{1,0:T(4,128)S(1)}) custom-call(f32[577,384]{1,0:T(8,128)S(1)} %copy-done.26, f32[577,384]{1,0:T(8,128)S(1)} %copy-done.4, bf16[577,1536]{1,0:T(8,128)(2,1)S(1)} %copy-done.11, ...), custom_call_target="tpu_custom_call" | custom-call | flops 1048576 | bytes 65536 | tf_op jit(solution)/shard_map/hidden_back/pallas_call | solution.py:650
  158.2 2.8 third_split_row.1
  181.5 10.2 %attend_back.1 = (f32[577,384]{1,0:T(8,128)S(1)}, bf16[768,384]{1,0:T(8,128)(2,1)S(1)}, bf16[832,384]{1,0:T(8,128)(2,1)S(1)}, f32[32,384]{1,0:T(8,128)S(1)}) custom-call(f32[577,384]{1,0:T(8,128)S(1)} %copy-done.24, f32[577,384]{1,0:T(8,128)S(1)} %bitcast.39, bf16[577,1152]{1,0:T(8,128)(2,1)S(1)} %copy-done.17, bf16[577,384]{1,0:T(8,128)(2,1)S(1)} %copy-done.35, ...), custom_call_target="tpu_custom_call" | custom-call | flops 1048576 | bytes 65536 | tf_op jit(solution)/shard_map/attend_back/pallas_call | solution.py:650
  196.1 2.8 collective-permute-start.23
  201.6 3.6 %collective-permute-done.22.refs_1_ = bf16[384,384]{1,0:T(8,128)(2,1)S(1)} collective-permute-done((bf16[384,384]{1,0:T(8,128)(2,1)S(1)}, bf16[384,384]{1,0:T(8,128)(2,1)S(1)}, u32[]{:S(2)}, u32[]{:S(2)}) %collective-permute-start.22) | collective-permute-done | bytes 294944 | tf_op jit(solution)/shard_map/ppermute | solution.py:85
  205.3 6.9 %collective-permute-done.23.refs_2_ = bf16[384,384]{1,0:T(8,128)(2,1)S(1)} collective-permute-done((bf16[384,384]{1,0:T(8,128)(2,1)S(1)}, bf16[384,384]{1,0:T(8,128)(2,1)S(1)}, u32[]{:S(2)}, u32[]{:S(2)}) %collective-permute-start.23) | collective-permute-done | bytes 294944 | tf_op jit(solution)/shard_map/ppermute | solution.py:85
  216.7 2.4 collective-permute-start.31
  223.0 9.0 %collective-permute-done.26.refs_2_ = bf16[192,384]{1,0:T(8,128)(2,1)S(1)} collective-permute-done((bf16[192,384]{1,0:T(8,128)(2,1)S(1)}, bf16[192,384]{1,0:T(8,128)(2,1)S(1)}, u32[]{:S(2)}, u32[]{:S(2)}) %collective-permute-start.26) | collective-permute-done | bytes 147488 | tf_op jit(solution)/shard_map/ppermute | solution.py:85
  235.6 2.4 collective-permute-start.35
  237.9 2.6 collective-permute-start.36
  241.2 3.6 %collective-permute-start.38 = (bf16[160,384]{1,0:T(8,128)(2,1)S(1)}, bf16[160,384]{1,0:T(8,128)(2,1)S(1)}, u32[]{:S(2)}, u32[]{:S(2)}) collective-permute-start(bf16[160,384]{1,0:T(8,128)(2,1)S(1)} %get-tuple-element.187), channel_id=1, source_target_pairs={{0,96},{16,112},{32,64},{48,80},{64,32},{80,48},{96,0},{112,16},{1... | collective-permute-start | bytes 368648 | tf_op jit(solution)/shard_map/ppermute | solution.py:102
  244.8 2.6 collective-permute-start.39
  250.2 2.4 collective-permute-done.39.refs_6_
  253.4 3.6 %collective-permute-start.40 = (bf16[96,384]{1,0:T(8,128)(2,1)S(1)}, bf16[96,384]{1,0:T(8,128)(2,1)S(1)}, u32[]{:S(2)}, u32[]{:S(2)}) collective-permute-start(bf16[96,384]{1,0:T(8,128)(2,1)S(1)} %get-tuple-element.192.refs_4_), channel_id=1, source_target_pairs={{0,12},{1,13},{2,14},{3,15},{4,0},{5,1},{6,2},{7,3},{8,4},{9,5},{1... | collective-permute-start | bytes 221192 | tf_op jit(solution)/shard_map/ppermute | solution.py:85
  259.1 2.6 collective-permute-done.41
  262.6 3.9 %collective-permute-start.44 = (bf16[384,384]{1,0:T(8,128)(2,1)S(1)}, bf16[384,384]{1,0:T(8,128)(2,1)S(1)}, u32[]{:S(2)}, u32[]{:S(2)}) collective-permute-start(bf16[384,384]{1,0:T(8,128)(2,1)S(1)} %constant_dynamic-update-slice_fusion.2.refs_0_), channel_id=1, source_target_pairs={{0,1},{1,0},{2,3},{3,2},{4,5},{5,4},{6,7},{7,6},{8,9},{9,8},{10,11... | collective-permute-start | bytes 884744 | tf_op jit(solution)/shard_map/ppermute | solution.py:85
  268.1 5.2 %collective-permute-start.45 = (bf16[384,384]{1,0:T(8,128)(2,1)S(1)}, bf16[384,384]{1,0:T(8,128)(2,1)S(1)}, u32[]{:S(2)}, u32[]{:S(2)}) collective-permute-start(bf16[384,384]{1,0:T(8,128)(2,1)S(1)} %collective-permute-done.43.refs_1_), channel_id=1, source_target_pairs={{0,1},{1,0},{2,3},{3,2},{4,5},{5,4},{6,7},{7,6},{8,9},{9,8},{10,11... | collective-permute-start | bytes 884744 | tf_op jit(solution)/shard_map/ppermute | solution.py:85
  277.7 11.3 %newton.1 = f32[96,384]{1,0:T(8,128)} custom-call(s32[8]{0:T(128)S(1)} %copy-done.46, bf16[384,384]{1,0:T(8,128)(2,1)S(1)} %constant_dynamic-update-slice_fusion.2.refs_0_, bf16[384,384]{1,0:T(8,128)(2,1)S(1)} %collective-permute-done.43.refs_1_, bf16[384,384]{1,0:T(8,128)(2,1)S(1)} %collective-permute-done.44.refs_2_, ...), custom_call_target="tpu_custom_call" | custom-call | tf_op jit(solution)/shard_map/newton/pallas_call | solution.py:123
  (255 shorter events, 114.6 us)
Async XLA Ops:
  9.1 11.4 %collective-permute-start.1 = (bf16[256,384]{1,0:T(8,128)(2,1)S(1)}, bf16[256,384]{1,0:T(8,128)(2,1)S(1)}, u32[]{:S(2)}, u32[]{:S(2)}) collective-permute-start(bf16[256,384]{1,0:T(8,128)(2,1)S(1)} %pad_maximum_fusion.refs_0_), channel_id=1, source_target_pairs={{0,48},{16,0},{32,16},{48,32},{64,112},{80,64},{96,80},{112,96},{1... | collective-permute-start | bytes 589832 | tf_op jit(solution)/shard_map/ppermute | solution.py:102
  13.0 11.9 %collective-permute-start.3 = (bf16[256,384]{1,0:T(8,128)(2,1)S(1)}, bf16[256,384]{1,0:T(8,128)(2,1)S(1)}, u32[]{:S(2)}, u32[]{:S(2)}) collective-permute-start(bf16[256,384]{1,0:T(8,128)(2,1)S(1)} %pad_maximum_fusion.refs_0_), channel_id=1, source_target_pairs={{0,16},{16,32},{32,48},{48,0},{64,80},{80,96},{96,112},{112,64},{1... | collective-permute-start | bytes 589832 | tf_op jit(solution)/shard_map/ppermute | solution.py:102
  28.8 9.4 %collective-permute-start.5 = (bf16[416,384]{1,0:T(8,128)(2,1)S(1)}, bf16[416,384]{1,0:T(8,128)(2,1)S(1)}, u32[]{:S(2)}, u32[]{:S(2)}) collective-permute-start(bf16[416,384]{1,0:T(8,128)(2,1)S(1)} %get-tuple-element.101.refs_0_), channel_id=1, source_target_pairs={{0,8},{1,9},{2,10},{3,11},{4,12},{5,13},{6,14},{7,15},{8,0},{9,1},... | collective-permute-start | bytes 958472 | tf_op jit(solution)/shard_map/ppermute | solution.py:85
  29.4 17.2 %collective-permute-start.6 = (bf16[416,384]{1,0:T(8,128)(2,1)S(1)}, bf16[416,384]{1,0:T(8,128)(2,1)S(1)}, u32[]{:S(2)}, u32[]{:S(2)}) collective-permute-start(bf16[416,384]{1,0:T(8,128)(2,1)S(1)} %get-tuple-element.101.refs_0_), channel_id=1, source_target_pairs={{0,4},{1,5},{2,6},{3,7},{4,8},{5,9},{6,10},{7,11},{8,12},{9,13},{1... | collective-permute-start | bytes 958472 | tf_op jit(solution)/shard_map/ppermute | solution.py:85
  47.6 8.6 %collective-permute-start.11 = (bf16[416,384]{1,0:T(8,128)(2,1)S(1)}, bf16[416,384]{1,0:T(8,128)(2,1)S(1)}, u32[]{:S(2)}, u32[]{:S(2)}) collective-permute-start(bf16[416,384]{1,0:T(8,128)(2,1)S(1)} %get-tuple-element.107), channel_id=1, source_target_pairs={{0,2},{1,3},{2,0},{3,1},{4,6},{5,7},{6,4},{7,5},{8,10},{9,11},{10,... | collective-permute-start | bytes 958472 | tf_op jit(solution)/shard_map/ppermute | solution.py:85
  60.6 15.8 %collective-permute-start.7 = (bf16[384,384]{1,0:T(8,128)(2,1)}, bf16[384,384]{1,0:T(8,128)(2,1)}, u32[]{:S(2)}, u32[]{:S(2)}) collective-permute-start(bf16[384,384]{1,0:T(8,128)(2,1)} %get-tuple-element.112.refs_0_), channel_id=1, source_target_pairs={{0,12},{1,13},{2,14},{3,15},{4,0},{5,1},{6,2},{7,3},{8,4},{9,5},{1... | collective-permute-start | bytes 884744 | tf_op jit(solution)/shard_map/ppermute | solution.py:85
  60.6 15.8 %collective-permute-start.8 = (bf16[384,384]{1,0:T(8,128)(2,1)}, bf16[384,384]{1,0:T(8,128)(2,1)}, u32[]{:S(2)}, u32[]{:S(2)}) collective-permute-start(bf16[384,384]{1,0:T(8,128)(2,1)} %get-tuple-element.112.refs_0_), channel_id=1, source_target_pairs={{0,8},{1,9},{2,10},{3,11},{4,12},{5,13},{6,14},{7,15},{8,0},{9,1},... | collective-permute-start | bytes 884744 | tf_op jit(solution)/shard_map/ppermute | solution.py:85
  61.2 16.5 %collective-permute-start.9 = (bf16[384,384]{1,0:T(8,128)(2,1)}, bf16[384,384]{1,0:T(8,128)(2,1)}, u32[]{:S(2)}, u32[]{:S(2)}) collective-permute-start(bf16[384,384]{1,0:T(8,128)(2,1)} %get-tuple-element.112.refs_0_), channel_id=1, source_target_pairs={{0,4},{1,5},{2,6},{3,7},{4,8},{5,9},{6,10},{7,11},{8,12},{9,13},{1... | collective-permute-start | bytes 884744 | tf_op jit(solution)/shard_map/ppermute | solution.py:85
  62.1 15.6 %collective-permute-start.10 = (bf16[768,384]{1,0:T(8,128)(2,1)}, bf16[768,384]{1,0:T(8,128)(2,1)}, u32[]{:S(2)}, u32[]{:S(2)}) collective-permute-start(bf16[768,384]{1,0:T(8,128)(2,1)} %get-tuple-element.106.refs_0_), channel_id=1, source_target_pairs={{0,2},{1,3},{2,0},{3,1},{4,6},{5,7},{6,4},{7,5},{8,10},{9,11},{10,... | collective-permute-start | bytes 1769480 | tf_op jit(solution)/shard_map/ppermute | solution.py:85
  63.4 19.0 %collective-permute-start.14 = (bf16[768,384]{1,0:T(8,128)(2,1)}, bf16[768,384]{1,0:T(8,128)(2,1)}, u32[]{:S(2)}, u32[]{:S(2)}) collective-permute-start(bf16[768,384]{1,0:T(8,128)(2,1)} %get-tuple-element.106.refs_0_), channel_id=1, source_target_pairs={{0,1},{1,0},{2,3},{3,2},{4,5},{5,4},{6,7},{7,6},{8,9},{9,8},{10,11... | collective-permute-start | bytes 1769480 | tf_op jit(solution)/shard_map/ppermute | solution.py:85
  80.0 21.1 %collective-permute-start.13 = (bf16[1152,384]{1,0:T(8,128)(2,1)}, bf16[1152,384]{1,0:T(8,128)(2,1)}, u32[]{:S(2)}, u32[]{:S(2)}) collective-permute-start(bf16[1152,384]{1,0:T(8,128)(2,1)} %third_merge_x.1.refs_0_), channel_id=1, source_target_pairs={{0,2},{1,3},{2,0},{3,1},{4,6},{5,7},{6,4},{7,5},{8,10},{9,11},{10,... | collective-permute-start | bytes 2654216 | tf_op jit(solution)/shard_map/ppermute | solution.py:85
  81.3 21.6 %collective-permute-start.16 = (bf16[1152,384]{1,0:T(8,128)(2,1)}, bf16[1152,384]{1,0:T(8,128)(2,1)}, u32[]{:S(2)}, u32[]{:S(2)}) collective-permute-start(bf16[1152,384]{1,0:T(8,128)(2,1)} %third_merge_x.1.refs_0_), channel_id=1, source_target_pairs={{0,1},{1,0},{2,3},{3,2},{4,5},{5,4},{6,7},{7,6},{8,9},{9,8},{10,11... | collective-permute-start | bytes 2654216 | tf_op jit(solution)/shard_map/ppermute | solution.py:85
  138.6 18.0 %collective-permute-start.18 = (bf16[2304,384]{1,0:T(8,128)(2,1)}, bf16[2304,384]{1,0:T(8,128)(2,1)}, u32[]{:S(2)}, u32[]{:S(2)}) collective-permute-start(bf16[2304,384]{1,0:T(8,128)(2,1)} %get-tuple-element.135), channel_id=1, source_target_pairs={{0,1},{1,0},{2,3},{3,2},{4,5},{5,4},{6,7},{7,6},{8,9},{9,8},{10,11... | collective-permute-start | bytes 5308424 | tf_op jit(solution)/shard_map/ppermute | solution.py:85
  154.6 37.1 %collective-permute-start.19 = (bf16[1536,384]{1,0:T(8,128)(2,1)}, bf16[1536,384]{1,0:T(8,128)(2,1)}, u32[]{:S(2)}, u32[]{:S(2)}) collective-permute-start(bf16[1536,384]{1,0:T(8,128)(2,1)} %copy-done.47), channel_id=1, source_target_pairs={{0,1},{1,0},{2,3},{3,2},{4,5},{5,4},{6,7},{7,6},{8,9},{9,8},{10,11... | collective-permute-start | bytes 3538952 | tf_op jit(solution)/shard_map/ppermute | solution.py:85
  160.9 32.4 %collective-permute-start.20 = (bf16[1152,384]{1,0:T(8,128)(2,1)}, bf16[1152,384]{1,0:T(8,128)(2,1)}, u32[]{:S(2)}, u32[]{:S(2)}) collective-permute-start(bf16[1152,384]{1,0:T(8,128)(2,1)} %get-tuple-element.154), channel_id=1, source_target_pairs={{0,2},{1,3},{2,0},{3,1},{4,6},{5,7},{6,4},{7,5},{8,10},{9,11},{10,... | collective-permute-start | bytes 2654216 | tf_op jit(solution)/shard_map/ppermute | solution.py:85
  194.0 18.2 %collective-permute-start.21 = (bf16[768,384]{1,0:T(8,128)(2,1)S(1)}, bf16[768,384]{1,0:T(8,128)(2,1)S(1)}, u32[]{:S(2)}, u32[]{:S(2)}) collective-permute-start(bf16[768,384]{1,0:T(8,128)(2,1)S(1)} %get-tuple-element.155), channel_id=1, source_target_pairs={{0,2},{1,3},{2,0},{3,1},{4,6},{5,7},{6,4},{7,5},{8,10},{9,11},{10,... | collective-permute-start | bytes 1769480 | tf_op jit(solution)/shard_map/ppermute | solution.py:85
  195.7 9.5 %collective-permute-start.22 = (bf16[384,384]{1,0:T(8,128)(2,1)S(1)}, bf16[384,384]{1,0:T(8,128)(2,1)S(1)}, u32[]{:S(2)}, u32[]{:S(2)}) collective-permute-start(bf16[384,384]{1,0:T(8,128)(2,1)S(1)} %get-tuple-element.158), channel_id=1, source_target_pairs={{0,4},{1,5},{2,6},{3,7},{4,8},{5,9},{6,10},{7,11},{8,12},{9,13},{1... | collective-permute-start | bytes 884744 | tf_op jit(solution)/shard_map/ppermute | solution.py:85
  196.1 16.1 %collective-permute-start.23 = (bf16[384,384]{1,0:T(8,128)(2,1)S(1)}, bf16[384,384]{1,0:T(8,128)(2,1)S(1)}, u32[]{:S(2)}, u32[]{:S(2)}) collective-permute-start(bf16[384,384]{1,0:T(8,128)(2,1)S(1)} %get-tuple-element.159), channel_id=1, source_target_pairs={{0,8},{1,9},{2,10},{3,11},{4,12},{5,13},{6,14},{7,15},{8,0},{9,1},... | collective-permute-start | bytes 884744 | tf_op jit(solution)/shard_map/ppermute | solution.py:85
  198.9 13.3 %collective-permute-start.24 = (bf16[384,384]{1,0:T(8,128)(2,1)S(1)}, bf16[384,384]{1,0:T(8,128)(2,1)S(1)}, u32[]{:S(2)}, u32[]{:S(2)}) collective-permute-start(bf16[384,384]{1,0:T(8,128)(2,1)S(1)} %get-tuple-element.160), channel_id=1, source_target_pairs={{0,12},{1,13},{2,14},{3,15},{4,0},{5,1},{6,2},{7,3},{8,4},{9,5},{1... | collective-permute-start | bytes 884744 | tf_op jit(solution)/shard_map/ppermute | solution.py:85
  201.0 15.2 %collective-permute-start.29 = (bf16[448,384]{1,0:T(8,128)(2,1)S(1)}, bf16[448,384]{1,0:T(8,128)(2,1)S(1)}, u32[]{:S(2)}, u32[]{:S(2)}) collective-permute-start(bf16[448,384]{1,0:T(8,128)(2,1)S(1)} %get-tuple-element.174), channel_id=1, source_target_pairs={{0,2},{1,3},{2,0},{3,1},{4,6},{5,7},{6,4},{7,5},{8,10},{9,11},{10,... | collective-permute-start | bytes 1032200 | tf_op jit(solution)/shard_map/ppermute | solution.py:85
  212.3 9.2 %collective-permute-start.25 = (bf16[192,384]{1,0:T(8,128)(2,1)S(1)}, bf16[192,384]{1,0:T(8,128)(2,1)S(1)}, u32[]{:S(2)}, u32[]{:S(2)}) collective-permute-start(bf16[192,384]{1,0:T(8,128)(2,1)S(1)} %get-tuple-element.163), channel_id=1, source_target_pairs={{0,4},{1,5},{2,6},{3,7},{4,8},{5,9},{6,10},{7,11},{8,12},{9,13},{1... | collective-permute-start | bytes 442376 | tf_op jit(solution)/shard_map/ppermute | solution.py:85
  216.4 17.9 %collective-permute-start.30 = (bf16[256,384]{1,0:T(8,128)(2,1)S(1)}, bf16[256,384]{1,0:T(8,128)(2,1)S(1)}, u32[]{:S(2)}, u32[]{:S(2)}) collective-permute-start(bf16[256,384]{1,0:T(8,128)(2,1)S(1)} %get-tuple-element.177), channel_id=1, source_target_pairs={{0,4},{1,5},{2,6},{3,7},{4,8},{5,9},{6,10},{7,11},{8,12},{9,13},{1... | collective-permute-start | bytes 589832 | tf_op jit(solution)/shard_map/ppermute | solution.py:85
  216.7 17.7 %collective-permute-start.31 = (bf16[256,384]{1,0:T(8,128)(2,1)S(1)}, bf16[256,384]{1,0:T(8,128)(2,1)S(1)}, u32[]{:S(2)}, u32[]{:S(2)}) collective-permute-start(bf16[256,384]{1,0:T(8,128)(2,1)S(1)} %get-tuple-element.178), channel_id=1, source_target_pairs={{0,8},{1,9},{2,10},{3,11},{4,12},{5,13},{6,14},{7,15},{8,0},{9,1},... | collective-permute-start | bytes 589832 | tf_op jit(solution)/shard_map/ppermute | solution.py:85
  219.0 15.3 %collective-permute-start.32 = (bf16[256,384]{1,0:T(8,128)(2,1)S(1)}, bf16[256,384]{1,0:T(8,128)(2,1)S(1)}, u32[]{:S(2)}, u32[]{:S(2)}) collective-permute-start(bf16[256,384]{1,0:T(8,128)(2,1)S(1)} %get-tuple-element.179), channel_id=1, source_target_pairs={{0,12},{1,13},{2,14},{3,15},{4,0},{5,1},{6,2},{7,3},{8,4},{9,5},{1... | collective-permute-start | bytes 589832 | tf_op jit(solution)/shard_map/ppermute | solution.py:85
  220.8 11.3 %collective-permute-start.26 = (bf16[192,384]{1,0:T(8,128)(2,1)S(1)}, bf16[192,384]{1,0:T(8,128)(2,1)S(1)}, u32[]{:S(2)}, u32[]{:S(2)}) collective-permute-start(bf16[192,384]{1,0:T(8,128)(2,1)S(1)} %get-tuple-element.164), channel_id=1, source_target_pairs={{0,8},{1,9},{2,10},{3,11},{4,12},{5,13},{6,14},{7,15},{8,0},{9,1},... | collective-permute-start | bytes 442376 | tf_op jit(solution)/shard_map/ppermute | solution.py:85
  221.5 12.7 %collective-permute-start.27 = (bf16[192,384]{1,0:T(8,128)(2,1)S(1)}, bf16[192,384]{1,0:T(8,128)(2,1)S(1)}, u32[]{:S(2)}, u32[]{:S(2)}) collective-permute-start(bf16[192,384]{1,0:T(8,128)(2,1)S(1)} %get-tuple-element.165), channel_id=1, source_target_pairs={{0,12},{1,13},{2,14},{3,15},{4,0},{5,1},{6,2},{7,3},{8,4},{9,5},{1... | collective-permute-start | bytes 442376 | tf_op jit(solution)/shard_map/ppermute | solution.py:85
  235.3 9.6 %collective-permute-start.34 = (bf16[160,384]{1,0:T(8,128)(2,1)S(1)}, bf16[160,384]{1,0:T(8,128)(2,1)S(1)}, u32[]{:S(2)}, u32[]{:S(2)}) collective-permute-start(bf16[160,384]{1,0:T(8,128)(2,1)S(1)} %get-tuple-element.183), channel_id=1, source_target_pairs={{0,32},{16,48},{32,0},{48,16},{64,96},{80,112},{96,64},{112,80},{1... | collective-permute-start | bytes 368648 | tf_op jit(solution)/shard_map/ppermute | solution.py:102
  235.6 11.9 %collective-permute-start.35 = (bf16[160,384]{1,0:T(8,128)(2,1)S(1)}, bf16[160,384]{1,0:T(8,128)(2,1)S(1)}, u32[]{:S(2)}, u32[]{:S(2)}) collective-permute-start(bf16[160,384]{1,0:T(8,128)(2,1)S(1)} %get-tuple-element.184), channel_id=1, source_target_pairs={{0,48},{16,0},{32,16},{48,32},{64,112},{80,64},{96,80},{112,96},{1... | collective-permute-start | bytes 368648 | tf_op jit(solution)/shard_map/ppermute | solution.py:102
  237.9 9.5 %collective-permute-start.36 = (bf16[160,384]{1,0:T(8,128)(2,1)S(1)}, bf16[160,384]{1,0:T(8,128)(2,1)S(1)}, u32[]{:S(2)}, u32[]{:S(2)}) collective-permute-start(bf16[160,384]{1,0:T(8,128)(2,1)S(1)} %get-tuple-element.185), channel_id=1, source_target_pairs={{0,64},{16,80},{32,96},{48,112},{64,0},{80,16},{96,32},{112,48},{1... | collective-permute-start | bytes 368648 | tf_op jit(solution)/shard_map/ppermute | solution.py:102
  241.2 9.0 %collective-permute-start.38 = (bf16[160,384]{1,0:T(8,128)(2,1)S(1)}, bf16[160,384]{1,0:T(8,128)(2,1)S(1)}, u32[]{:S(2)}, u32[]{:S(2)}) collective-permute-start(bf16[160,384]{1,0:T(8,128)(2,1)S(1)} %get-tuple-element.187), channel_id=1, source_target_pairs={{0,96},{16,112},{32,64},{48,80},{64,32},{80,48},{96,0},{112,16},{1... | collective-permute-start | bytes 368648 | tf_op jit(solution)/shard_map/ppermute | solution.py:102
  262.6 15.1 %collective-permute-start.44 = (bf16[384,384]{1,0:T(8,128)(2,1)S(1)}, bf16[384,384]{1,0:T(8,128)(2,1)S(1)}, u32[]{:S(2)}, u32[]{:S(2)}) collective-permute-start(bf16[384,384]{1,0:T(8,128)(2,1)S(1)} %constant_dynamic-update-slice_fusion.2.refs_0_), channel_id=1, source_target_pairs={{0,1},{1,0},{2,3},{3,2},{4,5},{5,4},{6,7},{7,6},{8,9},{9,8},{10,11... | collective-permute-start | bytes 884744 | tf_op jit(solution)/shard_map/ppermute | solution.py:85
  268.1 9.5 %collective-permute-start.45 = (bf16[384,384]{1,0:T(8,128)(2,1)S(1)}, bf16[384,384]{1,0:T(8,128)(2,1)S(1)}, u32[]{:S(2)}, u32[]{:S(2)}) collective-permute-start(bf16[384,384]{1,0:T(8,128)(2,1)S(1)} %collective-permute-done.43.refs_1_), channel_id=1, source_target_pairs={{0,1},{1,0},{2,3},{3,2},{4,5},{5,4},{6,7},{7,6},{8,9},{9,8},{10,11... | collective-permute-start | bytes 884744 | tf_op jit(solution)/shard_map/ppermute | solution.py:85
  (72 other events, 387.8 us)
